TPU v7x, 512 devices: a whole 4x4x16 slice. The times are simulated.
512 devices in a mesh: blk: 64 (over x_hi, z, core), help: 8 (over y, x_lo).
Axes of the slice: x: 4 (x_hi: 2, x_lo: 2; x = x_hi * 2 + x_lo), y: 4, z: 16, core: 2. Of those that a mesh axis runs over, the one named last changes fastest.
Arguments:
- features_t: bfloat16 [256, 98304], P(None, 'blk'), may hold values from -6 to 6
- weight: bfloat16 [256, 256], replicated, may hold values from -0.375 to 0.375
- bias: float32 [256], P('help'), may hold values from -3 to 3
- cotangent_t: bfloat16 [256, 98304], P('help', 'blk'), may hold values from -6 to 6
- tile_vals: bfloat16 [64, 8, 80, 128, 128], P('blk', 'help'), may hold values from -0.078125 to 0.078125
- slot_row: int32 [64, 8, 80], P('blk', 'help'), may hold values from 0 to 12, as said below
- slot_col: int32 [64, 8, 80], P('blk', 'help'), may hold values from 0 to 59, as said below
Outputs:
- output_t: bfloat16 [256, 98304], P('help', 'blk')
- propagated_grad: float32 [256, 98304], P('help', 'blk')
- weight_grad: float32 [256, 256], P(None, 'help')
- bias_grad: float32 [256], P('help')
Inputs may be any that keep to these rules, and one draw needn't show every extreme that they name: `slot_row`: each device has 80 slots, the used ones first; a slot holding 12 is unused. In every node-row block one helper uses all 80 slots and every other one at least 40. A slot's column tile is tile slot_col % 12 of node-row block (own block + slot_col // 12 - 2) taken around the loop of 64 blocks.
All inputs are finite; a program needn't handle non-finite values.
Results may differ from a plain program's by a relative error of at most 0.0045.
Values may be sent and summed in bfloat16 or wider, within the bound.
No kernel may reach another device: no remote copies, remote signals or barrier semaphores. Data moves between devices by JAX's collectives and lax.ppermute only.
A program may use at most 64 MiB of HBM per device.

v0:
```python
import math

import jax
import jax.numpy as jnp
from jax import lax
from jax.sharding import PartitionSpec as P

BAND = 2


def shifted(block, axis, distance):
    devices = range(lax.axis_size(axis))
    route = [((i - distance) % len(devices), i) for i in devices]
    return lax.ppermute(block, axis, route)


def gather_window(block):
    placed = []
    for offset in range(-BAND, BAND + 1):
        if offset == 0:
            placed.append(block)
        else:
            placed.append(shifted(block, "blk", -offset))
    stacked = jnp.stack(placed, axis=0)
    return stacked


def aggregate(stacked, tiles, rows, cols, row_tiles):
    tile = tiles.shape[-1]
    spans = stacked.shape[0]
    width = stacked.shape[1]
    banded = stacked.reshape(spans, width, row_tiles, tile)
    column_ids = jnp.arange(spans * row_tiles, dtype=jnp.int32).reshape(spans, row_tiles)
    picker = (cols[:, None, None] == column_ids[None, :, :]).astype(jnp.bfloat16)
    pieces = jnp.einsum("kbt,bftc->kfc", picker, banded, preferred_element_type=jnp.float32).astype(
        jnp.bfloat16
    )
    products = jnp.einsum("kfc,krc->kfr", pieces, tiles, preferred_element_type=jnp.float32)
    onehot = (rows[None, :] == jnp.arange(row_tiles, dtype=jnp.int32)[:, None]).astype(jnp.float32)
    summed = jnp.einsum("tk,kfr->ftr", onehot, products, precision=lax.Precision.HIGHEST)
    return summed.reshape(width, row_tiles * tile)


def per_device(features_t, weight, bias, cotangent_t, tile_vals, slot_row, slot_col):
    tiles = tile_vals[0, 0]
    rows = slot_row[0, 0]
    cols = slot_col[0, 0]
    tile = tiles.shape[-1]
    row_tiles = features_t.shape[1] // tile
    helper = lax.axis_index("help")
    share = cotangent_t.shape[0]
    partial_value = aggregate(gather_window(features_t), tiles, rows, cols, row_tiles)
    agg_share = lax.psum_scatter(partial_value, "help", scatter_dimension=0, tiled=True).astype(
        jnp.bfloat16
    )
    agg_full = lax.all_gather(agg_share, "help", axis=0, tiled=True)
    weight_cols = lax.dynamic_slice_in_dim(weight, helper * share, share, 1)
    pre = jnp.einsum("io,in->on", weight_cols, agg_full, preferred_element_type=jnp.float32)
    pre = pre + bias[:, None]
    output_t = jax.nn.elu(pre).astype(jnp.bfloat16)
    slope = jnp.where(pre > 0.0, jnp.ones_like(pre), jnp.exp(jnp.minimum(pre, 0.0)))
    grad_pre = (cotangent_t.astype(jnp.float32) * slope).astype(jnp.bfloat16)
    local_weight = jnp.einsum("in,on->io", agg_full, grad_pre, preferred_element_type=jnp.float32)
    local_bias = jnp.sum(grad_pre.astype(jnp.float32), axis=1)
    weight_sum, bias_sum = lax.psum((local_weight, local_bias), "blk")
    nodes_total = features_t.shape[1] * lax.axis_size("blk")
    scale = 1.0 / math.sqrt(nodes_total)
    grad_full = lax.all_gather(grad_pre, "help", axis=0, tiled=True)
    back = jnp.dot(weight, grad_full, preferred_element_type=jnp.float32).astype(jnp.bfloat16)
    back_partial = aggregate(gather_window(back), tiles, rows, cols, row_tiles)
    propagated = lax.psum_scatter(back_partial, "help", scatter_dimension=0, tiled=True)
    return (output_t, propagated, weight_sum * scale, bias_sum * scale)


def solution(mesh):
    placed = (
        P(None, "blk"),
        P(),
        P("help"),
        P("help", "blk"),
        P("blk", "help", None, None, None),
        P("blk", "help", None),
        P("blk", "help", None),
    )
    return jax.shard_map(
        per_device,
        mesh=mesh,
        in_specs=placed,
        out_specs=(P("help", "blk"), P("help", "blk"), P(None, "help"), P("help")),
        check_vma=False,
    )
```

profile of v0, /device:TPU:1, one launch (start us, length us, event | category | flops | bytes accessed | tf_op | source)
XLA Modules:
  0.0 540.8 jit_solution(9257986240852171921)
XLA Ops:
  8.8 14.4 %collective-permute-start.3 = (bf16[256,1536]{0,1:T(8,128)(2,1)S(1)}, bf16[256,1536]{0,1:T(8,128)(2,1)}, u32[]{:S(2)}, u32[]{:S(2)}) collective-permute-start(bf16[256,1536]{0,1:T(8,128)(2,1)S(1)} %copy.42), channel_id=1, source_target_pairs={{16,0},{24,8},{32,16},{40,24},{48,32},{56,40},{64,48},{72,56},{80,... | collective-permute-start | bytes 2359304 | tf_op jit(solution)/shard_map/ppermute | solution.py:14
  23.2 2.9 collective-permute-start.2
  26.1 2.7 collective-permute-start.1
  32.5 6.9 %collective-permute-done.3 = bf16[256,1536]{0,1:T(8,128)(2,1)} collective-permute-done((bf16[256,1536]{0,1:T(8,128)(2,1)S(1)}, bf16[256,1536]{0,1:T(8,128)(2,1)}, u32[]{:S(2)}, u32[]{:S(2)}) %collective-permute-start.3) | collective-permute-done | bytes 786464 | tf_op jit(solution)/shard_map/ppermute | solution.py:14
  42.0 2.6 copy.50
  47.2 12.3 %collective-permute-done = bf16[256,1536]{0,1:T(8,128)(2,1)} collective-permute-done((bf16[256,1536]{0,1:T(8,128)(2,1)S(1)}, bf16[256,1536]{0,1:T(8,128)(2,1)}, u32[]{:S(2)}, u32[]{:S(2)}) %collective-permute-start) | collective-permute-done | bytes 786464 | tf_op jit(solution)/shard_map/ppermute | solution.py:14
  59.4 2.9 copy.47
  70.7 23.6 %fusion.10 = f32[256,12,128]{2,1,0:T(8,128)} fusion(f32[80,256,128]{2,1,0:T(8,128)S(1)} %fusion.6, s32[80]{0:T(128)S(1)} %bitcast.54), kind=kOutput, calls=%fused_computation.14 | convolution fusion | flops 377488320 | bytes 12058944 | tf_op jit(solution)/shard_map/tk,kfr->ftr/dot_general | solution.py:40
  94.3 2.8 copy.54
  97.0 3.0 copy.67
  100.1 38.0 %reduce-scatter.7.cloned.1.call-done = f32[32,1536]{1,0:T(8,128)} async-done(((f32[256,1536]{1,0:T(8,128)}), f32[32,1536]{1,0:T(8,128)}) %reduce-scatter.7.cloned.1.call-update) | async-done | bytes 196624 | tf_op jit(solution)/shard_map/reduce_scatter | solution.py:53
  139.1 25.7 %all_gather.6 = bf16[256,1536]{1,0:T(8,128)(2,1)S(1)} all-gather(bf16[32,1536]{1,0:T(8,128)(2,1)S(1)} %convert_element_type.32), channel_id=1, replica_groups=mesh['blk'=64,'help'=8] {'help'}, dimensions={0}, use_global_device_ids=true | all-gather | bytes 884736 | tf_op jit(solution)/shard_map/all_gather | solution.py:56
  166.9 25.6 %all_gather.7 = bf16[256,1536]{1,0:T(8,128)(2,1)S(1)} all-gather(bf16[32,1536]{1,0:T(8,128)(2,1)S(1)} %get-tuple-element.19), channel_id=1, replica_groups=mesh['blk'=64,'help'=8] {'help'}, dimensions={0}, use_global_device_ids=true | all-gather | bytes 884736 | tf_op jit(solution)/shard_map/all_gather | solution.py:68
  194.8 17.6 %collective-permute-start.6 = (bf16[256,1536]{0,1:T(8,128)(2,1)}, bf16[256,1536]{0,1:T(8,128)(2,1)}, u32[]{:S(2)}, u32[]{:S(2)}) collective-permute-start(bf16[256,1536]{0,1:T(8,128)(2,1)} %bitcast.14), channel_id=1, source_target_pairs={{8,0},{16,8},{24,16},{32,24},{40,32},{48,40},{56,48},{64,56},{72,6... | collective-permute-start | bytes 2359304 | tf_op jit(solution)/shard_map/ppermute | solution.py:14
  212.4 7.7 %collective-permute-start.7 = (bf16[256,1536]{0,1:T(8,128)(2,1)}, bf16[256,1536]{0,1:T(8,128)(2,1)}, u32[]{:S(2)}, u32[]{:S(2)}) collective-permute-start(bf16[256,1536]{0,1:T(8,128)(2,1)} %bitcast.14), channel_id=1, source_target_pairs={{16,0},{24,8},{32,16},{40,24},{48,32},{56,40},{64,48},{72,56},{80,... | collective-permute-start | bytes 2359304 | tf_op jit(solution)/shard_map/ppermute | solution.py:14
  226.6 3.5 collective-permute-done.6
  230.1 2.6 copy.59
  232.7 5.1 collective-permute-done.7
  237.8 2.6 copy.60
  243.0 10.8 %collective-permute-done.4 = bf16[256,1536]{0,1:T(8,128)(2,1)} collective-permute-done((bf16[256,1536]{0,1:T(8,128)(2,1)}, bf16[256,1536]{0,1:T(8,128)(2,1)}, u32[]{:S(2)}, u32[]{:S(2)}) %collective-permute-start.4) | collective-permute-done | bytes 786464 | tf_op jit(solution)/shard_map/ppermute | solution.py:14
  264.6 10.9 %fusion.13 = f32[256,12,128]{2,1,0:T(8,128)} fusion(f32[80,256,128]{2,1,0:T(8,128)S(1)} %fusion.4, s32[80]{0:T(128)S(1)} %bitcast.55), kind=kOutput, calls=%fused_computation.15 | convolution fusion | flops 377488320 | bytes 12058944 | tf_op jit(solution)/shard_map/tk,kfr->ftr/dot_general | solution.py:40
  275.5 2.7 copy.63
  278.3 3.0 copy.69
  281.7 250.9 %all-reduce = (f32[256,32]{0,1:T(8,128)S(1)}, f32[32]{0:T(128)S(1)}) all-reduce(f32[256,32]{0,1:T(8,128)S(1)} %fusion.36, f32[32]{0:T(128)S(1)} %get-tuple-element.18), channel_id=1, replica_groups=mesh['blk'=64,'help'=8] {'blk'}, use_global_device_ids=true, to_apply=%region_2.3 | all-reduce | flops 8224 | bytes 65792 | tf_op jit(solution)/shard_map/psum | solution.py:65
  (55 shorter events, 45.2 us)
Async XLA Ops:
  7.2 61.9 %copy-start = (bf16[1,1,80,128,128]{4,3,2,1,0:T(8,128)(2,1)S(1)}, bf16[1,1,80,128,128]{4,3,2,1,0:T(8,128)(2,1)}, u32[]{:S(2)}) copy-start(bf16[1,1,80,128,128]{4,3,2,1,0:T(8,128)(2,1)} %param.11) | copy-start | bytes 7864324
  7.2 131.0 %reduce-scatter.7.cloned.1.call-start = ((), (), s32[]{:S(2)}) async-start(), calls=%async_computation.2 | async-start | bytes 1769472 | tf_op jit(solution)/shard_map/reduce_scatter | solution.py:53
  8.8 30.6 %collective-permute-start.3 = (bf16[256,1536]{0,1:T(8,128)(2,1)S(1)}, bf16[256,1536]{0,1:T(8,128)(2,1)}, u32[]{:S(2)}, u32[]{:S(2)}) collective-permute-start(bf16[256,1536]{0,1:T(8,128)(2,1)S(1)} %copy.42), channel_id=1, source_target_pairs={{16,0},{24,8},{32,16},{40,24},{48,32},{56,40},{64,48},{72,56},{80,... | collective-permute-start | bytes 2359304 | tf_op jit(solution)/shard_map/ppermute | solution.py:14
  23.2 18.8 %collective-permute-start.2 = (bf16[256,1536]{0,1:T(8,128)(2,1)S(1)}, bf16[256,1536]{0,1:T(8,128)(2,1)}, u32[]{:S(2)}, u32[]{:S(2)}) collective-permute-start(bf16[256,1536]{0,1:T(8,128)(2,1)S(1)} %copy.42), channel_id=1, source_target_pairs={{8,0},{16,8},{24,16},{32,24},{40,32},{48,40},{56,48},{64,56},{72,6... | collective-permute-start | bytes 2359304 | tf_op jit(solution)/shard_map/ppermute | solution.py:14
  26.1 18.5 %collective-permute-start.1 = (bf16[256,1536]{0,1:T(8,128)(2,1)S(1)}, bf16[256,1536]{0,1:T(8,128)(2,1)}, u32[]{:S(2)}, u32[]{:S(2)}) collective-permute-start(bf16[256,1536]{0,1:T(8,128)(2,1)S(1)} %copy.42), channel_id=1, source_target_pairs={{504,0},{0,8},{8,16},{16,24},{24,32},{32,40},{40,48},{48,56},{56,6... | collective-permute-start | bytes 2359304 | tf_op jit(solution)/shard_map/ppermute | solution.py:14
  28.8 30.7 %collective-permute-start = (bf16[256,1536]{0,1:T(8,128)(2,1)S(1)}, bf16[256,1536]{0,1:T(8,128)(2,1)}, u32[]{:S(2)}, u32[]{:S(2)}) collective-permute-start(bf16[256,1536]{0,1:T(8,128)(2,1)S(1)} %copy.42), channel_id=1, source_target_pairs={{496,0},{504,8},{0,16},{8,24},{16,32},{24,40},{32,48},{40,56},{48,... | collective-permute-start | bytes 2359304 | tf_op jit(solution)/shard_map/ppermute | solution.py:14
  62.4 4.5 copy-start.4
  62.4 4.8 copy-start.1
  62.4 5.1 copy-start.5
  69.1 1.6 copy-start.6
  94.3 70.6 %copy-start.7 = (f32[32]{0:T(128)S(1)}, f32[32]{0:T(128)}, u32[]{:S(2)}) copy-start(f32[32]{0:T(128)} %param.9) | copy-start | bytes 388
  100.1 433.6 %reduce-scatter.9.cloned.1.call-start = ((), (), s32[]{:S(2)}) async-start(), calls=%async_computation.3 | async-start | bytes 1769472
  194.8 35.3 %collective-permute-start.6 = (bf16[256,1536]{0,1:T(8,128)(2,1)}, bf16[256,1536]{0,1:T(8,128)(2,1)}, u32[]{:S(2)}, u32[]{:S(2)}) collective-permute-start(bf16[256,1536]{0,1:T(8,128)(2,1)} %bitcast.14), channel_id=1, source_target_pairs={{8,0},{16,8},{24,16},{32,24},{40,32},{48,40},{56,48},{64,56},{72,6... | collective-permute-start | bytes 2359304 | tf_op jit(solution)/shard_map/ppermute | solution.py:14
  212.4 25.4 %collective-permute-start.7 = (bf16[256,1536]{0,1:T(8,128)(2,1)}, bf16[256,1536]{0,1:T(8,128)(2,1)}, u32[]{:S(2)}, u32[]{:S(2)}) collective-permute-start(bf16[256,1536]{0,1:T(8,128)(2,1)} %bitcast.14), channel_id=1, source_target_pairs={{16,0},{24,8},{32,16},{40,24},{48,32},{56,40},{64,48},{72,56},{80,... | collective-permute-start | bytes 2359304 | tf_op jit(solution)/shard_map/ppermute | solution.py:14
  220.1 20.3 %collective-permute-start.5 = (bf16[256,1536]{0,1:T(8,128)(2,1)}, bf16[256,1536]{0,1:T(8,128)(2,1)}, u32[]{:S(2)}, u32[]{:S(2)}) collective-permute-start(bf16[256,1536]{0,1:T(8,128)(2,1)} %bitcast.14), channel_id=1, source_target_pairs={{504,0},{0,8},{8,16},{16,24},{24,32},{32,40},{40,48},{48,56},{56,6... | collective-permute-start | bytes 2359304 | tf_op jit(solution)/shard_map/ppermute | solution.py:14
  222.0 31.8 %collective-permute-start.4 = (bf16[256,1536]{0,1:T(8,128)(2,1)}, bf16[256,1536]{0,1:T(8,128)(2,1)}, u32[]{:S(2)}, u32[]{:S(2)}) collective-permute-start(bf16[256,1536]{0,1:T(8,128)(2,1)} %bitcast.14), channel_id=1, source_target_pairs={{496,0},{504,8},{0,16},{8,24},{16,32},{24,40},{32,48},{40,56},{48,... | collective-permute-start | bytes 2359304 | tf_op jit(solution)/shard_map/ppermute | solution.py:14
  256.4 4.5 copy-start.2
  256.4 4.8 copy-start.3
Sparse Core Ops, SparseCore 0:
  100.2 37.8 reduce-scatter.6
  281.5 39.0 reduce-scatter.8
where the time goes:
time: 546 us; the launch traced here: 541 us
  blocking collectives  302 us (55%)
  waiting for transfers between devices  76.7 us (14%)
  starting transfers between devices  51.1 us (9%)
  local copies, waits for them, and re-layouts  48.6 us (9%)
  matrix products  45.4 us (8%)
  between operations  14.5 us (3%)
    psum x1, blocking collectives, per_device(): weight_sum, bias_sum = lax.psum((local_weight, local_bias), 'blk')  251 us
    ppermute x8, starting transfers between devices, shifted(): return lax.ppermute(block, axis, route)  51.1 us
    ppermute x8, waiting for transfers between devices, shifted(): return lax.ppermute(block, axis, route)  38.6 us
    reduce_scatter x1, waiting for transfers between devices, per_device(): lax.psum_scatter(partial_value, 'help', scatter_dimension=0, tiled=True)  38 us
    dot_general x2, matrix products, aggregate(): jnp.einsum('tk,kfr->ftr', onehot, products, precision=lax.Precision.HIGHEST)  34.5 us
    another operation x12, local copies, waits for them, and re-layouts, gather_window(): stacked = jnp.stack(placed, axis=0)  26 us
    all_gather x1, blocking collectives, per_device(): agg_full = lax.all_gather(agg_share, 'help', axis=0, tiled=True)  25.7 us
    all_gather x1, blocking collectives, per_device(): grad_full = lax.all_gather(grad_pre, 'help', axis=0, tiled=True)  25.6 us
  transfers between devices with their start and end apart: 10, of which 6 were waited for; matrix products, arithmetic and copies ran while one was open for 4% of the time, Pallas kernels for 0%

commit v1 on v0

v1 whole, which is shorter than its diff:
```python
import functools
import math

import jax
import jax.numpy as jnp
from jax import lax
from jax.experimental import pallas as pl
from jax.experimental.pallas import tpu as pltpu
from jax.sharding import PartitionSpec as P

BAND = 2
AXES = ("blk", "help")
ANY = pl.BlockSpec(memory_space=pl.ANY)
VMEM = pl.BlockSpec(memory_space=pltpu.VMEM)
SMEM = pl.BlockSpec(memory_space=pltpu.SMEM)
NT = (((1,), (1,)), ((), ()))
NN = (((1,), (0,)), ((), ()))
TN = (((0,), (0,)), ((), ()))
UNROLL = 8


def move(block, source):
    blks, helps = lax.axis_size("blk"), lax.axis_size("help")
    route = []
    for b in range(blks):
        for h in range(helps):
            sb, sh = source(b, h)
            route.append(((sb % blks) * helps + sh, b * helps + h))
    return lax.ppermute(block, AXES, route)


def step_two(b, h, sign, blks):
    other = (b + 2 * sign) % blks
    half = blks // 2
    return (other, h if other // half == b // half else h ^ 1)


def window(block):
    blks = lax.axis_size("blk")
    swap = lambda b, h: (b ^ 1, h)
    one = move(block, lambda b, h: step_two(b, h, 1 if b % 2 == 0 else -1, blks))
    zero = move(block, swap)
    two = move(block, lambda b, h: step_two(b, h, -1 if b % 2 == 0 else 1, blks))
    three = move(one, swap)
    return (block, zero, one, two, three)


def load_all(refs, win, tiles, tiles_v, sems):
    copies = [pltpu.make_async_copy(ref, win.at[i], sems.at[i]) for i, ref in enumerate(refs)]
    copies.append(pltpu.make_async_copy(tiles, tiles_v, sems.at[len(refs)]))
    for copy in copies:
        copy.start()
    return copies


def add_slots(rows, bufs, cols, tiles_v, acc, piece, dims):
    slots, tile = tiles_v.shape[0], tiles_v.shape[1]

    @pl.loop(0, slots // UNROLL)
    def _(step):
        for j in range(UNROLL):
            k = step * UNROLL + j
            product = lax.dot_general(
                tiles_v[k],
                piece(bufs[k], pl.multiple_of(cols[k] * tile, tile)),
                dims,
                preferred_element_type=jnp.float32,
            )
            place = pl.ds(pl.multiple_of(rows[k] * tile, tile), tile)
            acc[place, :] += product


def forward_kernel(rows, bufs, cols, b0, b1, b2, b3, b4, tiles, out, win, tiles_v, acc, sems):
    tile = tiles_v.shape[1]
    copies = load_all((b0, b1, b2, b3, b4), win, tiles, tiles_v, sems)
    acc[...] = jnp.zeros_like(acc)
    for copy in copies:
        copy.wait()
    add_slots(rows, bufs, cols, tiles_v, acc, lambda s, c: win[s, :, pl.ds(c, tile)], NT)
    out[...] = acc[: out.shape[0], :].astype(jnp.bfloat16)


def backward_kernel(rows, bufs, cols, b0, b1, b2, b3, b4, tiles, out, win, tiles_v, acc, sems):
    tile = tiles_v.shape[1]
    copies = load_all((b0, b1, b2, b3, b4), win, tiles, tiles_v, sems)
    acc[...] = jnp.zeros_like(acc)
    for copy in copies:
        copy.wait()
    add_slots(rows, bufs, cols, tiles_v, acc, lambda s, c: win[s, pl.ds(c, tile), :], NN)
    width = out.shape[0]
    eye = (
        lax.broadcasted_iota(jnp.int32, (width, width), 0)
        == lax.broadcasted_iota(jnp.int32, (width, width), 1)
    ).astype(jnp.bfloat16)
    for t in range(out.shape[1] // tile):
        part = acc[t * tile : (t + 1) * tile, :].astype(jnp.bfloat16)
        out[:, t * tile : (t + 1) * tile] = lax.dot_general(
            eye, part, NT, preferred_element_type=jnp.float32
        ).astype(jnp.bfloat16)


def aggregate(kernel, blocks, tiles, slots, out_shape):
    count, tile = tiles.shape[0], tiles.shape[1]
    nodes = max(blocks[0].shape)
    width = min(blocks[0].shape)
    return pl.pallas_call(
        kernel,
        out_shape=jax.ShapeDtypeStruct(out_shape, jnp.bfloat16),
        in_specs=[SMEM] * 3 + [ANY] * 6,
        out_specs=VMEM,
        scratch_shapes=[
            pltpu.VMEM((5,) + blocks[0].shape, jnp.bfloat16),
            pltpu.VMEM(tiles.shape, jnp.bfloat16),
            pltpu.VMEM((nodes + tile, width), jnp.float32),
            pltpu.SemaphoreType.DMA((6,)),
        ],
        compiler_params=pltpu.CompilerParams(vmem_limit_bytes=24 * 2**20),
        cost_estimate=pl.CostEstimate(
            flops=2 * count * tile * tile * width,
            bytes_accessed=10 * 2**20,
            transcendentals=0,
        ),
    )(*slots, *blocks, tiles)


def middle_kernel(parts, cotb, weight, weight_t, out, back, grads):
    nodes = parts.shape[1]
    total = parts[0].astype(jnp.float32)
    for s in range(1, parts.shape[0]):
        total = total + parts[s].astype(jnp.float32)
    agg = total.astype(jnp.bfloat16)
    extra = cotb[:, nodes:].astype(jnp.float32)
    bias = extra[:, 0:1] + extra[:, 1:2] + extra[:, 2:3]
    pre = lax.dot_general(weight_t[...], agg, NT, preferred_element_type=jnp.float32) + bias
    decay = jnp.exp(jnp.minimum(pre, 0.0))
    out[...] = jnp.where(pre > 0.0, pre, decay - 1.0).astype(jnp.bfloat16)
    slope = jnp.where(pre > 0.0, 1.0, decay)
    grad = (cotb[:, :nodes].astype(jnp.float32) * slope).astype(jnp.bfloat16)
    back_n = lax.dot_general(
        grad, weight_t[...], TN, preferred_element_type=jnp.float32
    ).astype(jnp.bfloat16)
    for s in range(back.shape[0]):
        back[s] = back_n
    width = agg.shape[1]
    grads[:, :width] = lax.dot_general(grad, agg, NN, preferred_element_type=jnp.float32)
    ones = jnp.ones((nodes, grads.shape[1] - width), jnp.bfloat16)
    grads[:, width:] = lax.dot_general(grad, ones, NN, preferred_element_type=jnp.float32)


def spread(x):
    return lax.all_to_all(x, "help", 0, 0)


def per_device(features_t, weight, bias, cotangent_t, tile_vals, slot_row, slot_col):
    tiles = tile_vals[0, 0]
    tile = tiles.shape[-1]
    width, nodes = features_t.shape
    row_tiles = nodes // tile
    helps = lax.axis_size("help")
    blks = lax.axis_size("blk")
    share = cotangent_t.shape[0]
    mine = nodes // helps

    odd = lax.axis_index("blk") % 2
    span = slot_col[0, 0] // row_tiles
    place = jnp.where(
        odd == 0,
        jnp.array([3, 4, 0, 1, 2], jnp.int32)[span],
        jnp.array([2, 1, 0, 4, 3], jnp.int32)[span],
    )
    slots = (slot_row[0, 0], place, slot_col[0, 0] % row_tiles)

    high = lax.reduce_precision(bias, 8, 7)
    middle = lax.reduce_precision(bias - high, 8, 7)
    low = bias - high - middle
    parts = jnp.stack([high, middle, low], axis=1).astype(jnp.bfloat16)
    lanes = 2 * tile
    cot = cotangent_t.reshape(share, helps, mine).transpose(1, 0, 2)
    tail = jnp.broadcast_to(
        jnp.pad(parts, ((0, 0), (0, lanes - mine - 3)))[None], (helps, share, lanes - mine)
    )
    cotb = spread(jnp.concatenate([cot, tail], axis=2)).reshape(width, lanes)

    partial_value = aggregate(
        forward_kernel, window(features_t), tiles, slots, (nodes, width)
    )
    received = spread(partial_value.reshape(helps, mine, width))
    out, back, grads = pl.pallas_call(
        middle_kernel,
        out_shape=(
            jax.ShapeDtypeStruct((width, mine), jnp.bfloat16),
            jax.ShapeDtypeStruct((helps, mine, width), jnp.bfloat16),
            jax.ShapeDtypeStruct((width, width + tile), jnp.float32),
        ),
        in_specs=[VMEM] * 4,
        out_specs=(VMEM,) * 3,
    )(received, cotb, weight, weight.T)
    back_full = spread(back).reshape(nodes, width)
    back_partial = aggregate(
        backward_kernel, window(back_full), tiles, slots, (width, nodes)
    )
    summed = spread(back_partial.reshape(helps, share, nodes))
    propagated = jnp.sum(summed.astype(jnp.float32), axis=0)

    output = spread(out.reshape(helps, share, mine)).transpose(1, 0, 2).reshape(share, nodes)

    total = jnp.sum(spread(grads.reshape(helps, share, width + tile)), axis=0)
    step = 1
    while step < blks:
        total = total + move(total, functools.partial(lambda s, b, h: (b ^ s, h), step))
        step *= 2
    total = total * (1.0 / math.sqrt(nodes * blks))
    return (output, propagated, total[:, :width].T, total[:, width])


def solution(mesh):
    placed = (
        P(None, "blk"),
        P(),
        P("help"),
        P("help", "blk"),
        P("blk", "help", None, None, None),
        P("blk", "help", None),
        P("blk", "help", None),
    )
    return jax.shard_map(
        per_device,
        mesh=mesh,
        in_specs=placed,
        out_specs=(P("help", "blk"), P("help", "blk"), P(None, "help"), P("help")),
        check_vma=False,
    )
```

time: 546 us -> 187 us (0.34)
  the two profiles are of different devices: /device:TPU:1 before, /device:TPU:34 now
where the time goes in v1:
time: 187 us; the launch traced here: 185 us
  starting transfers between devices  80.5 us (43%)
  waiting for transfers between devices  42.5 us (23%)
  blocking collectives  29.6 us (16%)
  Pallas kernels  14.2 us (8%)
  local copies, waits for them, and re-layouts  10 us (5%)
  other arithmetic  7.5 us (4%)
    ppermute x14, starting transfers between devices, move(): return lax.ppermute(block, AXES, route)  58.5 us
    ppermute x14, waiting for transfers between devices, move(): return lax.ppermute(block, AXES, route)  31.5 us
    all_to_all x2, blocking collectives, spread(): return lax.all_to_all(x, 'help', 0, 0)  29.6 us
    all_to_all x4, starting transfers between devices, spread(): return lax.all_to_all(x, 'help', 0, 0)  21.9 us
    pallas_call x2, Pallas kernels, aggregate(): pl.pallas_call(kernel, out_shape=jax.ShapeDtypeStruct(out_shape, jnp.bflo...  11.4 us
    all_to_all x4, waiting for transfers between devices, spread(): return lax.all_to_all(x, 'help', 0, 0)  11.1 us
    unnamed x20, local copies, waits for them, and re-layouts  6.79 us
  transfers between devices with their start and end apart: 18, of which 8 were waited for; matrix products, arithmetic and copies ran while one was open for 6% of the time, Pallas kernels for 6%

profile of v1, /device:TPU:34, one launch (start us, length us, event | category | flops | bytes accessed | tf_op | source)
XLA Modules:
  0.0 185.2 jit_solution(2501568863841204614)
XLA Ops:
  0.6 2.0 %collective-permute-start.1 = (bf16[256,1536]{1,0:T(8,128)(2,1)}, bf16[256,1536]{1,0:T(8,128)(2,1)S(1)}, u32[]{:S(2)}, u32[]{:S(2)}) collective-permute-start(bf16[256,1536]{1,0:T(8,128)(2,1)} %b0.1), channel_id=1, source_target_pairs={{16,0},{17,1},{18,2},{19,3},{20,4},{21,5},{22,6},{23,7},{505,8},{5... | collective-permute-start | bytes 2359304 | tf_op jit(solution)/shard_map/ppermute | solution.py:29
  2.7 3.3 %collective-permute-start = (bf16[256,1536]{1,0:T(8,128)(2,1)}, bf16[256,1536]{1,0:T(8,128)(2,1)S(1)}, u32[]{:S(2)}, u32[]{:S(2)}) collective-permute-start(bf16[256,1536]{1,0:T(8,128)(2,1)} %b0.1), channel_id=1, source_target_pairs={{8,0},{9,1},{10,2},{11,3},{12,4},{13,5},{14,6},{15,7},{0,8},{1,9},... | collective-permute-start | bytes 2359304 | tf_op jit(solution)/shard_map/ppermute | solution.py:29
  5.9 3.8 %collective-permute-start.2 = (bf16[256,1536]{1,0:T(8,128)(2,1)}, bf16[256,1536]{1,0:T(8,128)(2,1)S(1)}, u32[]{:S(2)}, u32[]{:S(2)}) collective-permute-start(bf16[256,1536]{1,0:T(8,128)(2,1)} %b0.1), channel_id=1, source_target_pairs={{497,0},{496,1},{499,2},{498,3},{501,4},{500,5},{503,6},{502,7},{2... | collective-permute-start | bytes 2359304 | tf_op jit(solution)/shard_map/ppermute | solution.py:29
  9.8 8.8 %collective-permute-done.1.b2 = bf16[256,1536]{1,0:T(8,128)(2,1)S(1)} collective-permute-done((bf16[256,1536]{1,0:T(8,128)(2,1)}, bf16[256,1536]{1,0:T(8,128)(2,1)S(1)}, u32[]{:S(2)}, u32[]{:S(2)}) %collective-permute-start.1) | collective-permute-done | bytes 786464 | tf_op jit(solution)/shard_map/ppermute | solution.py:29
  23.1 5.9 %all-to-all-start.1 = ((bf16[8,32,256]{2,1,0:T(8,128)(2,1)}), bf16[8,32,256]{2,1,0:T(8,128)(2,1)S(1)}, u32[]{:S(2)}, u32[]{:S(2)}) async-start(bf16[8,32,256]{2,1,0:T(8,128)(2,1)} %pad_maximum_fusion), calls=%async_computation.1 | async-start | bytes 262144 | tf_op jit(solution)/shard_map/all_to_all | solution.py:151
  34.0 5.3 %shard_map.120 = bf16[1536,256]{1,0:T(8,128)(2,1)} custom-call(s32[80]{0:T(128)S(1)} %bitcast.44, s32[80]{0:T(128)S(1)} %fusion.4.bufs, s32[80]{0:T(128)S(1)} %and_select_fusion.cols, bf16[256,1536]{1,0:T(8,128)(2,1)S(1)} %copy-done.3, bf16[256,1536]{1,0:T(8,128)(2,1)S(1)} %collective-permute-done.b1, bf16[256,1536]{1,0:T(8,128)(2,1)S(1)} %collective-permute-done.1.b2, ...), custom_call_target="tpu_custom_call" | custom-call | flops 671088640 | bytes 10485760 | tf_op jit(solution)/shard_map/pallas_call | solution.py:106
  39.9 5.7 %all-to-all-start = ((bf16[8,192,256]{2,1,0:T(8,128)(2,1)}), bf16[8,192,256]{2,1,0:T(8,128)(2,1)S(1)}, u32[]{:S(2)}, u32[]{:S(2)}) async-start(bf16[8,192,256]{2,1,0:T(8,128)(2,1)} %bitcast.6), calls=%async_computation | async-start | bytes 1572864 | tf_op jit(solution)/shard_map/all_to_all | solution.py:151
  46.4 11.0 %all-to-all-done.parts = bf16[8,192,256]{2,1,0:T(8,128)(2,1)S(1)} async-done(((bf16[8,192,256]{2,1,0:T(8,128)(2,1)}), bf16[8,192,256]{2,1,0:T(8,128)(2,1)S(1)}, u32[]{:S(2)}, u32[]{:S(2)}) %all-to-all-start) | async-done | bytes 786464 | tf_op jit(solution)/shard_map/all_to_all | solution.py:151
  58.4 2.8 %shard_map.121 = (bf16[256,192]{1,0:T(8,128)(2,1)}, bf16[8,192,256]{2,1,0:T(8,128)(2,1)}, f32[256,384]{1,0:T(8,128)}) custom-call(bf16[8,192,256]{2,1,0:T(8,128)(2,1)} %copy-done.6, bf16[256,256]{1,0:T(8,128)(2,1)} %bitcast.46, bf16[256,256]{1,0:T(8,128)(2,1)} %weight.1, bf16[256,256]{1,0:T(8,128)(2,1)} %bitcast.47), custom_call_target="tpu_custom_call" | custom-call | tf_op jit(solution)/shard_map/pallas_call | solution.py:188
  61.2 15.6 %all_to_all.30 = bf16[8,192,256]{2,1,0:T(8,128)(2,1)S(1)} all-to-all(bf16[8,192,256]{2,1,0:T(8,128)(2,1)} %get-tuple-element.8), channel_id=1, replica_groups=mesh['blk'=64,'help'=8] {'help'}, dimensions={0} | all-to-all | bytes 1572864 | tf_op jit(solution)/shard_map/all_to_all | solution.py:151
  76.8 10.6 %collective-permute-start.5 = (bf16[1536,256]{1,0:T(8,128)(2,1)S(1)}, bf16[1536,256]{1,0:T(8,128)(2,1)}, u32[]{:S(2)}, u32[]{:S(2)}) collective-permute-start(bf16[1536,256]{1,0:T(8,128)(2,1)S(1)} %bitcast.39), channel_id=1, source_target_pairs={{16,0},{17,1},{18,2},{19,3},{20,4},{21,5},{22,6},{23,7},{505,8},{5... | collective-permute-start | bytes 2359304 | tf_op jit(solution)/shard_map/ppermute | solution.py:29
  87.4 1.9 %collective-permute-start.6 = (bf16[1536,256]{1,0:T(8,128)(2,1)S(1)}, bf16[1536,256]{1,0:T(8,128)(2,1)}, u32[]{:S(2)}, u32[]{:S(2)}) collective-permute-start(bf16[1536,256]{1,0:T(8,128)(2,1)S(1)} %bitcast.40), channel_id=1, source_target_pairs={{497,0},{496,1},{499,2},{498,3},{501,4},{500,5},{503,6},{502,7},{2... | collective-permute-start | bytes 2359304 | tf_op jit(solution)/shard_map/ppermute | solution.py:29
  91.2 12.6 %collective-permute-done.5.b2 = bf16[1536,256]{1,0:T(8,128)(2,1)} collective-permute-done((bf16[1536,256]{1,0:T(8,128)(2,1)S(1)}, bf16[1536,256]{1,0:T(8,128)(2,1)}, u32[]{:S(2)}, u32[]{:S(2)}) %collective-permute-start.5) | collective-permute-done | bytes 786464 | tf_op jit(solution)/shard_map/ppermute | solution.py:29
  105.8 14.0 %all_to_all.31 = f32[8,32,384]{2,1,0:T(8,128)} all-to-all(f32[8,32,384]{2,1,0:T(8,128)} %bitcast.50), channel_id=1, replica_groups=mesh['blk'=64,'help'=8] {'help'}, dimensions={0} | all-to-all | bytes 786432 | tf_op jit(solution)/shard_map/all_to_all | solution.py:151
  124.0 7.6 %collective-permute-start.9 = (f32[32,384]{1,0:T(8,128)S(1)}, f32[32,384]{1,0:T(8,128)S(1)}, u32[]{:S(2)}, u32[]{:S(2)}) collective-permute-start(f32[32,384]{1,0:T(8,128)S(1)} %add.52), channel_id=1, source_target_pairs={{16,0},{17,1},{18,2},{19,3},{20,4},{21,5},{22,6},{23,7},{24,8},{25... | collective-permute-start | bytes 147464 | tf_op jit(solution)/shard_map/ppermute | solution.py:29
  131.6 2.1 %collective-permute-done.9 = f32[32,384]{1,0:T(8,128)S(1)} collective-permute-done((f32[32,384]{1,0:T(8,128)S(1)}, f32[32,384]{1,0:T(8,128)S(1)}, u32[]{:S(2)}, u32[]{:S(2)}) %collective-permute-start.9) | collective-permute-done | bytes 49184 | tf_op jit(solution)/shard_map/ppermute | solution.py:29
  136.2 4.5 %all-to-all-start.2 = ((bf16[8,32,192]{2,1,0:T(8,128)(2,1)}), bf16[8,32,192]{2,1,0:T(8,128)(2,1)S(1)}, u32[]{:S(2)}, u32[]{:S(2)}) async-start(bf16[8,32,192]{2,1,0:T(8,128)(2,1)} %bitcast.51), calls=%async_computation.2 | async-start | bytes 262144 | tf_op jit(solution)/shard_map/all_to_all | solution.py:151
  142.9 3.0 %collective-permute-start.11 = (f32[32,384]{1,0:T(8,128)}, f32[32,384]{1,0:T(8,128)}, u32[]{:S(2)}, u32[]{:S(2)}) collective-permute-start(f32[32,384]{1,0:T(8,128)} %add.54), channel_id=1, source_target_pairs={{64,0},{65,1},{66,2},{67,3},{68,4},{69,5},{70,6},{71,7},{72,8},{73... | collective-permute-start | bytes 147464 | tf_op jit(solution)/shard_map/ppermute | solution.py:29
  146.0 6.1 %shard_map.122 = bf16[256,1536]{1,0:T(8,128)(2,1)S(1)} custom-call(s32[80]{0:T(128)S(1)} %bitcast.45, s32[80]{0:T(128)S(1)} %fusion.4.bufs, s32[80]{0:T(128)S(1)} %and_select_fusion.cols, bf16[1536,256]{1,0:T(8,128)(2,1)S(1)} %bitcast.42, bf16[1536,256]{1,0:T(8,128)(2,1)} %collective-permute-done.4.b1, bf16[1536,256]{1,0:T(8,128)(2,1)} %collective-permute-done.5.b2, ...), custom_call_target="tpu_custom_call" | custom-call | flops 671088640 | bytes 10485760 | tf_op jit(solution)/shard_map/pallas_call | solution.py:106
  153.0 5.7 %all-to-all-start.4 = ((bf16[8,32,1536]{2,1,0:T(8,128)(2,1)}), bf16[8,32,1536]{2,1,0:T(8,128)(2,1)S(1)}, u32[]{:S(2)}, u32[]{:S(2)}) async-start(bf16[8,32,1536]{2,1,0:T(8,128)(2,1)} %bitcast.43), calls=%async_computation.4 | async-start | bytes 1572864 | tf_op jit(solution)/shard_map/all_to_all | solution.py:151
  159.6 12.9 %collective-permute-start.12 = (f32[32,384]{1,0:T(8,128)S(1)}, f32[32,384]{1,0:T(8,128)S(1)}, u32[]{:S(2)}, u32[]{:S(2)}) collective-permute-start(f32[32,384]{1,0:T(8,128)S(1)} %add.55), channel_id=1, source_target_pairs={{128,0},{129,1},{130,2},{131,3},{132,4},{133,5},{134,6},{135,7},{1... | collective-permute-start | bytes 147464 | tf_op jit(solution)/shard_map/ppermute | solution.py:29
  172.5 3.2 %collective-permute-done.12 = f32[32,384]{1,0:T(8,128)S(1)} collective-permute-done((f32[32,384]{1,0:T(8,128)S(1)}, f32[32,384]{1,0:T(8,128)S(1)}, u32[]{:S(2)}, u32[]{:S(2)}) %collective-permute-start.12) | collective-permute-done | bytes 49184 | tf_op jit(solution)/shard_map/ppermute | solution.py:29
  175.7 3.7 %collective-permute-start.13 = (f32[32,384]{1,0:T(8,128)S(1)}, f32[32,384]{1,0:T(8,128)S(1)}, u32[]{:S(2)}, u32[]{:S(2)}) collective-permute-start(f32[32,384]{1,0:T(8,128)S(1)} %add.56), channel_id=1, source_target_pairs={{256,0},{257,1},{258,2},{259,3},{260,4},{261,5},{262,6},{263,7},{2... | collective-permute-start | bytes 147464 | tf_op jit(solution)/shard_map/ppermute | solution.py:29
  180.3 2.9 %collective-permute-done.13 = f32[32,384]{1,0:T(8,128)S(1)} collective-permute-done((f32[32,384]{1,0:T(8,128)S(1)}, f32[32,384]{1,0:T(8,128)S(1)}, u32[]{:S(2)}, u32[]{:S(2)}) %collective-permute-start.13) | collective-permute-done | bytes 49184 | tf_op jit(solution)/shard_map/ppermute | solution.py:29
  (58 shorter events, 29.0 us)
Async XLA Ops:
  0.6 17.9 %collective-permute-start.1 = (bf16[256,1536]{1,0:T(8,128)(2,1)}, bf16[256,1536]{1,0:T(8,128)(2,1)S(1)}, u32[]{:S(2)}, u32[]{:S(2)}) collective-permute-start(bf16[256,1536]{1,0:T(8,128)(2,1)} %b0.1), channel_id=1, source_target_pairs={{16,0},{17,1},{18,2},{19,3},{20,4},{21,5},{22,6},{23,7},{505,8},{5... | collective-permute-start | bytes 2359304 | tf_op jit(solution)/shard_map/ppermute | solution.py:29
  2.7 27.7 %collective-permute-start = (bf16[256,1536]{1,0:T(8,128)(2,1)}, bf16[256,1536]{1,0:T(8,128)(2,1)S(1)}, u32[]{:S(2)}, u32[]{:S(2)}) collective-permute-start(bf16[256,1536]{1,0:T(8,128)(2,1)} %b0.1), channel_id=1, source_target_pairs={{8,0},{9,1},{10,2},{11,3},{12,4},{13,5},{14,6},{15,7},{0,8},{1,9},... | collective-permute-start | bytes 2359304 | tf_op jit(solution)/shard_map/ppermute | solution.py:29
  5.9 24.5 %collective-permute-start.2 = (bf16[256,1536]{1,0:T(8,128)(2,1)}, bf16[256,1536]{1,0:T(8,128)(2,1)S(1)}, u32[]{:S(2)}, u32[]{:S(2)}) collective-permute-start(bf16[256,1536]{1,0:T(8,128)(2,1)} %b0.1), channel_id=1, source_target_pairs={{497,0},{496,1},{499,2},{498,3},{501,4},{500,5},{503,6},{502,7},{2... | collective-permute-start | bytes 2359304 | tf_op jit(solution)/shard_map/ppermute | solution.py:29
  18.6 11.9 %collective-permute-start.3 = (bf16[256,1536]{1,0:T(8,128)(2,1)S(1)}, bf16[256,1536]{1,0:T(8,128)(2,1)S(1)}, u32[]{:S(2)}, u32[]{:S(2)}) collective-permute-start(bf16[256,1536]{1,0:T(8,128)(2,1)S(1)} %collective-permute-done.1.b2), channel_id=1, source_target_pairs={{8,0},{9,1},{10,2},{11,3},{12,4},{13,5},{14,6},{15,7},{0,8},{1,9},... | collective-permute-start | bytes 2359304 | tf_op jit(solution)/shard_map/ppermute | solution.py:29
  23.1 16.2 %all-to-all-start.1 = ((bf16[8,32,256]{2,1,0:T(8,128)(2,1)}), bf16[8,32,256]{2,1,0:T(8,128)(2,1)S(1)}, u32[]{:S(2)}, u32[]{:S(2)}) async-start(bf16[8,32,256]{2,1,0:T(8,128)(2,1)} %pad_maximum_fusion), calls=%async_computation.1 | async-start | bytes 262144 | tf_op jit(solution)/shard_map/all_to_all | solution.py:151
  30.4 1.7 copy-start
  32.2 1.1 copy-start.3
  34.0 11.7 %copy-start.7 = (bf16[256,256]{1,0:T(8,128)(2,1)S(1)}, bf16[256,256]{1,0:T(8,128)(2,1)}, u32[]{:S(2)}) copy-start(bf16[256,256]{1,0:T(8,128)(2,1)} %weight.1) | copy-start | bytes 393220
  39.9 17.5 %all-to-all-start = ((bf16[8,192,256]{2,1,0:T(8,128)(2,1)}), bf16[8,192,256]{2,1,0:T(8,128)(2,1)S(1)}, u32[]{:S(2)}, u32[]{:S(2)}) async-start(bf16[8,192,256]{2,1,0:T(8,128)(2,1)} %bitcast.6), calls=%async_computation | async-start | bytes 1572864 | tf_op jit(solution)/shard_map/all_to_all | solution.py:151
  45.7 100.3 %copy-start.1 = (bf16[1,1,80,128,128]{4,3,2,1,0:T(8,128)(2,1)S(1)}, bf16[1,1,80,128,128]{4,3,2,1,0:T(8,128)(2,1)}, u32[]{:S(2)}) copy-start(bf16[1,1,80,128,128]{4,3,2,1,0:T(8,128)(2,1)} %param.13) | copy-start | bytes 7864324
  45.7 100.3 %copy-start.5 = (s32[1,1,80]{2,1,0:T(1,128)S(1)}, s32[1,1,80]{2,1,0:T(1,128)}, u32[]{:S(2)}) copy-start(s32[1,1,80]{2,1,0:T(1,128)} %param.14) | copy-start | bytes 964
  76.8 27.1 %collective-permute-start.5 = (bf16[1536,256]{1,0:T(8,128)(2,1)S(1)}, bf16[1536,256]{1,0:T(8,128)(2,1)}, u32[]{:S(2)}, u32[]{:S(2)}) collective-permute-start(bf16[1536,256]{1,0:T(8,128)(2,1)S(1)} %bitcast.39), channel_id=1, source_target_pairs={{16,0},{17,1},{18,2},{19,3},{20,4},{21,5},{22,6},{23,7},{505,8},{5... | collective-permute-start | bytes 2359304 | tf_op jit(solution)/shard_map/ppermute | solution.py:29
  87.4 58.6 %collective-permute-start.6 = (bf16[1536,256]{1,0:T(8,128)(2,1)S(1)}, bf16[1536,256]{1,0:T(8,128)(2,1)}, u32[]{:S(2)}, u32[]{:S(2)}) collective-permute-start(bf16[1536,256]{1,0:T(8,128)(2,1)S(1)} %bitcast.40), channel_id=1, source_target_pairs={{497,0},{496,1},{499,2},{498,3},{501,4},{500,5},{503,6},{502,7},{2... | collective-permute-start | bytes 2359304 | tf_op jit(solution)/shard_map/ppermute | solution.py:29
  89.3 56.7 %collective-permute-start.4 = (bf16[1536,256]{1,0:T(8,128)(2,1)S(1)}, bf16[1536,256]{1,0:T(8,128)(2,1)}, u32[]{:S(2)}, u32[]{:S(2)}) collective-permute-start(bf16[1536,256]{1,0:T(8,128)(2,1)S(1)} %bitcast.41), channel_id=1, source_target_pairs={{8,0},{9,1},{10,2},{11,3},{12,4},{13,5},{14,6},{15,7},{0,8},{1,9},... | collective-permute-start | bytes 2359304 | tf_op jit(solution)/shard_map/ppermute | solution.py:29
  103.8 42.1 %collective-permute-start.7 = (bf16[1536,256]{1,0:T(8,128)(2,1)}, bf16[1536,256]{1,0:T(8,128)(2,1)}, u32[]{:S(2)}, u32[]{:S(2)}) collective-permute-start(bf16[1536,256]{1,0:T(8,128)(2,1)} %collective-permute-done.5.b2), channel_id=1, source_target_pairs={{8,0},{9,1},{10,2},{11,3},{12,4},{13,5},{14,6},{15,7},{0,8},{1,9},... | collective-permute-start | bytes 2359304 | tf_op jit(solution)/shard_map/ppermute | solution.py:29
  120.8 3.1 %collective-permute-start.8 = (f32[32,384]{1,0:T(8,128)S(1)}, f32[32,384]{1,0:T(8,128)S(1)}, u32[]{:S(2)}, u32[]{:S(2)}) collective-permute-start(f32[32,384]{1,0:T(8,128)S(1)} %reduce_sum.19), channel_id=1, source_target_pairs={{8,0},{9,1},{10,2},{11,3},{12,4},{13,5},{14,6},{15,7},{0,8},{1,9},... | collective-permute-start | bytes 147464 | tf_op jit(solution)/shard_map/ppermute | solution.py:29
  124.0 9.7 %collective-permute-start.9 = (f32[32,384]{1,0:T(8,128)S(1)}, f32[32,384]{1,0:T(8,128)S(1)}, u32[]{:S(2)}, u32[]{:S(2)}) collective-permute-start(f32[32,384]{1,0:T(8,128)S(1)} %add.52), channel_id=1, source_target_pairs={{16,0},{17,1},{18,2},{19,3},{20,4},{21,5},{22,6},{23,7},{24,8},{25... | collective-permute-start | bytes 147464 | tf_op jit(solution)/shard_map/ppermute | solution.py:29
  134.3 7.2 %collective-permute-start.10 = (f32[32,384]{1,0:T(8,128)}, f32[32,384]{1,0:T(8,128)}, u32[]{:S(2)}, u32[]{:S(2)}) collective-permute-start(f32[32,384]{1,0:T(8,128)} %add.53), channel_id=1, source_target_pairs={{32,0},{33,1},{34,2},{35,3},{36,4},{37,5},{38,6},{39,7},{40,8},{41... | collective-permute-start | bytes 147464 | tf_op jit(solution)/shard_map/ppermute | solution.py:29
  136.2 16.8 %all-to-all-start.2 = ((bf16[8,32,192]{2,1,0:T(8,128)(2,1)}), bf16[8,32,192]{2,1,0:T(8,128)(2,1)S(1)}, u32[]{:S(2)}, u32[]{:S(2)}) async-start(bf16[8,32,192]{2,1,0:T(8,128)(2,1)} %bitcast.51), calls=%async_computation.2 | async-start | bytes 262144 | tf_op jit(solution)/shard_map/all_to_all | solution.py:151
  142.9 15.8 %collective-permute-start.11 = (f32[32,384]{1,0:T(8,128)}, f32[32,384]{1,0:T(8,128)}, u32[]{:S(2)}, u32[]{:S(2)}) collective-permute-start(f32[32,384]{1,0:T(8,128)} %add.54), channel_id=1, source_target_pairs={{64,0},{65,1},{66,2},{67,3},{68,4},{69,5},{70,6},{71,7},{72,8},{73... | collective-permute-start | bytes 147464 | tf_op jit(solution)/shard_map/ppermute | solution.py:29
  152.1 0.9 copy-start.2
  153.0 31.5 %all-to-all-start.4 = ((bf16[8,32,1536]{2,1,0:T(8,128)(2,1)}), bf16[8,32,1536]{2,1,0:T(8,128)(2,1)S(1)}, u32[]{:S(2)}, u32[]{:S(2)}) async-start(bf16[8,32,1536]{2,1,0:T(8,128)(2,1)} %bitcast.43), calls=%async_computation.4 | async-start | bytes 1572864 | tf_op jit(solution)/shard_map/all_to_all | solution.py:151
  159.6 16.1 %collective-permute-start.12 = (f32[32,384]{1,0:T(8,128)S(1)}, f32[32,384]{1,0:T(8,128)S(1)}, u32[]{:S(2)}, u32[]{:S(2)}) collective-permute-start(f32[32,384]{1,0:T(8,128)S(1)} %add.55), channel_id=1, source_target_pairs={{128,0},{129,1},{130,2},{131,3},{132,4},{133,5},{134,6},{135,7},{1... | collective-permute-start | bytes 147464 | tf_op jit(solution)/shard_map/ppermute | solution.py:29
  175.7 7.5 %collective-permute-start.13 = (f32[32,384]{1,0:T(8,128)S(1)}, f32[32,384]{1,0:T(8,128)S(1)}, u32[]{:S(2)}, u32[]{:S(2)}) collective-permute-start(f32[32,384]{1,0:T(8,128)S(1)} %add.56), channel_id=1, source_target_pairs={{256,0},{257,1},{258,2},{259,3},{260,4},{261,5},{262,6},{263,7},{2... | collective-permute-start | bytes 147464 | tf_op jit(solution)/shard_map/ppermute | solution.py:29
  (3 other events, 2.2 us)

commit v2 on v1

v2 whole, which is shorter than its diff:
```python
import functools
import math

import jax
import jax.numpy as jnp
from jax import lax
from jax.experimental import pallas as pl
from jax.experimental.pallas import tpu as pltpu
from jax.sharding import PartitionSpec as P

BAND = 2
AXES = ("blk", "help")
ANY = pl.BlockSpec(memory_space=pl.ANY)
VMEM = pl.BlockSpec(memory_space=pltpu.VMEM)
SMEM = pl.BlockSpec(memory_space=pltpu.SMEM)
NT = (((1,), (1,)), ((), ()))
NN = (((1,), (0,)), ((), ()))
TN = (((0,), (0,)), ((), ()))


def move(block, source):
    blks, helps = lax.axis_size("blk"), lax.axis_size("help")
    route = []
    for b in range(blks):
        for h in range(helps):
            sb, sh = source(b, h)
            route.append(((sb % blks) * helps + sh, b * helps + h))
    return lax.ppermute(block, AXES, route)


def step_two(b, h, sign, blks):
    other = (b + 2 * sign) % blks
    half = blks // 2
    return (other, h if other // half == b // half else h ^ 1)


def window(block):
    blks = lax.axis_size("blk")
    swap = lambda b, h: (b ^ 1, h)
    one = move(block, lambda b, h: step_two(b, h, 1 if b % 2 == 0 else -1, blks))
    zero = move(block, swap)
    two = move(block, lambda b, h: step_two(b, h, -1 if b % 2 == 0 else 1, blks))
    three = move(one, swap)
    return (block, zero, one, two, three)


def load_all(refs, places, sems):
    copies = [
        pltpu.make_async_copy(ref, place, sems.at[i])
        for i, (ref, place) in enumerate(zip(refs, places))
    ]
    for copy in copies:
        copy.start()
    return copies


def add_pairs(pairs, rows, tiles, acc, piece, axis, dims):
    tile = tiles.shape[1]
    count = rows.shape[0]
    unroll = count // 2

    @pl.loop(0, count // unroll)
    def _(step):
        for j in range(unroll):
            i = step * unroll + j
            one, two = pairs[2 * i], pairs[2 * i + 1]
            left = jnp.concatenate([tiles[one & 127], tiles[two & 127]], axis=1)
            right = jnp.concatenate(
                [piece(pl.multiple_of((s >> 7) * tile, tile)) for s in (one, two)], axis=axis
            )
            product = lax.dot_general(left, right, dims, preferred_element_type=jnp.float32)
            acc[pl.ds(pl.multiple_of(rows[i] * tile, tile), tile), :] += product


def forward_kernel(pairs, rows, b0, b1, b2, b3, b4, tiles, cot, bias, out, win, acc, sems, stage, out_sems):
    tile = tiles.shape[1]
    nodes = cot.shape[1]
    refs = (b0, b1, b2, b3, b4)
    copies = load_all(refs, [win.at[:, i * nodes : (i + 1) * nodes] for i in range(5)], sems)
    acc[...] = jnp.zeros_like(acc)
    win[:, 5 * nodes :] = jnp.zeros((win.shape[0], tile), jnp.bfloat16)
    mine = nodes // out.shape[0]
    share = cot.shape[0]
    high = bias[...].astype(jnp.bfloat16)
    rest = bias[...] - high.astype(jnp.float32)
    middle = rest.astype(jnp.bfloat16)
    low = (rest - middle.astype(jnp.float32)).astype(jnp.bfloat16)
    lane = lax.broadcasted_iota(jnp.int32, (share, out.shape[2] - mine), 1)
    parts = jnp.where(lane == 0, high, jnp.where(lane == 1, middle, low))
    for h in range(out.shape[0]):
        stage[h, mine:, :mine] = cot[:, h * mine : (h + 1) * mine]
        stage[h, mine:, mine:] = parts
    for copy in copies:
        copy.wait()
    add_pairs(pairs, rows, tiles, acc, lambda c: win[:, pl.ds(c, tile)], 1, NT)
    leaving = []
    for h in range(out.shape[0]):
        stage[h, :mine, :] = acc[h * mine : (h + 1) * mine, :].astype(jnp.bfloat16)
        leaving.append(pltpu.make_async_copy(stage.at[h], out.at[h], out_sems.at[h]))
        leaving[h].start()
    for copy in leaving:
        copy.wait()


def backward_kernel(pairs, rows, b0, b1, b2, b3, b4, tiles, out, win, acc, sems, stage, out_sems):
    tile = tiles.shape[1]
    helps, share, nodes = out.shape
    width = helps * share
    refs = (b0, b1, b2, b3, b4)
    copies = load_all(refs, [win.at[i * nodes : (i + 1) * nodes, :] for i in range(5)], sems)
    acc[...] = jnp.zeros_like(acc)
    win[5 * nodes :, :] = jnp.zeros((tile, win.shape[1]), jnp.bfloat16)
    for copy in copies:
        copy.wait()
    add_pairs(pairs, rows, tiles, acc, lambda c: win[pl.ds(c, tile), :], 0, NN)
    eye = (
        lax.broadcasted_iota(jnp.int32, (width, width), 0)
        == lax.broadcasted_iota(jnp.int32, (width, width), 1)
    ).astype(jnp.bfloat16)
    for t in range(nodes // tile):
        part = acc[t * tile : (t + 1) * tile, :].astype(jnp.bfloat16)
        turned = lax.dot_general(eye, part, NT, preferred_element_type=jnp.float32)
        stage[:, :, t * tile : (t + 1) * tile] = turned.astype(jnp.bfloat16).reshape(helps, share, tile)
    leaving = [pltpu.make_async_copy(stage.at[h], out.at[h], out_sems.at[h]) for h in range(helps)]
    for copy in leaving:
        copy.start()
    for copy in leaving:
        copy.wait()


def aggregate(kernel, blocks, tiles, slots, out_shape, *extra):
    count, tile = tiles.shape[0], tiles.shape[1]
    nodes = max(blocks[0].shape)
    width = min(blocks[0].shape)
    forward = blocks[0].shape[1] == nodes
    span = 5 * nodes + tile
    parts = out_shape[0]
    return pl.pallas_call(
        kernel,
        out_shape=pltpu.HBM(out_shape, jnp.bfloat16),
        in_specs=[SMEM] * 2 + [ANY] * 5 + [VMEM] * (1 + len(extra)),
        out_specs=ANY,
        scratch_shapes=[
            pltpu.VMEM((width, span) if forward else (span, width), jnp.bfloat16),
            pltpu.VMEM((nodes + tile, width), jnp.float32),
            pltpu.SemaphoreType.DMA((5,)),
            pltpu.VMEM(out_shape, jnp.bfloat16),
            pltpu.SemaphoreType.DMA((parts,)),
        ],
        compiler_params=pltpu.CompilerParams(vmem_limit_bytes=20 * 2**20),
        cost_estimate=pl.CostEstimate(
            flops=2 * count * tile * tile * width,
            bytes_accessed=6 * 2**20,
            transcendentals=0,
        ),
    )(*slots, *blocks, tiles, *extra)


def prepare_kernel(row_tiles, odd, rows, cols, tiles, cot, own, pairs, heads, tiles_v, cot_v, own_v, following, sems):
    copies = load_all((tiles, cot, own), (tiles_v, cot_v, own_v), sems)
    spans = 2 * BAND + 1
    count = rows.shape[0]
    for r in range(row_tiles + 1):
        following[r] = 0

    @pl.loop(0, count, unroll=4)
    def _(k):
        r = rows[k]
        following[r] = following[r] + 1

    first = jnp.int32(0)
    for r in range(row_tiles):
        used = following[r]
        following[r] = first
        first = first + ((used + 1) >> 1) * 2
    following[row_tiles] = jnp.int32(pairs.shape[0])

    @pl.loop(0, heads.shape[0], unroll=4)
    def _(i):
        heads[i] = row_tiles
        pairs[2 * i] = 128 * spans * row_tiles
        pairs[2 * i + 1] = 128 * spans * row_tiles

    swapped = odd[0] == 1

    @pl.loop(0, count, unroll=4)
    def _(k):
        r = rows[k]
        place = following[r]
        following[r] = place + 1
        span = jnp.int32(0)
        for s in range(1, spans):
            span = span + (cols[k] >= s * row_tiles).astype(jnp.int32)
        even = jnp.where(span >= 2, span - 2, span + 3)
        other = jnp.where(span <= 2, 2 - span, 7 - span)
        buf = jnp.where(swapped, other, even)
        flat = buf * row_tiles + cols[k] - span * row_tiles

        @pl.when(r < row_tiles)
        def _():
            pairs[place] = k + 128 * flat
            heads[place >> 1] = r

    for copy in copies:
        copy.wait()


def middle_kernel(parts, weight_t, back, side):
    mine = back.shape[1]
    total = parts[0, :mine].astype(jnp.float32)
    for s in range(1, parts.shape[0]):
        total = total + parts[s, :mine].astype(jnp.float32)
    agg = total.astype(jnp.bfloat16)
    cotb = jnp.concatenate([parts[s, mine:] for s in range(parts.shape[0])], axis=0)
    extra = cotb[:, mine : mine + 64].astype(jnp.float32)
    bias = extra[:, 0:1] + extra[:, 1:2] + extra[:, 2:3]
    pre = lax.dot_general(weight_t[...], agg, NT, preferred_element_type=jnp.float32) + bias
    decay = jnp.exp(jnp.minimum(pre, 0.0))
    slope = jnp.where(pre > 0.0, 1.0, decay)
    grad = (cotb[:, :mine].astype(jnp.float32) * slope).astype(jnp.bfloat16)
    back_n = lax.dot_general(
        grad, weight_t[...], TN, preferred_element_type=jnp.float32
    ).astype(jnp.bfloat16)
    for s in range(back.shape[0]):
        back[s] = back_n
    width = agg.shape[1]
    side[:, :width] = lax.dot_general(
        grad, agg, NN, preferred_element_type=jnp.float32
    ).astype(jnp.bfloat16)
    side[:, width : width + mine] = jnp.where(pre > 0.0, pre, decay - 1.0).astype(jnp.bfloat16)
    rest = side.shape[1] - width - mine
    sums = jnp.sum(grad.astype(jnp.float32), axis=1, keepdims=True)
    high = sums.astype(jnp.bfloat16)
    low = (sums - high.astype(jnp.float32)).astype(jnp.bfloat16)
    lane = lax.broadcasted_iota(jnp.int32, (width, rest), 1)
    side[:, width + mine :] = jnp.where(lane == 0, high, low)


def side_kernel(parts, out, total):
    width = total.shape[1] - 128
    nodes = out.shape[1] // parts.shape[0]
    sums = parts[0].astype(jnp.float32)
    for s in range(1, parts.shape[0]):
        sums = sums + parts[s].astype(jnp.float32)
    for s in range(parts.shape[0]):
        out[:, s * nodes : (s + 1) * nodes] = parts[s, :, width : width + nodes]
    total[:, :width] = sums[:, :width]
    at = width + nodes
    both = sums[:, at : at + 1] + sums[:, at + 1 : at + 2]
    total[:, width:] = jnp.broadcast_to(both, (total.shape[0], 128))


def spread(x):
    return lax.all_to_all(x, "help", 0, 0)


def small_call(kernel, outs, *args):
    return pl.pallas_call(
        kernel,
        out_shape=tuple(jax.ShapeDtypeStruct(*o) for o in outs),
        in_specs=[VMEM] * len(args),
        out_specs=(VMEM,) * len(outs),
        compiler_params=pltpu.CompilerParams(vmem_limit_bytes=16 * 2**20),
    )(*args)


def after(value, other):
    return lax.optimization_barrier((value, other))[0]


def per_device(features_t, weight, bias, cotangent_t, tile_vals, slot_row, slot_col):
    tiles = tile_vals[0, 0]
    tile = tiles.shape[-1]
    width, nodes = features_t.shape
    row_tiles = nodes // tile
    helps = lax.axis_size("help")
    blks = lax.axis_size("blk")
    share = cotangent_t.shape[0]
    mine = nodes // helps
    count = tiles.shape[0]

    pair_count = (count + row_tiles + 3) // 4 * 2
    own = features_t
    around = window(own)[1:]
    pairs, heads, tiles, cot, own = pl.pallas_call(
        functools.partial(prepare_kernel, row_tiles),
        out_shape=(
            jax.ShapeDtypeStruct((2 * pair_count,), jnp.int32),
            jax.ShapeDtypeStruct((pair_count,), jnp.int32),
            pltpu.VMEM(tiles.shape, jnp.bfloat16),
            pltpu.VMEM(cotangent_t.shape, jnp.bfloat16),
            pltpu.VMEM(own.shape, jnp.bfloat16),
        ),
        in_specs=[SMEM] * 3 + [ANY] * 3,
        out_specs=(SMEM,) * 2 + (ANY,) * 3,
        scratch_shapes=[pltpu.SMEM((row_tiles + 1,), jnp.int32), pltpu.SemaphoreType.DMA((3,))],
        compiler_params=pltpu.CompilerParams(vmem_limit_bytes=2 * 2**20),
    )(
        (lax.axis_index("blk") % 2).astype(jnp.int32).reshape(1),
        slot_row[0, 0],
        slot_col[0, 0],
        tiles,
        cotangent_t,
        own,
    )
    slots = (pairs, heads)

    sent = aggregate(
        forward_kernel,
        (own, *around),
        tiles,
        slots,
        (helps, mine + share, width),
        cot,
        bias.reshape(share, 1),
    )
    back, side = small_call(
        middle_kernel,
        [((helps, mine, width), jnp.bfloat16), ((width, 2 * width), jnp.bfloat16)],
        spread(sent),
        weight.T,
    )
    back_full = spread(back).reshape(nodes, width)
    blocks = window(back_full)
    value = aggregate(backward_kernel, blocks, tiles, slots, (helps, share, nodes))
    summed = spread(value)
    propagated = jnp.sum(summed.astype(jnp.float32), axis=0)

    side = after(side.reshape(helps, share, 2 * width), back_full)
    output, total = small_call(
        side_kernel,
        [((share, nodes), jnp.bfloat16), ((share, width + tile), jnp.float32)],
        spread(side),
    )
    flip = lambda s: functools.partial(lambda s, b, h: (b ^ s, h), s)
    total = (total + move(total, flip(1))) + (
        move(total, flip(blks // 2)) + move(total, flip(blks // 2 + 1))
    )
    step = 2
    while step < blks // 2:
        if step == blks // 8:
            total = after(total, blocks[3])
        if step == blks // 4:
            total = after(total, value)
        total = total + move(total, flip(step))
        step *= 2
    total = total * (1.0 / math.sqrt(nodes * blks))
    return (output, propagated, total[:, :width].T, total[:, width])


def solution(mesh):
    placed = (
        P(None, "blk"),
        P(),
        P("help"),
        P("help", "blk"),
        P("blk", "help", None, None, None),
        P("blk", "help", None),
        P("blk", "help", None),
    )
    return jax.shard_map(
        per_device,
        mesh=mesh,
        in_specs=placed,
        out_specs=(P("help", "blk"), P("help", "blk"), P(None, "help"), P("help")),
        check_vma=False,
    )
```

time: 187 us -> 178 us (0.952)
  the two profiles are of different devices: /device:TPU:34 before, /device:TPU:2 now
where the time goes in v2:
time: 178 us
  waiting for transfers between devices  62.9 us (35%)
  starting transfers between devices  62.5 us (35%)
  blocking collectives  26.8 us (15%)
  Pallas kernels  14.1 us (8%)
  local copies, waits for them, and re-layouts  9.62 us (5%)
    ppermute x15, starting transfers between devices, move(): return lax.ppermute(block, AXES, route)  51.8 us
    ppermute x15, waiting for transfers between devices, move(): return lax.ppermute(block, AXES, route)  50.8 us
    all_to_all x2, blocking collectives, spread(): return lax.all_to_all(x, 'help', 0, 0)  26.8 us
    all_to_all x2, waiting for transfers between devices, spread(): return lax.all_to_all(x, 'help', 0, 0)  12.1 us
    all_to_all x2, starting transfers between devices, spread(): return lax.all_to_all(x, 'help', 0, 0)  10.7 us
    pallas_call x2, Pallas kernels, aggregate(): pl.pallas_call(kernel, out_shape=pltpu.HBM(out_shape, jnp.bfloat16), in_s...  9.65 us
    unnamed x13, local copies, waits for them, and re-layouts  7.64 us
  transfers between devices with their start and end apart: 17, of which 8 were waited for; matrix products, arithmetic and copies ran while one was open for 2% of the time, Pallas kernels for 4%

profile of v2, /device:TPU:2, one launch (start us, length us, event | category | flops | bytes accessed | tf_op | source)
XLA Modules:
  0.0 177.5 jit_solution(8181312687256966517)
XLA Ops:
  0.6 12.3 %collective-permute-start.1 = (bf16[256,1536]{1,0:T(8,128)(2,1)}, bf16[256,1536]{1,0:T(8,128)(2,1)S(1)}, u32[]{:S(2)}, u32[]{:S(2)}) collective-permute-start(bf16[256,1536]{1,0:T(8,128)(2,1)} %own.1), channel_id=1, source_target_pairs={{16,0},{17,1},{18,2},{19,3},{20,4},{21,5},{22,6},{23,7},{505,8},{5... | collective-permute-start | bytes 2359304 | tf_op jit(solution)/shard_map/ppermute | solution.py:28
  13.0 1.9 %collective-permute-start = (bf16[256,1536]{1,0:T(8,128)(2,1)}, bf16[256,1536]{1,0:T(8,128)(2,1)}, u32[]{:S(2)}, u32[]{:S(2)}) collective-permute-start(bf16[256,1536]{1,0:T(8,128)(2,1)} %own.1), channel_id=1, source_target_pairs={{8,0},{9,1},{10,2},{11,3},{12,4},{13,5},{14,6},{15,7},{0,8},{1,9},... | collective-permute-start | bytes 2359304 | tf_op jit(solution)/shard_map/ppermute | solution.py:28
  14.9 1.9 %collective-permute-start.2 = (bf16[256,1536]{1,0:T(8,128)(2,1)}, bf16[256,1536]{1,0:T(8,128)(2,1)}, u32[]{:S(2)}, u32[]{:S(2)}) collective-permute-start(bf16[256,1536]{1,0:T(8,128)(2,1)} %own.1), channel_id=1, source_target_pairs={{497,0},{496,1},{499,2},{498,3},{501,4},{500,5},{503,6},{502,7},{2... | collective-permute-start | bytes 2359304 | tf_op jit(solution)/shard_map/ppermute | solution.py:28
  16.8 9.9 %collective-permute-done.1.b2 = bf16[256,1536]{1,0:T(8,128)(2,1)S(1)} collective-permute-done((bf16[256,1536]{1,0:T(8,128)(2,1)}, bf16[256,1536]{1,0:T(8,128)(2,1)S(1)}, u32[]{:S(2)}, u32[]{:S(2)}) %collective-permute-start.1) | collective-permute-done | bytes 786464 | tf_op jit(solution)/shard_map/ppermute | solution.py:28
  34.5 3.1 %shard_map.102 = (s32[92]{0:T(128)S(1)}, s32[46]{0:T(128)S(1)}, bf16[80,128,128]{2,1,0:T(8,128)(2,1)S(1)}, bf16[32,1536]{1,0:T(8,128)(2,1)S(1)}, bf16[256,1536]{1,0:T(8,128)(2,1)S(1)}) custom-call(s32[1]{0:T(128)} %bitcast.odd, s32[80]{0:T(128)S(1)} %bitcast.17, s32[80]{0:T(128)S(1)} %bitcast.18, bf16[80,128,128]{2,1,0:T(8,128)(2,1)S(1)} %bitcast.14, ...), custom_call_target="tpu_custom_call" | custom-call | tf_op jit(solution)/shard_map/pallas_call | solution.py:285
  37.6 5.6 %shard_map.103 = bf16[8,224,256]{2,1,0:T(8,128)(2,1)} custom-call(s32[92]{0:T(128)S(1)} %get-tuple-element.16.pairs, s32[46]{0:T(128)S(1)} %get-tuple-element.17.rows, bf16[256,1536]{1,0:T(8,128)(2,1)S(1)} %get-tuple-element.18.b0, bf16[256,1536]{1,0:T(8,128)(2,1)} %collective-permute-done.b1, bf16[256,1536]{1,0:T(8,128)(2,1)S(1)} %collective-permute-done.1.b2, ...), custom_call_target="tpu_custom_call" | custom-call | flops 671088640 | bytes 6291456 | tf_op jit(solution)/shard_map/pallas_call | solution.py:138
  43.3 6.3 %all-to-all-start = ((bf16[8,224,256]{2,1,0:T(8,128)(2,1)}), bf16[8,224,256]{2,1,0:T(8,128)(2,1)S(1)}, u32[]{:S(2)}, u32[]{:S(2)}) async-start(bf16[8,224,256]{2,1,0:T(8,128)(2,1)} %shard_map.103), calls=%async_computation | async-start | bytes 1835008 | tf_op jit(solution)/shard_map/all_to_all | solution.py:254
  51.2 12.1 %all-to-all-done.parts = bf16[8,224,256]{2,1,0:T(8,128)(2,1)S(1)} async-done(((bf16[8,224,256]{2,1,0:T(8,128)(2,1)}), bf16[8,224,256]{2,1,0:T(8,128)(2,1)S(1)}, u32[]{:S(2)}, u32[]{:S(2)}) %all-to-all-start) | async-done | bytes 917536 | tf_op jit(solution)/shard_map/all_to_all | solution.py:254
  64.9 15.6 %all_to_all.20 = bf16[8,192,256]{2,1,0:T(8,128)(2,1)S(1)} all-to-all(bf16[8,192,256]{2,1,0:T(8,128)(2,1)S(1)} %get-tuple-element.22), channel_id=1, replica_groups=mesh['blk'=64,'help'=8] {'help'}, dimensions={0} | all-to-all | bytes 1572864 | tf_op jit(solution)/shard_map/all_to_all | solution.py:254
  80.5 7.7 %collective-permute-start.5 = (bf16[1536,256]{1,0:T(8,128)(2,1)S(1)}, bf16[1536,256]{1,0:T(8,128)(2,1)S(1)}, u32[]{:S(2)}, u32[]{:S(2)}) collective-permute-start(bf16[1536,256]{1,0:T(8,128)(2,1)S(1)} %bitcast.10), channel_id=1, source_target_pairs={{16,0},{17,1},{18,2},{19,3},{20,4},{21,5},{22,6},{23,7},{505,8},{5... | collective-permute-start | bytes 2359304 | tf_op jit(solution)/shard_map/ppermute | solution.py:28
  88.2 1.9 %collective-permute-start.6 = (bf16[1536,256]{1,0:T(8,128)(2,1)S(1)}, bf16[1536,256]{1,0:T(8,128)(2,1)S(1)}, u32[]{:S(2)}, u32[]{:S(2)}) collective-permute-start(bf16[1536,256]{1,0:T(8,128)(2,1)S(1)} %bitcast.11), channel_id=1, source_target_pairs={{497,0},{496,1},{499,2},{498,3},{501,4},{500,5},{503,6},{502,7},{2... | collective-permute-start | bytes 2359304 | tf_op jit(solution)/shard_map/ppermute | solution.py:28
  92.1 13.6 %collective-permute-done.5.b2 = bf16[1536,256]{1,0:T(8,128)(2,1)S(1)} collective-permute-done((bf16[1536,256]{1,0:T(8,128)(2,1)S(1)}, bf16[1536,256]{1,0:T(8,128)(2,1)S(1)}, u32[]{:S(2)}, u32[]{:S(2)}) %collective-permute-start.5) | collective-permute-done | bytes 786464 | tf_op jit(solution)/shard_map/ppermute | solution.py:28
  107.6 11.1 %all_to_all.21.parts = bf16[8,32,512]{2,1,0:T(8,128)(2,1)S(1)} all-to-all(bf16[8,32,512]{2,1,0:T(8,128)(2,1)S(1)} %bitcast.16), channel_id=1, replica_groups=mesh['blk'=64,'help'=8] {'help'}, dimensions={0} | all-to-all | bytes 524288 | tf_op jit(solution)/shard_map/all_to_all | solution.py:254
  121.4 1.9 %collective-permute-start.8 = (f32[32,384]{1,0:T(8,128)S(1)}, f32[32,384]{1,0:T(8,128)S(1)}, u32[]{:S(2)}, u32[]{:S(2)}) collective-permute-start(f32[32,384]{1,0:T(8,128)S(1)} %get-tuple-element.25), channel_id=1, source_target_pairs={{8,0},{9,1},{10,2},{11,3},{12,4},{13,5},{14,6},{15,7},{0,8},{1,9},... | collective-permute-start | bytes 147464 | tf_op jit(solution)/shard_map/ppermute | solution.py:28
  123.3 3.4 %collective-permute-done.10 = f32[32,384]{1,0:T(8,128)S(1)} collective-permute-done((f32[32,384]{1,0:T(8,128)S(1)}, f32[32,384]{1,0:T(8,128)S(1)}, u32[]{:S(2)}, u32[]{:S(2)}) %collective-permute-start.10) | collective-permute-done | bytes 49184 | tf_op jit(solution)/shard_map/ppermute | solution.py:28
  126.7 2.1 %collective-permute-start.9 = (f32[32,384]{1,0:T(8,128)S(1)}, f32[32,384]{1,0:T(8,128)S(1)}, u32[]{:S(2)}, u32[]{:S(2)}) collective-permute-start(f32[32,384]{1,0:T(8,128)S(1)} %get-tuple-element.25), channel_id=1, source_target_pairs={{256,0},{257,1},{258,2},{259,3},{260,4},{261,5},{262,6},{263,7},{2... | collective-permute-start | bytes 147464 | tf_op jit(solution)/shard_map/ppermute | solution.py:28
  128.9 5.4 %collective-permute-done.9 = f32[32,384]{1,0:T(8,128)S(1)} collective-permute-done((f32[32,384]{1,0:T(8,128)S(1)}, f32[32,384]{1,0:T(8,128)S(1)}, u32[]{:S(2)}, u32[]{:S(2)}) %collective-permute-start.9) | collective-permute-done | bytes 49184 | tf_op jit(solution)/shard_map/ppermute | solution.py:28
  136.2 4.1 %collective-permute-done.11 = f32[32,384]{1,0:T(8,128)S(1)} collective-permute-done((f32[32,384]{1,0:T(8,128)S(1)}, f32[32,384]{1,0:T(8,128)S(1)}, u32[]{:S(2)}, u32[]{:S(2)}) %collective-permute-start.11) | collective-permute-done | bytes 49184 | tf_op jit(solution)/shard_map/ppermute | solution.py:28
  140.2 1.9 %collective-permute-start.12 = (f32[32,384]{1,0:T(8,128)S(1)}, f32[32,384]{1,0:T(8,128)S(1)}, u32[]{:S(2)}, u32[]{:S(2)}) collective-permute-start(f32[32,384]{1,0:T(8,128)S(1)} %add.29), channel_id=1, source_target_pairs={{32,0},{33,1},{34,2},{35,3},{36,4},{37,5},{38,6},{39,7},{40,8},{41... | collective-permute-start | bytes 147464 | tf_op jit(solution)/shard_map/ppermute | solution.py:28
  142.2 4.0 %shard_map.106 = bf16[8,32,1536]{2,1,0:T(8,128)(2,1)} custom-call(s32[92]{0:T(128)S(1)} %get-tuple-element.16.pairs, s32[46]{0:T(128)S(1)} %get-tuple-element.17.rows, bf16[1536,256]{1,0:T(8,128)(2,1)S(1)} %bitcast.13, bf16[1536,256]{1,0:T(8,128)(2,1)S(1)} %collective-permute-done.4.b1, bf16[1536,256]{1,0:T(8,128)(2,1)S(1)} %collective-permute-done.5.b2, ...), custom_call_target="tpu_custom_call" | custom-call | flops 671088640 | bytes 6291456 | tf_op jit(solution)/shard_map/pallas_call | solution.py:138
  146.2 4.4 %all-to-all-start.3 = ((bf16[8,32,1536]{2,1,0:T(8,128)(2,1)}), bf16[8,32,1536]{2,1,0:T(8,128)(2,1)S(1)}, u32[]{:S(2)}, u32[]{:S(2)}) async-start(bf16[8,32,1536]{2,1,0:T(8,128)(2,1)} %shard_map.106), calls=%async_computation.3 | async-start | bytes 1572864 | tf_op jit(solution)/shard_map/all_to_all | solution.py:254
  152.5 8.0 %collective-permute-done.13 = f32[32,384]{1,0:T(8,128)S(1)} collective-permute-done((f32[32,384]{1,0:T(8,128)S(1)}, f32[32,384]{1,0:T(8,128)S(1)}, u32[]{:S(2)}, u32[]{:S(2)}) %collective-permute-start.13) | collective-permute-done | bytes 49184 | tf_op jit(solution)/shard_map/ppermute | solution.py:28
  160.5 8.5 %collective-permute-start.14 = (f32[32,384]{1,0:T(8,128)S(1)}, f32[32,384]{1,0:T(8,128)S(1)}, u32[]{:S(2)}, u32[]{:S(2)}) collective-permute-start(f32[32,384]{1,0:T(8,128)S(1)} %add.31), channel_id=1, source_target_pairs={{128,0},{129,1},{130,2},{131,3},{132,4},{133,5},{134,6},{135,7},{1... | collective-permute-start | bytes 147464 | tf_op jit(solution)/shard_map/ppermute | solution.py:28
  169.0 6.4 %collective-permute-done.14 = f32[32,384]{1,0:T(8,128)S(1)} collective-permute-done((f32[32,384]{1,0:T(8,128)S(1)}, f32[32,384]{1,0:T(8,128)S(1)}, u32[]{:S(2)}, u32[]{:S(2)}) %collective-permute-start.14) | collective-permute-done | bytes 49184 | tf_op jit(solution)/shard_map/ppermute | solution.py:28
  (39 shorter events, 23.3 us)
Async XLA Ops:
  0.6 26.1 %collective-permute-start.1 = (bf16[256,1536]{1,0:T(8,128)(2,1)}, bf16[256,1536]{1,0:T(8,128)(2,1)S(1)}, u32[]{:S(2)}, u32[]{:S(2)}) collective-permute-start(bf16[256,1536]{1,0:T(8,128)(2,1)} %own.1), channel_id=1, source_target_pairs={{16,0},{17,1},{18,2},{19,3},{20,4},{21,5},{22,6},{23,7},{505,8},{5... | collective-permute-start | bytes 2359304 | tf_op jit(solution)/shard_map/ppermute | solution.py:28
  13.0 24.6 %collective-permute-start = (bf16[256,1536]{1,0:T(8,128)(2,1)}, bf16[256,1536]{1,0:T(8,128)(2,1)}, u32[]{:S(2)}, u32[]{:S(2)}) collective-permute-start(bf16[256,1536]{1,0:T(8,128)(2,1)} %own.1), channel_id=1, source_target_pairs={{8,0},{9,1},{10,2},{11,3},{12,4},{13,5},{14,6},{15,7},{0,8},{1,9},... | collective-permute-start | bytes 2359304 | tf_op jit(solution)/shard_map/ppermute | solution.py:28
  14.9 22.7 %collective-permute-start.2 = (bf16[256,1536]{1,0:T(8,128)(2,1)}, bf16[256,1536]{1,0:T(8,128)(2,1)}, u32[]{:S(2)}, u32[]{:S(2)}) collective-permute-start(bf16[256,1536]{1,0:T(8,128)(2,1)} %own.1), channel_id=1, source_target_pairs={{497,0},{496,1},{499,2},{498,3},{501,4},{500,5},{503,6},{502,7},{2... | collective-permute-start | bytes 2359304 | tf_op jit(solution)/shard_map/ppermute | solution.py:28
  26.7 10.9 %collective-permute-start.3 = (bf16[256,1536]{1,0:T(8,128)(2,1)S(1)}, bf16[256,1536]{1,0:T(8,128)(2,1)}, u32[]{:S(2)}, u32[]{:S(2)}) collective-permute-start(bf16[256,1536]{1,0:T(8,128)(2,1)S(1)} %collective-permute-done.1.b2), channel_id=1, source_target_pairs={{8,0},{9,1},{10,2},{11,3},{12,4},{13,5},{14,6},{15,7},{0,8},{1,9},... | collective-permute-start | bytes 2359304 | tf_op jit(solution)/shard_map/ppermute | solution.py:28
  29.4 1.7 copy-start
  31.1 1.1 copy-start.1
  32.3 0.9 copy-start.3
  33.2 0.7 copy-start.4
  33.8 0.7 copy-start.5
  43.3 20.1 %all-to-all-start = ((bf16[8,224,256]{2,1,0:T(8,128)(2,1)}), bf16[8,224,256]{2,1,0:T(8,128)(2,1)S(1)}, u32[]{:S(2)}, u32[]{:S(2)}) async-start(bf16[8,224,256]{2,1,0:T(8,128)(2,1)} %shard_map.103), calls=%async_computation | async-start | bytes 1835008 | tf_op jit(solution)/shard_map/all_to_all | solution.py:254
  63.3 0.9 copy-start.2
  80.5 25.2 %collective-permute-start.5 = (bf16[1536,256]{1,0:T(8,128)(2,1)S(1)}, bf16[1536,256]{1,0:T(8,128)(2,1)S(1)}, u32[]{:S(2)}, u32[]{:S(2)}) collective-permute-start(bf16[1536,256]{1,0:T(8,128)(2,1)S(1)} %bitcast.10), channel_id=1, source_target_pairs={{16,0},{17,1},{18,2},{19,3},{20,4},{21,5},{22,6},{23,7},{505,8},{5... | collective-permute-start | bytes 2359304 | tf_op jit(solution)/shard_map/ppermute | solution.py:28
  88.2 53.9 %collective-permute-start.6 = (bf16[1536,256]{1,0:T(8,128)(2,1)S(1)}, bf16[1536,256]{1,0:T(8,128)(2,1)S(1)}, u32[]{:S(2)}, u32[]{:S(2)}) collective-permute-start(bf16[1536,256]{1,0:T(8,128)(2,1)S(1)} %bitcast.11), channel_id=1, source_target_pairs={{497,0},{496,1},{499,2},{498,3},{501,4},{500,5},{503,6},{502,7},{2... | collective-permute-start | bytes 2359304 | tf_op jit(solution)/shard_map/ppermute | solution.py:28
  90.1 52.0 %collective-permute-start.4 = (bf16[1536,256]{1,0:T(8,128)(2,1)S(1)}, bf16[1536,256]{1,0:T(8,128)(2,1)S(1)}, u32[]{:S(2)}, u32[]{:S(2)}) collective-permute-start(bf16[1536,256]{1,0:T(8,128)(2,1)S(1)} %bitcast.12), channel_id=1, source_target_pairs={{8,0},{9,1},{10,2},{11,3},{12,4},{13,5},{14,6},{15,7},{0,8},{1,9},... | collective-permute-start | bytes 2359304 | tf_op jit(solution)/shard_map/ppermute | solution.py:28
  105.7 36.5 %collective-permute-start.7 = (bf16[1536,256]{1,0:T(8,128)(2,1)S(1)}, bf16[1536,256]{1,0:T(8,128)(2,1)S(1)}, u32[]{:S(2)}, u32[]{:S(2)}) collective-permute-start(bf16[1536,256]{1,0:T(8,128)(2,1)S(1)} %collective-permute-done.5.b2), channel_id=1, source_target_pairs={{8,0},{9,1},{10,2},{11,3},{12,4},{13,5},{14,6},{15,7},{0,8},{1,9},... | collective-permute-start | bytes 2359304 | tf_op jit(solution)/shard_map/ppermute | solution.py:28
  119.5 7.3 %collective-permute-start.10 = (f32[32,384]{1,0:T(8,128)S(1)}, f32[32,384]{1,0:T(8,128)S(1)}, u32[]{:S(2)}, u32[]{:S(2)}) collective-permute-start(f32[32,384]{1,0:T(8,128)S(1)} %get-tuple-element.25), channel_id=1, source_target_pairs={{264,0},{265,1},{266,2},{267,3},{268,4},{269,5},{270,6},{271,7},{2... | collective-permute-start | bytes 147464 | tf_op jit(solution)/shard_map/ppermute | solution.py:28
  121.4 7.5 %collective-permute-start.8 = (f32[32,384]{1,0:T(8,128)S(1)}, f32[32,384]{1,0:T(8,128)S(1)}, u32[]{:S(2)}, u32[]{:S(2)}) collective-permute-start(f32[32,384]{1,0:T(8,128)S(1)} %get-tuple-element.25), channel_id=1, source_target_pairs={{8,0},{9,1},{10,2},{11,3},{12,4},{13,5},{14,6},{15,7},{0,8},{1,9},... | collective-permute-start | bytes 147464 | tf_op jit(solution)/shard_map/ppermute | solution.py:28
  126.7 7.5 %collective-permute-start.9 = (f32[32,384]{1,0:T(8,128)S(1)}, f32[32,384]{1,0:T(8,128)S(1)}, u32[]{:S(2)}, u32[]{:S(2)}) collective-permute-start(f32[32,384]{1,0:T(8,128)S(1)} %get-tuple-element.25), channel_id=1, source_target_pairs={{256,0},{257,1},{258,2},{259,3},{260,4},{261,5},{262,6},{263,7},{2... | collective-permute-start | bytes 147464 | tf_op jit(solution)/shard_map/ppermute | solution.py:28
  134.2 6.0 %collective-permute-start.11 = (f32[32,384]{1,0:T(8,128)S(1)}, f32[32,384]{1,0:T(8,128)S(1)}, u32[]{:S(2)}, u32[]{:S(2)}) collective-permute-start(f32[32,384]{1,0:T(8,128)S(1)} %add_add_fusion), channel_id=1, source_target_pairs={{16,0},{17,1},{18,2},{19,3},{20,4},{21,5},{22,6},{23,7},{24,8},{25... | collective-permute-start | bytes 147464 | tf_op jit(solution)/shard_map/ppermute | solution.py:28
  140.2 10.4 %collective-permute-start.12 = (f32[32,384]{1,0:T(8,128)S(1)}, f32[32,384]{1,0:T(8,128)S(1)}, u32[]{:S(2)}, u32[]{:S(2)}) collective-permute-start(f32[32,384]{1,0:T(8,128)S(1)} %add.29), channel_id=1, source_target_pairs={{32,0},{33,1},{34,2},{35,3},{36,4},{37,5},{38,6},{39,7},{40,8},{41... | collective-permute-start | bytes 147464 | tf_op jit(solution)/shard_map/ppermute | solution.py:28
  146.2 30.5 %all-to-all-start.3 = ((bf16[8,32,1536]{2,1,0:T(8,128)(2,1)}), bf16[8,32,1536]{2,1,0:T(8,128)(2,1)S(1)}, u32[]{:S(2)}, u32[]{:S(2)}) async-start(bf16[8,32,1536]{2,1,0:T(8,128)(2,1)} %shard_map.106), calls=%async_computation.3 | async-start | bytes 1572864 | tf_op jit(solution)/shard_map/all_to_all | solution.py:254
  150.6 9.9 %collective-permute-start.13 = (f32[32,384]{1,0:T(8,128)S(1)}, f32[32,384]{1,0:T(8,128)S(1)}, u32[]{:S(2)}, u32[]{:S(2)}) collective-permute-start(f32[32,384]{1,0:T(8,128)S(1)} %add.30), channel_id=1, source_target_pairs={{64,0},{65,1},{66,2},{67,3},{68,4},{69,5},{70,6},{71,7},{72,8},{73... | collective-permute-start | bytes 147464 | tf_op jit(solution)/shard_map/ppermute | solution.py:28
  160.5 14.9 %collective-permute-start.14 = (f32[32,384]{1,0:T(8,128)S(1)}, f32[32,384]{1,0:T(8,128)S(1)}, u32[]{:S(2)}, u32[]{:S(2)}) collective-permute-start(f32[32,384]{1,0:T(8,128)S(1)} %add.31), channel_id=1, source_target_pairs={{128,0},{129,1},{130,2},{131,3},{132,4},{133,5},{134,6},{135,7},{1... | collective-permute-start | bytes 147464 | tf_op jit(solution)/shard_map/ppermute | solution.py:28

commit v3 on v2

v3 whole, which is shorter than its diff:
```python
import functools
import math

import jax
import jax.numpy as jnp
from jax import lax
from jax.experimental import pallas as pl
from jax.experimental.pallas import tpu as pltpu
from jax.sharding import PartitionSpec as P

BAND = 2
AXES = ("blk", "help")
ANY = pl.BlockSpec(memory_space=pl.ANY)
VMEM = pl.BlockSpec(memory_space=pltpu.VMEM)
SMEM = pl.BlockSpec(memory_space=pltpu.SMEM)
NT = (((1,), (1,)), ((), ()))
NN = (((1,), (0,)), ((), ()))
TN = (((0,), (0,)), ((), ()))


def move(block, source):
    blks, helps = lax.axis_size("blk"), lax.axis_size("help")
    route = []
    for b in range(blks):
        for h in range(helps):
            sb, sh = source(b, h)
            route.append(((sb % blks) * helps + sh, b * helps + h))
    return lax.ppermute(block, AXES, route)


def step_two(b, h, sign, blks):
    other = (b + 2 * sign) % blks
    half = blks // 2
    return (other, h if other // half == b // half else h ^ 1)


def after(value, other):
    return lax.optimization_barrier((value, other))[0]


def near(block):
    blks = lax.axis_size("blk")
    one = move(block, lambda b, h: step_two(b, h, 1 if b % 2 == 0 else -1, blks))
    zero = move(block, lambda b, h: (b ^ 1, h))
    two = move(block, lambda b, h: step_two(b, h, -1 if b % 2 == 0 else 1, blks))
    return zero, one, two


def load_all(refs, places, sems):
    copies = [
        pltpu.make_async_copy(ref, place, sems.at[i])
        for i, (ref, place) in enumerate(zip(refs, places))
    ]
    for copy in copies:
        copy.start()
    return copies


def add_pairs(pairs, rows, tiles, acc, piece, axis, dims):
    tile = tiles.shape[1]
    count = rows.shape[0]
    unroll = count // 2

    @pl.loop(0, count // unroll)
    def _(step):
        for j in range(unroll):
            i = step * unroll + j
            one, two = pairs[2 * i], pairs[2 * i + 1]
            left = jnp.concatenate([tiles[one & 127], tiles[two & 127]], axis=1)
            right = jnp.concatenate(
                [piece(pl.multiple_of((s >> 7) * tile, tile)) for s in (one, two)], axis=axis
            )
            product = lax.dot_general(left, right, dims, preferred_element_type=jnp.float32)
            acc[pl.ds(pl.multiple_of(rows[i] * tile, tile), tile), :] += product


def forward_kernel(pairs, rows, b0, b1, b2, b3, b4, tiles, extra, out, win, acc, sems, stage, out_sems):
    tile = tiles.shape[1]
    nodes = b0.shape[1]
    helps = out.shape[0]
    mine = nodes // helps
    refs = (b0, b1, b2, b3, b4)
    copies = load_all(refs, [win.at[:, i * nodes : (i + 1) * nodes] for i in range(5)], sems)
    leaving = []
    for h in range(helps):
        leaving.append(pltpu.make_async_copy(extra.at[h], out.at[h, mine:], out_sems.at[helps + h]))
        leaving[h].start()
    acc[...] = jnp.zeros_like(acc)
    win[:, 5 * nodes :] = jnp.zeros((win.shape[0], tile), jnp.bfloat16)
    for copy in copies:
        copy.wait()
    add_pairs(pairs, rows, tiles, acc, lambda c: win[:, pl.ds(c, tile)], 1, NT)
    for h in range(helps):
        stage[h] = acc[h * mine : (h + 1) * mine, :].astype(jnp.bfloat16)
        leaving.append(pltpu.make_async_copy(stage.at[h], out.at[h, :mine], out_sems.at[h]))
        leaving[helps + h].start()
    for copy in leaving:
        copy.wait()


def backward_kernel(pairs, rows, b0, b1, b2, b3, b4, tiles, out, win, acc, sems, stage, out_sems):
    tile = tiles.shape[1]
    helps, share, nodes = out.shape
    width = helps * share
    refs = (b0, b1, b2, b3, b4)
    copies = load_all(refs, [win.at[i * nodes : (i + 1) * nodes, :] for i in range(5)], sems)
    acc[...] = jnp.zeros_like(acc)
    win[5 * nodes :, :] = jnp.zeros((tile, win.shape[1]), jnp.bfloat16)
    for copy in copies:
        copy.wait()
    add_pairs(pairs, rows, tiles, acc, lambda c: win[pl.ds(c, tile), :], 0, NN)
    eye = (
        lax.broadcasted_iota(jnp.int32, (width, width), 0)
        == lax.broadcasted_iota(jnp.int32, (width, width), 1)
    ).astype(jnp.bfloat16)
    for t in range(nodes // tile):
        part = acc[t * tile : (t + 1) * tile, :].astype(jnp.bfloat16)
        turned = lax.dot_general(eye, part, NT, preferred_element_type=jnp.float32)
        stage[:, :, t * tile : (t + 1) * tile] = turned.astype(jnp.bfloat16).reshape(helps, share, tile)
    leaving = [pltpu.make_async_copy(stage.at[h], out.at[h], out_sems.at[h]) for h in range(helps)]
    for copy in leaving:
        copy.start()
    for copy in leaving:
        copy.wait()


def aggregate(kernel, blocks, tiles, slots, out_shape, *extra):
    count, tile = tiles.shape[0], tiles.shape[1]
    nodes = max(blocks[0].shape)
    width = min(blocks[0].shape)
    forward = blocks[0].shape[1] == nodes
    span = 5 * nodes + tile
    parts = out_shape[0]
    return pl.pallas_call(
        kernel,
        out_shape=pltpu.HBM(out_shape, jnp.bfloat16),
        in_specs=[SMEM] * 2 + [ANY] * 5 + [VMEM] + [ANY] * len(extra),
        out_specs=ANY,
        scratch_shapes=[
            pltpu.VMEM((width, span) if forward else (span, width), jnp.bfloat16),
            pltpu.VMEM((nodes + tile, width), jnp.float32),
            pltpu.SemaphoreType.DMA((5,)),
            pltpu.VMEM((parts, nodes // parts, width) if forward else out_shape, jnp.bfloat16),
            pltpu.SemaphoreType.DMA((2 * parts,)),
        ],
        compiler_params=pltpu.CompilerParams(vmem_limit_bytes=20 * 2**20),
        cost_estimate=pl.CostEstimate(
            flops=2 * count * tile * tile * width,
            bytes_accessed=6 * 2**20,
            transcendentals=0,
        ),
    )(*slots, *blocks, tiles, *extra)


def prepare_kernel(row_tiles, odd, rows, cols, bias, tiles, cot, own, pairs, heads, extra, tiles_v, own_v, following, cot_v, sems):
    copies = load_all((tiles, cot, own), (tiles_v, cot_v, own_v), sems)
    spans = 2 * BAND + 1
    count = rows.shape[0]
    for r in range(row_tiles + 1):
        following[r] = 0

    @pl.loop(0, count, unroll=4)
    def _(k):
        r = rows[k]
        following[r] = following[r] + 1

    first = jnp.int32(0)
    for r in range(row_tiles):
        used = following[r]
        following[r] = first
        first = first + ((used + 1) >> 1) * 2
    following[row_tiles] = jnp.int32(pairs.shape[0])

    @pl.loop(0, heads.shape[0], unroll=4)
    def _(i):
        heads[i] = row_tiles
        pairs[2 * i] = 128 * spans * row_tiles
        pairs[2 * i + 1] = 128 * spans * row_tiles

    swapped = odd[0] == 1

    @pl.loop(0, count, unroll=4)
    def _(k):
        r = rows[k]
        place = following[r]
        following[r] = place + 1
        span = jnp.int32(0)
        for s in range(1, spans):
            span = span + (cols[k] >= s * row_tiles).astype(jnp.int32)
        even = jnp.where(span >= 2, span - 2, span + 3)
        other = jnp.where(span <= 2, 2 - span, 7 - span)
        buf = jnp.where(swapped, other, even)
        flat = buf * row_tiles + cols[k] - span * row_tiles

        @pl.when(r < row_tiles)
        def _():
            pairs[place] = k + 128 * flat
            heads[place >> 1] = r

    helps, share, lanes = extra.shape
    mine = cot_v.shape[1] // helps
    high = bias[...].astype(jnp.bfloat16)
    rest = bias[...] - high.astype(jnp.float32)
    middle = rest.astype(jnp.bfloat16)
    low = (rest - middle.astype(jnp.float32)).astype(jnp.bfloat16)
    lane = lax.broadcasted_iota(jnp.int32, (share, lanes - mine), 1)
    bias_parts = jnp.where(lane == 0, high, jnp.where(lane == 1, middle, low))
    for copy in copies:
        copy.wait()
    for h in range(helps):
        extra[h, :, :mine] = cot_v[:, h * mine : (h + 1) * mine]
        extra[h, :, mine:] = bias_parts


def middle_kernel(parts, weight_t, out):
    helps, length, width = out.shape
    share = width // helps
    mine = length - 2 * share
    total = parts[0, :mine].astype(jnp.float32)
    for s in range(1, helps):
        total = total + parts[s, :mine].astype(jnp.float32)
    agg = total.astype(jnp.bfloat16)
    cotb = jnp.concatenate([parts[s, mine:] for s in range(helps)], axis=0)
    extra = cotb[:, mine:].astype(jnp.float32)
    bias = extra[:, 0:1] + extra[:, 1:2] + extra[:, 2:3]
    pre = lax.dot_general(weight_t[...], agg, NT, preferred_element_type=jnp.float32) + bias
    decay = jnp.exp(jnp.minimum(pre, 0.0))
    slope = jnp.where(pre > 0.0, 1.0, decay)
    grad = (cotb[:, :mine].astype(jnp.float32) * slope).astype(jnp.bfloat16)
    back = lax.dot_general(
        grad, weight_t[...], TN, preferred_element_type=jnp.float32
    ).astype(jnp.bfloat16)
    terms = lax.dot_general(grad, agg, NN, preferred_element_type=jnp.float32).astype(jnp.bfloat16)
    result = jnp.where(pre > 0.0, pre, decay - 1.0).astype(jnp.bfloat16)
    sums = jnp.sum(grad.astype(jnp.float32), axis=1, keepdims=True)
    high = sums.astype(jnp.bfloat16)
    low = (sums - high.astype(jnp.float32)).astype(jnp.bfloat16)
    lane = lax.broadcasted_iota(jnp.int32, (width, width - mine), 1)
    sums = jnp.where(lane == 0, high, low)
    for h in range(helps):
        own = slice(h * share, (h + 1) * share)
        out[h, :mine, :] = back
        out[h, mine : mine + share, :] = terms[own]
        out[h, mine + share :, :mine] = result[own]
        out[h, mine + share :, mine:] = sums[own]


def divide_kernel(parts, back, out, total, side, sems):
    helps, _, width = parts.shape
    mine = back.shape[0] // helps
    share = total.shape[0]
    copies = []
    for s in range(helps):
        copies.append(pltpu.make_async_copy(parts.at[s, mine:], side.at[s], sems.at[s]))
        copies.append(
            pltpu.make_async_copy(
                parts.at[s, :mine], back.at[s * mine : (s + 1) * mine], sems.at[helps + s]
            )
        )
    for copy in copies:
        copy.start()
    for copy in copies[0::2]:
        copy.wait()
    sums = side[0].astype(jnp.float32)
    for s in range(1, helps):
        sums = sums + side[s].astype(jnp.float32)
    total[:, :width] = sums[:share]
    both = sums[share:, mine : mine + 1] + sums[share:, mine + 1 : mine + 2]
    total[:, width:] = jnp.broadcast_to(both, (share, total.shape[1] - width))
    for s in range(helps):
        out[:, s * mine : (s + 1) * mine] = side[s, share:, :mine]
    for copy in copies[1::2]:
        copy.wait()


def spread(x):
    return lax.all_to_all(x, "help", 0, 0)


def round_of_four(total, one, two):
    got = [
        move(total, functools.partial(lambda s, b, h: (b ^ s, h), s)) for s in (one, two, one ^ two)
    ]
    return (total + got[0]) + (got[1] + got[2])


def per_device(features_t, weight, bias, cotangent_t, tile_vals, slot_row, slot_col):
    tiles = tile_vals[0, 0]
    tile = tiles.shape[-1]
    width, nodes = features_t.shape
    row_tiles = nodes // tile
    helps = lax.axis_size("help")
    blks = lax.axis_size("blk")
    share = cotangent_t.shape[0]
    mine = nodes // helps
    count = tiles.shape[0]
    swap = lambda b, h: (b ^ 1, h)

    zero, one, two = near(features_t)
    pair_count = (count + row_tiles + 3) // 4 * 2
    pairs, heads, extra, tiles, own = pl.pallas_call(
        functools.partial(prepare_kernel, row_tiles),
        out_shape=(
            jax.ShapeDtypeStruct((2 * pair_count,), jnp.int32),
            jax.ShapeDtypeStruct((pair_count,), jnp.int32),
            jax.ShapeDtypeStruct((helps, share, width), jnp.bfloat16),
            pltpu.VMEM(tiles.shape, jnp.bfloat16),
            pltpu.VMEM(features_t.shape, jnp.bfloat16),
        ),
        in_specs=[SMEM] * 3 + [VMEM] + [ANY] * 3,
        out_specs=(SMEM,) * 2 + (VMEM,) + (ANY,) * 2,
        scratch_shapes=[
            pltpu.SMEM((row_tiles + 1,), jnp.int32),
            pltpu.VMEM(cotangent_t.shape, jnp.bfloat16),
            pltpu.SemaphoreType.DMA((3,)),
        ],
        compiler_params=pltpu.CompilerParams(vmem_limit_bytes=4 * 2**20),
    )(
        (lax.axis_index("blk") % 2).astype(jnp.int32).reshape(1),
        slot_row[0, 0],
        slot_col[0, 0],
        bias.reshape(share, 1),
        tiles,
        cotangent_t,
        features_t,
    )
    slots = (pairs, heads)
    three = move(after(one, own), swap)
    sent = aggregate(
        forward_kernel,
        (own, zero, one, two, three),
        tiles,
        slots,
        (helps, mine + share, width),
        extra,
    )
    length = mine + 2 * share
    sent = pl.pallas_call(
        middle_kernel,
        out_shape=jax.ShapeDtypeStruct((helps, length, width), jnp.bfloat16),
        in_specs=[VMEM] * 2,
        out_specs=VMEM,
        compiler_params=pltpu.CompilerParams(vmem_limit_bytes=16 * 2**20),
    )(spread(sent), weight.T)
    back, output, total = pl.pallas_call(
        divide_kernel,
        out_shape=(
            pltpu.VMEM((nodes, width), jnp.bfloat16),
            jax.ShapeDtypeStruct((share, nodes), jnp.bfloat16),
            jax.ShapeDtypeStruct((share, width + tile), jnp.float32),
        ),
        in_specs=[ANY],
        out_specs=(ANY, VMEM, VMEM),
        scratch_shapes=[
            pltpu.VMEM((helps, 2 * share, width), jnp.bfloat16),
            pltpu.SemaphoreType.DMA((2 * helps,)),
        ],
        compiler_params=pltpu.CompilerParams(vmem_limit_bytes=4 * 2**20),
    )(spread(sent))
    zero, one, two = near(back)
    half = blks // 2
    total = round_of_four(total, 1, half)
    total = round_of_four(total, 2, 4)
    three = move(after(one, (total, two)), swap)
    value = aggregate(
        backward_kernel, (back, zero, one, two, three), tiles, slots, (helps, share, nodes)
    )
    propagated = jnp.sum(spread(value).astype(jnp.float32), axis=0)
    total = round_of_four(total, 8, 16)
    total = total * (1.0 / math.sqrt(nodes * blks))
    return (output, propagated, total[:, :width].T, total[:, width])


def solution(mesh):
    placed = (
        P(None, "blk"),
        P(),
        P("help"),
        P("help", "blk"),
        P("blk", "help", None, None, None),
        P("blk", "help", None),
        P("blk", "help", None),
    )
    return jax.shard_map(
        per_device,
        mesh=mesh,
        in_specs=placed,
        out_specs=(P("help", "blk"), P("help", "blk"), P(None, "help"), P("help")),
        check_vma=False,
    )
```

time: 178 us -> 156 us (0.88)
  the two profiles are of different devices: /device:TPU:2 before, /device:TPU:1 now
where the time goes in v3:
time: 156 us; the launch traced here: 154 us
  starting transfers between devices  85.6 us (55%)
  waiting for transfers between devices  25.8 us (17%)
  Pallas kernels  15.6 us (10%)
  blocking collectives  15.5 us (10%)
  local copies, waits for them, and re-layouts  9.62 us (6%)
    ppermute x17, starting transfers between devices, move(): return lax.ppermute(block, AXES, route)  77.9 us
    all_to_all x1, blocking collectives, spread(): return lax.all_to_all(x, 'help', 0, 0)  15.5 us
    ppermute x17, waiting for transfers between devices, move(): return lax.ppermute(block, AXES, route)  15 us
    all_to_all x2, waiting for transfers between devices, spread(): return lax.all_to_all(x, 'help', 0, 0)  10.8 us
    pallas_call x2, Pallas kernels, aggregate(): pl.pallas_call(kernel, out_shape=pltpu.HBM(out_shape, jnp.bfloat16), in_s...  9.56 us
    all_to_all x2, starting transfers between devices, spread(): return lax.all_to_all(x, 'help', 0, 0)  7.74 us
    unnamed x13, local copies, waits for them, and re-layouts  7.64 us
    pallas_call x1, Pallas kernels, per_device(): pl.pallas_call(functools.partial(prepare_kernel, row_tiles), out_shape=(j...  3.18 us
  transfers between devices with their start and end apart: 19, of which 7 were waited for; matrix products, arithmetic and copies ran while one was open for 2% of the time, Pallas kernels for 2%

profile of v3, /device:TPU:1, one launch (start us, length us, event | category | flops | bytes accessed | tf_op | source)
XLA Modules:
  0.0 154.0 jit_solution(5245691669723869192)
XLA Ops:
  0.6 4.4 %collective-permute-start.1 = (bf16[256,1536]{1,0:T(8,128)(2,1)}, bf16[256,1536]{1,0:T(8,128)(2,1)S(1)}, u32[]{:S(2)}, u32[]{:S(2)}) collective-permute-start(bf16[256,1536]{1,0:T(8,128)(2,1)} %own.1), channel_id=1, source_target_pairs={{16,0},{17,1},{18,2},{19,3},{20,4},{21,5},{22,6},{23,7},{505,8},{5... | collective-permute-start | bytes 2359304 | tf_op jit(solution)/shard_map/ppermute | solution.py:28
  5.0 12.6 %collective-permute-start = (bf16[256,1536]{1,0:T(8,128)(2,1)}, bf16[256,1536]{1,0:T(8,128)(2,1)}, u32[]{:S(2)}, u32[]{:S(2)}) collective-permute-start(bf16[256,1536]{1,0:T(8,128)(2,1)} %own.1), channel_id=1, source_target_pairs={{8,0},{9,1},{10,2},{11,3},{12,4},{13,5},{14,6},{15,7},{0,8},{1,9},... | collective-permute-start | bytes 2359304 | tf_op jit(solution)/shard_map/ppermute | solution.py:28
  17.7 2.6 %collective-permute-start.2 = (bf16[256,1536]{1,0:T(8,128)(2,1)}, bf16[256,1536]{1,0:T(8,128)(2,1)}, u32[]{:S(2)}, u32[]{:S(2)}) collective-permute-start(bf16[256,1536]{1,0:T(8,128)(2,1)} %own.1), channel_id=1, source_target_pairs={{497,0},{496,1},{499,2},{498,3},{501,4},{500,5},{503,6},{502,7},{2... | collective-permute-start | bytes 2359304 | tf_op jit(solution)/shard_map/ppermute | solution.py:28
  26.1 3.2 %shard_map.102 = (s32[92]{0:T(128)S(1)}, s32[46]{0:T(128)S(1)}, bf16[8,32,256]{2,1,0:T(8,128)(2,1)S(1)}, bf16[80,128,128]{2,1,0:T(8,128)(2,1)S(1)}, bf16[256,1536]{1,0:T(8,128)(2,1)S(1)}) custom-call(s32[1]{0:T(128)} %bitcast.odd, s32[80]{0:T(128)S(1)} %bitcast.10, s32[80]{0:T(128)S(1)} %bitcast.11, f32[32,1]{1,0:T(8,128)S(1)} %copy.13.bias, ...), custom_call_target="tpu_custom_call" | custom-call | tf_op jit(solution)/shard_map/pallas_call | solution.py:301
  29.3 2.1 %collective-permute-start.3 = (bf16[256,1536]{1,0:T(8,128)(2,1)S(1)}, bf16[256,1536]{1,0:T(8,128)(2,1)S(1)}, u32[]{:S(2)}, u32[]{:S(2)}) collective-permute-start(bf16[256,1536]{1,0:T(8,128)(2,1)S(1)} %collective-permute-done.1.b2), channel_id=1, source_target_pairs={{8,0},{9,1},{10,2},{11,3},{12,4},{13,5},{14,6},{15,7},{0,8},{1,9},... | collective-permute-start | bytes 2359304 | tf_op jit(solution)/shard_map/ppermute | solution.py:28
  31.4 2.1 %collective-permute-done.2.b3 = bf16[256,1536]{1,0:T(8,128)(2,1)} collective-permute-done((bf16[256,1536]{1,0:T(8,128)(2,1)}, bf16[256,1536]{1,0:T(8,128)(2,1)}, u32[]{:S(2)}, u32[]{:S(2)}) %collective-permute-start.2) | collective-permute-done | bytes 786464 | tf_op jit(solution)/shard_map/ppermute | solution.py:28
  33.6 5.5 %shard_map.103 = bf16[8,224,256]{2,1,0:T(8,128)(2,1)} custom-call(s32[92]{0:T(128)S(1)} %get-tuple-element.14.pairs, s32[46]{0:T(128)S(1)} %get-tuple-element.15.rows, bf16[256,1536]{1,0:T(8,128)(2,1)S(1)} %get-tuple-element.16.b0, bf16[256,1536]{1,0:T(8,128)(2,1)} %collective-permute-done.b1, bf16[256,1536]{1,0:T(8,128)(2,1)S(1)} %collective-permute-done.1.b2, ...), custom_call_target="tpu_custom_call" | custom-call | flops 671088640 | bytes 6291456 | tf_op jit(solution)/shard_map/pallas_call | solution.py:134
  39.1 4.2 %all-to-all-start = ((bf16[8,224,256]{2,1,0:T(8,128)(2,1)}), bf16[8,224,256]{2,1,0:T(8,128)(2,1)S(1)}, u32[]{:S(2)}, u32[]{:S(2)}) async-start(bf16[8,224,256]{2,1,0:T(8,128)(2,1)} %shard_map.103), calls=%async_computation | async-start | bytes 1835008 | tf_op jit(solution)/shard_map/all_to_all | solution.py:277
  44.9 10.8 %all-to-all-done.parts = bf16[8,224,256]{2,1,0:T(8,128)(2,1)S(1)} async-done(((bf16[8,224,256]{2,1,0:T(8,128)(2,1)}), bf16[8,224,256]{2,1,0:T(8,128)(2,1)S(1)}, u32[]{:S(2)}, u32[]{:S(2)}) %all-to-all-start) | async-done | bytes 917536 | tf_op jit(solution)/shard_map/all_to_all | solution.py:277
  57.3 15.5 %all_to_all.15.parts = bf16[8,256,256]{2,1,0:T(8,128)(2,1)S(1)} all-to-all(bf16[8,256,256]{2,1,0:T(8,128)(2,1)S(1)} %shard_map.104), channel_id=1, replica_groups=mesh['blk'=64,'help'=8] {'help'}, dimensions={0} | all-to-all | bytes 2097152 | tf_op jit(solution)/shard_map/all_to_all | solution.py:277
  72.8 2.3 %shard_map.105 = (bf16[1536,256]{1,0:T(8,128)(2,1)S(1)}, bf16[32,1536]{1,0:T(8,128)(2,1)}, f32[32,384]{1,0:T(8,128)S(1)}) custom-call(bf16[8,256,256]{2,1,0:T(8,128)(2,1)S(1)} %all_to_all.15.parts), custom_call_target="tpu_custom_call" | custom-call | tf_op jit(solution)/shard_map/pallas_call | solution.py:345
  75.1 6.4 %collective-permute-start.5 = (bf16[1536,256]{1,0:T(8,128)(2,1)S(1)}, bf16[1536,256]{1,0:T(8,128)(2,1)S(1)}, u32[]{:S(2)}, u32[]{:S(2)}) collective-permute-start(bf16[1536,256]{1,0:T(8,128)(2,1)S(1)} %get-tuple-element.21.b0), channel_id=1, source_target_pairs={{16,0},{17,1},{18,2},{19,3},{20,4},{21,5},{22,6},{23,7},{505,8},{5... | collective-permute-start | bytes 2359304 | tf_op jit(solution)/shard_map/ppermute | solution.py:28
  81.5 6.9 %collective-permute-start.6 = (bf16[1536,256]{1,0:T(8,128)(2,1)S(1)}, bf16[1536,256]{1,0:T(8,128)(2,1)S(1)}, u32[]{:S(2)}, u32[]{:S(2)}) collective-permute-start(bf16[1536,256]{1,0:T(8,128)(2,1)S(1)} %get-tuple-element.21.b0), channel_id=1, source_target_pairs={{497,0},{496,1},{499,2},{498,3},{501,4},{500,5},{503,6},{502,7},{2... | collective-permute-start | bytes 2359304 | tf_op jit(solution)/shard_map/ppermute | solution.py:28
  88.5 3.9 %collective-permute-start.7 = (f32[32,384]{1,0:T(8,128)S(1)}, f32[32,384]{1,0:T(8,128)S(1)}, u32[]{:S(2)}, u32[]{:S(2)}) collective-permute-start(f32[32,384]{1,0:T(8,128)S(1)} %get-tuple-element.22), channel_id=1, source_target_pairs={{8,0},{9,1},{10,2},{11,3},{12,4},{13,5},{14,6},{15,7},{0,8},{1,9},... | collective-permute-start | bytes 147464 | tf_op jit(solution)/shard_map/ppermute | solution.py:28
  94.2 5.0 %collective-permute-start.9 = (f32[32,384]{1,0:T(8,128)S(1)}, f32[32,384]{1,0:T(8,128)S(1)}, u32[]{:S(2)}, u32[]{:S(2)}) collective-permute-start(f32[32,384]{1,0:T(8,128)S(1)} %get-tuple-element.22), channel_id=1, source_target_pairs={{264,0},{265,1},{266,2},{267,3},{268,4},{269,5},{270,6},{271,7},{2... | collective-permute-start | bytes 147464 | tf_op jit(solution)/shard_map/ppermute | solution.py:28
  99.4 4.0 %collective-permute-done.9 = f32[32,384]{1,0:T(8,128)S(1)} collective-permute-done((f32[32,384]{1,0:T(8,128)S(1)}, f32[32,384]{1,0:T(8,128)S(1)}, u32[]{:S(2)}, u32[]{:S(2)}) %collective-permute-start.9) | collective-permute-done | bytes 49184 | tf_op jit(solution)/shard_map/ppermute | solution.py:28
  107.3 5.4 %collective-permute-start.12 = (f32[32,384]{1,0:T(8,128)S(1)}, f32[32,384]{1,0:T(8,128)S(1)}, u32[]{:S(2)}, u32[]{:S(2)}) collective-permute-start(f32[32,384]{1,0:T(8,128)S(1)} %add_add_fusion.1), channel_id=1, source_target_pairs={{48,0},{49,1},{50,2},{51,3},{52,4},{53,5},{54,6},{55,7},{56,8},{57... | collective-permute-start | bytes 147464 | tf_op jit(solution)/shard_map/ppermute | solution.py:28
  112.7 2.1 %collective-permute-start.4 = (bf16[1536,256]{1,0:T(8,128)(2,1)S(1)}, bf16[1536,256]{1,0:T(8,128)(2,1)S(1)}, u32[]{:S(2)}, u32[]{:S(2)}) collective-permute-start(bf16[1536,256]{1,0:T(8,128)(2,1)S(1)} %get-tuple-element.21.b0), channel_id=1, source_target_pairs={{8,0},{9,1},{10,2},{11,3},{12,4},{13,5},{14,6},{15,7},{0,8},{1,9},... | collective-permute-start | bytes 2359304 | tf_op jit(solution)/shard_map/ppermute | solution.py:28
  114.9 2.5 %collective-permute-start.13 = (bf16[1536,256]{1,0:T(8,128)(2,1)S(1)}, bf16[1536,256]{1,0:T(8,128)(2,1)S(1)}, u32[]{:S(2)}, u32[]{:S(2)}) collective-permute-start(bf16[1536,256]{1,0:T(8,128)(2,1)S(1)} %collective-permute-done.5.b2), channel_id=1, source_target_pairs={{8,0},{9,1},{10,2},{11,3},{12,4},{13,5},{14,6},{15,7},{0,8},{1,9},... | collective-permute-start | bytes 2359304 | tf_op jit(solution)/shard_map/ppermute | solution.py:28
  119.3 4.1 %shard_map.106 = bf16[8,32,1536]{2,1,0:T(8,128)(2,1)} custom-call(s32[92]{0:T(128)S(1)} %get-tuple-element.14.pairs, s32[46]{0:T(128)S(1)} %get-tuple-element.15.rows, bf16[1536,256]{1,0:T(8,128)(2,1)S(1)} %get-tuple-element.21.b0, bf16[1536,256]{1,0:T(8,128)(2,1)S(1)} %collective-permute-done.4.b1, bf16[1536,256]{1,0:T(8,128)(2,1)S(1)} %collective-permute-done.5.b2, ...), custom_call_target="tpu_custom_call" | custom-call | flops 671088640 | bytes 6291456 | tf_op jit(solution)/shard_map/pallas_call | solution.py:134
  123.4 3.6 %all-to-all-start.2 = ((bf16[8,32,1536]{2,1,0:T(8,128)(2,1)}), bf16[8,32,1536]{2,1,0:T(8,128)(2,1)S(1)}, u32[]{:S(2)}, u32[]{:S(2)}) async-start(bf16[8,32,1536]{2,1,0:T(8,128)(2,1)} %shard_map.106), calls=%async_computation.2 | async-start | bytes 1572864 | tf_op jit(solution)/shard_map/all_to_all | solution.py:277
  127.0 4.5 %collective-permute-start.14 = (f32[32,384]{1,0:T(8,128)S(1)}, f32[32,384]{1,0:T(8,128)S(1)}, u32[]{:S(2)}, u32[]{:S(2)}) collective-permute-start(f32[32,384]{1,0:T(8,128)S(1)} %add_add_fusion), channel_id=1, source_target_pairs={{64,0},{65,1},{66,2},{67,3},{68,4},{69,5},{70,6},{71,7},{72,8},{73... | collective-permute-start | bytes 147464 | tf_op jit(solution)/shard_map/ppermute | solution.py:28
  131.5 11.7 %collective-permute-start.15 = (f32[32,384]{1,0:T(8,128)S(1)}, f32[32,384]{1,0:T(8,128)S(1)}, u32[]{:S(2)}, u32[]{:S(2)}) collective-permute-start(f32[32,384]{1,0:T(8,128)S(1)} %add_add_fusion), channel_id=1, source_target_pairs={{128,0},{129,1},{130,2},{131,3},{132,4},{133,5},{134,6},{135,7},{1... | collective-permute-start | bytes 147464 | tf_op jit(solution)/shard_map/ppermute | solution.py:28
  145.1 6.8 %collective-permute-done.16 = f32[32,384]{1,0:T(8,128)S(1)} collective-permute-done((f32[32,384]{1,0:T(8,128)S(1)}, f32[32,384]{1,0:T(8,128)S(1)}, u32[]{:S(2)}, u32[]{:S(2)}) %collective-permute-start.16) | collective-permute-done | bytes 49184 | tf_op jit(solution)/shard_map/ppermute | solution.py:28
  (40 shorter events, 20.8 us)
Async XLA Ops:
  0.6 28.7 %collective-permute-start.1 = (bf16[256,1536]{1,0:T(8,128)(2,1)}, bf16[256,1536]{1,0:T(8,128)(2,1)S(1)}, u32[]{:S(2)}, u32[]{:S(2)}) collective-permute-start(bf16[256,1536]{1,0:T(8,128)(2,1)} %own.1), channel_id=1, source_target_pairs={{16,0},{17,1},{18,2},{19,3},{20,4},{21,5},{22,6},{23,7},{505,8},{5... | collective-permute-start | bytes 2359304 | tf_op jit(solution)/shard_map/ppermute | solution.py:28
  5.0 26.4 %collective-permute-start = (bf16[256,1536]{1,0:T(8,128)(2,1)}, bf16[256,1536]{1,0:T(8,128)(2,1)}, u32[]{:S(2)}, u32[]{:S(2)}) collective-permute-start(bf16[256,1536]{1,0:T(8,128)(2,1)} %own.1), channel_id=1, source_target_pairs={{8,0},{9,1},{10,2},{11,3},{12,4},{13,5},{14,6},{15,7},{0,8},{1,9},... | collective-permute-start | bytes 2359304 | tf_op jit(solution)/shard_map/ppermute | solution.py:28
  17.7 15.9 %collective-permute-start.2 = (bf16[256,1536]{1,0:T(8,128)(2,1)}, bf16[256,1536]{1,0:T(8,128)(2,1)}, u32[]{:S(2)}, u32[]{:S(2)}) collective-permute-start(bf16[256,1536]{1,0:T(8,128)(2,1)} %own.1), channel_id=1, source_target_pairs={{497,0},{496,1},{499,2},{498,3},{501,4},{500,5},{503,6},{502,7},{2... | collective-permute-start | bytes 2359304 | tf_op jit(solution)/shard_map/ppermute | solution.py:28
  21.1 1.7 %copy-start = (bf16[1,1,80,128,128]{4,3,2,1,0:T(8,128)(2,1)S(1)}, bf16[1,1,80,128,128]{4,3,2,1,0:T(8,128)(2,1)}, u32[]{:S(2)}) copy-start(bf16[1,1,80,128,128]{4,3,2,1,0:T(8,128)(2,1)} %param.11) | copy-start | bytes 7864324
  22.8 1.1 copy-start.1
  23.9 0.9 copy-start.3
  24.8 0.7 copy-start.4
  29.3 4.2 %collective-permute-start.3 = (bf16[256,1536]{1,0:T(8,128)(2,1)S(1)}, bf16[256,1536]{1,0:T(8,128)(2,1)S(1)}, u32[]{:S(2)}, u32[]{:S(2)}) collective-permute-start(bf16[256,1536]{1,0:T(8,128)(2,1)S(1)} %collective-permute-done.1.b2), channel_id=1, source_target_pairs={{8,0},{9,1},{10,2},{11,3},{12,4},{13,5},{14,6},{15,7},{0,8},{1,9},... | collective-permute-start | bytes 2359304 | tf_op jit(solution)/shard_map/ppermute | solution.py:28
  39.1 16.7 %all-to-all-start = ((bf16[8,224,256]{2,1,0:T(8,128)(2,1)}), bf16[8,224,256]{2,1,0:T(8,128)(2,1)S(1)}, u32[]{:S(2)}, u32[]{:S(2)}) async-start(bf16[8,224,256]{2,1,0:T(8,128)(2,1)} %shard_map.103), calls=%async_computation | async-start | bytes 1835008 | tf_op jit(solution)/shard_map/all_to_all | solution.py:277
  55.8 0.9 copy-start.2
  75.1 39.8 %collective-permute-start.5 = (bf16[1536,256]{1,0:T(8,128)(2,1)S(1)}, bf16[1536,256]{1,0:T(8,128)(2,1)S(1)}, u32[]{:S(2)}, u32[]{:S(2)}) collective-permute-start(bf16[1536,256]{1,0:T(8,128)(2,1)S(1)} %get-tuple-element.21.b0), channel_id=1, source_target_pairs={{16,0},{17,1},{18,2},{19,3},{20,4},{21,5},{22,6},{23,7},{505,8},{5... | collective-permute-start | bytes 2359304 | tf_op jit(solution)/shard_map/ppermute | solution.py:28
  81.5 33.4 %collective-permute-start.6 = (bf16[1536,256]{1,0:T(8,128)(2,1)S(1)}, bf16[1536,256]{1,0:T(8,128)(2,1)S(1)}, u32[]{:S(2)}, u32[]{:S(2)}) collective-permute-start(bf16[1536,256]{1,0:T(8,128)(2,1)S(1)} %get-tuple-element.21.b0), channel_id=1, source_target_pairs={{497,0},{496,1},{499,2},{498,3},{501,4},{500,5},{503,6},{502,7},{2... | collective-permute-start | bytes 2359304 | tf_op jit(solution)/shard_map/ppermute | solution.py:28
  88.5 10.8 %collective-permute-start.7 = (f32[32,384]{1,0:T(8,128)S(1)}, f32[32,384]{1,0:T(8,128)S(1)}, u32[]{:S(2)}, u32[]{:S(2)}) collective-permute-start(f32[32,384]{1,0:T(8,128)S(1)} %get-tuple-element.22), channel_id=1, source_target_pairs={{8,0},{9,1},{10,2},{11,3},{12,4},{13,5},{14,6},{15,7},{0,8},{1,9},... | collective-permute-start | bytes 147464 | tf_op jit(solution)/shard_map/ppermute | solution.py:28
  92.3 7.1 %collective-permute-start.8 = (f32[32,384]{1,0:T(8,128)S(1)}, f32[32,384]{1,0:T(8,128)S(1)}, u32[]{:S(2)}, u32[]{:S(2)}) collective-permute-start(f32[32,384]{1,0:T(8,128)S(1)} %get-tuple-element.22), channel_id=1, source_target_pairs={{256,0},{257,1},{258,2},{259,3},{260,4},{261,5},{262,6},{263,7},{2... | collective-permute-start | bytes 147464 | tf_op jit(solution)/shard_map/ppermute | solution.py:28
  94.2 9.1 %collective-permute-start.9 = (f32[32,384]{1,0:T(8,128)S(1)}, f32[32,384]{1,0:T(8,128)S(1)}, u32[]{:S(2)}, u32[]{:S(2)}) collective-permute-start(f32[32,384]{1,0:T(8,128)S(1)} %get-tuple-element.22), channel_id=1, source_target_pairs={{264,0},{265,1},{266,2},{267,3},{268,4},{269,5},{270,6},{271,7},{2... | collective-permute-start | bytes 147464 | tf_op jit(solution)/shard_map/ppermute | solution.py:28
  103.4 9.3 %collective-permute-start.10 = (f32[32,384]{1,0:T(8,128)S(1)}, f32[32,384]{1,0:T(8,128)S(1)}, u32[]{:S(2)}, u32[]{:S(2)}) collective-permute-start(f32[32,384]{1,0:T(8,128)S(1)} %add_add_fusion.1), channel_id=1, source_target_pairs={{16,0},{17,1},{18,2},{19,3},{20,4},{21,5},{22,6},{23,7},{24,8},{25... | collective-permute-start | bytes 147464 | tf_op jit(solution)/shard_map/ppermute | solution.py:28
  105.3 9.5 %collective-permute-start.11 = (f32[32,384]{1,0:T(8,128)S(1)}, f32[32,384]{1,0:T(8,128)S(1)}, u32[]{:S(2)}, u32[]{:S(2)}) collective-permute-start(f32[32,384]{1,0:T(8,128)S(1)} %add_add_fusion.1), channel_id=1, source_target_pairs={{32,0},{33,1},{34,2},{35,3},{36,4},{37,5},{38,6},{39,7},{40,8},{41... | collective-permute-start | bytes 147464 | tf_op jit(solution)/shard_map/ppermute | solution.py:28
  107.3 7.6 %collective-permute-start.12 = (f32[32,384]{1,0:T(8,128)S(1)}, f32[32,384]{1,0:T(8,128)S(1)}, u32[]{:S(2)}, u32[]{:S(2)}) collective-permute-start(f32[32,384]{1,0:T(8,128)S(1)} %add_add_fusion.1), channel_id=1, source_target_pairs={{48,0},{49,1},{50,2},{51,3},{52,4},{53,5},{54,6},{55,7},{56,8},{57... | collective-permute-start | bytes 147464 | tf_op jit(solution)/shard_map/ppermute | solution.py:28
  112.7 4.7 %collective-permute-start.4 = (bf16[1536,256]{1,0:T(8,128)(2,1)S(1)}, bf16[1536,256]{1,0:T(8,128)(2,1)S(1)}, u32[]{:S(2)}, u32[]{:S(2)}) collective-permute-start(bf16[1536,256]{1,0:T(8,128)(2,1)S(1)} %get-tuple-element.21.b0), channel_id=1, source_target_pairs={{8,0},{9,1},{10,2},{11,3},{12,4},{13,5},{14,6},{15,7},{0,8},{1,9},... | collective-permute-start | bytes 2359304 | tf_op jit(solution)/shard_map/ppermute | solution.py:28
  114.9 4.4 %collective-permute-start.13 = (bf16[1536,256]{1,0:T(8,128)(2,1)S(1)}, bf16[1536,256]{1,0:T(8,128)(2,1)S(1)}, u32[]{:S(2)}, u32[]{:S(2)}) collective-permute-start(bf16[1536,256]{1,0:T(8,128)(2,1)S(1)} %collective-permute-done.5.b2), channel_id=1, source_target_pairs={{8,0},{9,1},{10,2},{11,3},{12,4},{13,5},{14,6},{15,7},{0,8},{1,9},... | collective-permute-start | bytes 2359304 | tf_op jit(solution)/shard_map/ppermute | solution.py:28
  123.4 29.8 %all-to-all-start.2 = ((bf16[8,32,1536]{2,1,0:T(8,128)(2,1)}), bf16[8,32,1536]{2,1,0:T(8,128)(2,1)S(1)}, u32[]{:S(2)}, u32[]{:S(2)}) async-start(bf16[8,32,1536]{2,1,0:T(8,128)(2,1)} %shard_map.106), calls=%async_computation.2 | async-start | bytes 1572864 | tf_op jit(solution)/shard_map/all_to_all | solution.py:277
  127.0 18.1 %collective-permute-start.14 = (f32[32,384]{1,0:T(8,128)S(1)}, f32[32,384]{1,0:T(8,128)S(1)}, u32[]{:S(2)}, u32[]{:S(2)}) collective-permute-start(f32[32,384]{1,0:T(8,128)S(1)} %add_add_fusion), channel_id=1, source_target_pairs={{64,0},{65,1},{66,2},{67,3},{68,4},{69,5},{70,6},{71,7},{72,8},{73... | collective-permute-start | bytes 147464 | tf_op jit(solution)/shard_map/ppermute | solution.py:28
  131.5 13.6 %collective-permute-start.15 = (f32[32,384]{1,0:T(8,128)S(1)}, f32[32,384]{1,0:T(8,128)S(1)}, u32[]{:S(2)}, u32[]{:S(2)}) collective-permute-start(f32[32,384]{1,0:T(8,128)S(1)} %add_add_fusion), channel_id=1, source_target_pairs={{128,0},{129,1},{130,2},{131,3},{132,4},{133,5},{134,6},{135,7},{1... | collective-permute-start | bytes 147464 | tf_op jit(solution)/shard_map/ppermute | solution.py:28
  143.2 8.7 %collective-permute-start.16 = (f32[32,384]{1,0:T(8,128)S(1)}, f32[32,384]{1,0:T(8,128)S(1)}, u32[]{:S(2)}, u32[]{:S(2)}) collective-permute-start(f32[32,384]{1,0:T(8,128)S(1)} %add_add_fusion), channel_id=1, source_target_pairs={{192,0},{193,1},{194,2},{195,3},{196,4},{197,5},{198,6},{199,7},{2... | collective-permute-start | bytes 147464 | tf_op jit(solution)/shard_map/ppermute | solution.py:28
  (1 other events, 0.7 us)

commit v4 on v3

--- a/solution.py
+++ b/solution.py
@@ -44,6 +44,13 @@
     zero = move(block, lambda b, h: (b ^ 1, h))
     two = move(block, lambda b, h: step_two(b, h, -1 if b % 2 == 0 else 1, blks))
     return zero, one, two
+
+
+def unit(size):
+    place = (size, size)
+    return (
+        lax.broadcasted_iota(jnp.int32, place, 0) == lax.broadcasted_iota(jnp.int32, place, 1)
+    ).astype(jnp.bfloat16)
 
 
 def load_all(refs, places, sems):
@@ -109,10 +116,7 @@
     for copy in copies:
         copy.wait()
     add_pairs(pairs, rows, tiles, acc, lambda c: win[pl.ds(c, tile), :], 0, NN)
-    eye = (
-        lax.broadcasted_iota(jnp.int32, (width, width), 0)
-        == lax.broadcasted_iota(jnp.int32, (width, width), 1)
-    ).astype(jnp.bfloat16)
+    eye = unit(width)
     for t in range(nodes // tile):
         part = acc[t * tile : (t + 1) * tile, :].astype(jnp.bfloat16)
         turned = lax.dot_general(eye, part, NT, preferred_element_type=jnp.float32)
@@ -152,8 +156,11 @@
     )(*slots, *blocks, tiles, *extra)
 
 
-def prepare_kernel(row_tiles, odd, rows, cols, bias, tiles, cot, own, pairs, heads, extra, tiles_v, own_v, following, cot_v, sems):
+def prepare_kernel(row_tiles, odd, rows, cols, bias, weight, tiles, cot, own, pairs, heads, extra, weight_t, tiles_v, own_v, following, cot_v, sems):
     copies = load_all((tiles, cot, own), (tiles_v, cot_v, own_v), sems)
+    weight_t[...] = lax.dot_general(
+        unit(weight.shape[0]), weight[...], NT, preferred_element_type=jnp.float32
+    ).astype(jnp.bfloat16)
     spans = 2 * BAND + 1
     count = rows.shape[0]
     for r in range(row_tiles + 1):
@@ -298,17 +305,18 @@
 
     zero, one, two = near(features_t)
     pair_count = (count + row_tiles + 3) // 4 * 2
-    pairs, heads, extra, tiles, own = pl.pallas_call(
+    pairs, heads, extra, weight_t, tiles, own = pl.pallas_call(
         functools.partial(prepare_kernel, row_tiles),
         out_shape=(
             jax.ShapeDtypeStruct((2 * pair_count,), jnp.int32),
             jax.ShapeDtypeStruct((pair_count,), jnp.int32),
             jax.ShapeDtypeStruct((helps, share, width), jnp.bfloat16),
+            jax.ShapeDtypeStruct(weight.shape, jnp.bfloat16),
             pltpu.VMEM(tiles.shape, jnp.bfloat16),
             pltpu.VMEM(features_t.shape, jnp.bfloat16),
         ),
-        in_specs=[SMEM] * 3 + [VMEM] + [ANY] * 3,
-        out_specs=(SMEM,) * 2 + (VMEM,) + (ANY,) * 2,
+        in_specs=[SMEM] * 3 + [VMEM] * 2 + [ANY] * 3,
+        out_specs=(SMEM,) * 2 + (VMEM,) * 2 + (ANY,) * 2,
         scratch_shapes=[
             pltpu.SMEM((row_tiles + 1,), jnp.int32),
             pltpu.VMEM(cotangent_t.shape, jnp.bfloat16),
@@ -320,9 +328,8 @@
         slot_row[0, 0],
         slot_col[0, 0],
         bias.reshape(share, 1),
-        tiles,
-        cotangent_t,
-        features_t,
+        weight,
+        *(pltpu.with_memory_space_constraint(x, pltpu.HBM) for x in (tiles, cotangent_t, features_t)),
     )
     slots = (pairs, heads)
     three = move(after(one, own), swap)
@@ -341,7 +348,7 @@
         in_specs=[VMEM] * 2,
         out_specs=VMEM,
         compiler_params=pltpu.CompilerParams(vmem_limit_bytes=16 * 2**20),
-    )(spread(sent), weight.T)
+    )(spread(sent), weight_t)
     back, output, total = pl.pallas_call(
         divide_kernel,
         out_shape=(
@@ -359,14 +366,14 @@
     )(spread(sent))
     zero, one, two = near(back)
     half = blks // 2
-    total = round_of_four(total, 1, half)
-    total = round_of_four(total, 2, 4)
-    three = move(after(one, (total, two)), swap)
+    total = after(round_of_four(total, 1, half), two)
+    three = move(after(one, total), swap)
+    total = round_of_four(total, 8, 16)
     value = aggregate(
         backward_kernel, (back, zero, one, two, three), tiles, slots, (helps, share, nodes)
     )
     propagated = jnp.sum(spread(value).astype(jnp.float32), axis=0)
-    total = round_of_four(total, 8, 16)
+    total = round_of_four(total, 2, 4)
     total = total * (1.0 / math.sqrt(nodes * blks))
     return (output, propagated, total[:, :width].T, total[:, width])
 

time: 156 us -> 147 us (0.942)
  blocking collectives: 15.5 us -> 32.1 us
  waiting for transfers between devices: 25.8 us -> 10.7 us
  local copies, waits for them, and re-layouts: 9.62 us -> 4.19 us
  starting transfers between devices: 85.6 us -> 81.2 us
    all_to_all x1 -> x2, blocking collectives: 15.5 us -> 32.1 us  [spread(): return lax.all_to_all(x, 'help', 0, 0)]
    all_to_all x2 -> x1, waiting for transfers between devices: 10.8 us -> 0.01 us  [spread(): return lax.all_to_all(x, 'help', 0, 0)]
    unnamed x13 -> x6, local copies, waits for them, and re-layouts: 7.64 us -> 2.21 us
    ppermute x17, waiting for transfers between devices: 15 us -> 10.7 us  [move(): return lax.ppermute(block, AXES, route)]
    all_to_all x2 -> x1, starting transfers between devices: 7.74 us -> 3.56 us  [spread(): return lax.all_to_all(x, 'help', 0, 0)]
  transfers between devices with their start and end apart: 19 -> 18, of which waited for: 7 -> 3; matrix products, arithmetic and copies ran while one was open for 2% -> 1% of each run, Pallas kernels for 2% -> 5%
where the time goes in v4:
time: 147 us; the launch traced here: 144 us
  starting transfers between devices  81.2 us (55%)
  blocking collectives  32.1 us (22%)
  Pallas kernels  14.5 us (10%)
  waiting for transfers between devices  10.7 us (7%)
  local copies, waits for them, and re-layouts  4.19 us (3%)
    ppermute x17, starting transfers between devices, move(): return lax.ppermute(block, AXES, route)  77.7 us
    all_to_all x2, blocking collectives, spread(): return lax.all_to_all(x, 'help', 0, 0)  32.1 us
    ppermute x17, waiting for transfers between devices, move(): return lax.ppermute(block, AXES, route)  10.7 us
    pallas_call x2, Pallas kernels, aggregate(): pl.pallas_call(kernel, out_shape=pltpu.HBM(out_shape, jnp.bfloat16), in_s...  8.47 us
    all_to_all x1, starting transfers between devices, spread(): return lax.all_to_all(x, 'help', 0, 0)  3.56 us
    pallas_call x1, Pallas kernels, per_device(): pl.pallas_call(functools.partial(prepare_kernel, row_tiles), out_shape=(j...  3.13 us
  transfers between devices with their start and end apart: 18, of which 3 were waited for; matrix products, arithmetic and copies ran while one was open for 1% of the time, Pallas kernels for 5%

profile of v4, /device:TPU:1, one launch (start us, length us, event | category | flops | bytes accessed | tf_op | source)
XLA Modules:
  0.0 144.5 jit_solution(12311592051373507982)
XLA Ops:
  0.6 4.4 %collective-permute-start.1 = (bf16[256,1536]{1,0:T(8,128)(2,1)}, bf16[256,1536]{1,0:T(8,128)(2,1)S(1)}, u32[]{:S(2)}, u32[]{:S(2)}) collective-permute-start(bf16[256,1536]{1,0:T(8,128)(2,1)} %own.1), channel_id=1, source_target_pairs={{16,0},{17,1},{18,2},{19,3},{20,4},{21,5},{22,6},{23,7},{505,8},{5... | collective-permute-start | bytes 2359304 | tf_op jit(solution)/shard_map/ppermute | solution.py:28
  5.0 12.6 %collective-permute-start = (bf16[256,1536]{1,0:T(8,128)(2,1)}, bf16[256,1536]{1,0:T(8,128)(2,1)S(1)}, u32[]{:S(2)}, u32[]{:S(2)}) collective-permute-start(bf16[256,1536]{1,0:T(8,128)(2,1)} %own.1), channel_id=1, source_target_pairs={{8,0},{9,1},{10,2},{11,3},{12,4},{13,5},{14,6},{15,7},{0,8},{1,9},... | collective-permute-start | bytes 2359304 | tf_op jit(solution)/shard_map/ppermute | solution.py:28
  17.7 2.6 %collective-permute-start.2 = (bf16[256,1536]{1,0:T(8,128)(2,1)}, bf16[256,1536]{1,0:T(8,128)(2,1)S(1)}, u32[]{:S(2)}, u32[]{:S(2)}) collective-permute-start(bf16[256,1536]{1,0:T(8,128)(2,1)} %own.1), channel_id=1, source_target_pairs={{497,0},{496,1},{499,2},{498,3},{501,4},{500,5},{503,6},{502,7},{2... | collective-permute-start | bytes 2359304 | tf_op jit(solution)/shard_map/ppermute | solution.py:28
  23.3 3.1 %shard_map.102 = (s32[92]{0:T(128)S(1)}, s32[46]{0:T(128)S(1)}, bf16[8,32,256]{2,1,0:T(8,128)(2,1)S(1)}, bf16[256,256]{1,0:T(8,128)(2,1)S(1)}, bf16[80,128,128]{...) custom-call(s32[1]{0:T(128)} %bitcast.odd, s32[80]{0:T(128)S(1)} %bitcast.7, s32[80]{0:T(128)S(1)} %bitcast.8, ...), custom_call_target="tpu_custom_call" | custom-call | tf_op jit(solution)/shard_map/pallas_call | solution.py:308
  26.4 5.0 %collective-permute-start.3 = (bf16[256,1536]{1,0:T(8,128)(2,1)S(1)}, bf16[256,1536]{1,0:T(8,128)(2,1)S(1)}, u32[]{:S(2)}, u32[]{:S(2)}) collective-permute-start(bf16[256,1536]{1,0:T(8,128)(2,1)S(1)} %collective-permute-done.1.b2), channel_id=1, source_target_pairs={{8,0},{9,1},{10,2},{11,3},{12,4},{13,5},{14,6},{15,7},{0,8},{1,9},... | collective-permute-start | bytes 2359304 | tf_op jit(solution)/shard_map/ppermute | solution.py:28
  31.4 2.1 %collective-permute-done.2.b3 = bf16[256,1536]{1,0:T(8,128)(2,1)S(1)} collective-permute-done((bf16[256,1536]{1,0:T(8,128)(2,1)}, bf16[256,1536]{1,0:T(8,128)(2,1)S(1)}, u32[]{:S(2)}, u32[]{:S(2)}) %collective-permute-start.2) | collective-permute-done | bytes 786464 | tf_op jit(solution)/shard_map/ppermute | solution.py:28
  33.6 4.4 %shard_map.103 = bf16[8,224,256]{2,1,0:T(8,128)(2,1)} custom-call(s32[92]{0:T(128)S(1)} %get-tuple-element.16.pairs, s32[46]{0:T(128)S(1)} %get-tuple-element.17.rows, bf16[256,1536]{1,0:T(8,128)(2,1)S(1)} %get-tuple-element.18.b0, bf16[256,1536]{1,0:T(8,128)(2,1)S(1)} %collective-permute-done.b1, bf16[256,1536]{1,0:T(8,128)(2,1)S(1)} %collective-permute-done.1.b2, ...), custom_call_target="tpu_custom_call" | custom-call | flops 671088640 | bytes 6291456 | tf_op jit(solution)/shard_map/pallas_call | solution.py:138
  38.0 16.7 %all_to_all.15.parts = bf16[8,224,256]{2,1,0:T(8,128)(2,1)S(1)} all-to-all(bf16[8,224,256]{2,1,0:T(8,128)(2,1)} %shard_map.103), channel_id=1, replica_groups=mesh['blk'=64,'help'=8] {'help'}, dimensions={0} | all-to-all | bytes 1835008 | tf_op jit(solution)/shard_map/all_to_all | solution.py:284
  55.3 15.3 %all_to_all.16.parts = bf16[8,256,256]{2,1,0:T(8,128)(2,1)S(1)} all-to-all(bf16[8,256,256]{2,1,0:T(8,128)(2,1)S(1)} %shard_map.104), channel_id=1, replica_groups=mesh['blk'=64,'help'=8] {'help'}, dimensions={0} | all-to-all | bytes 2097152 | tf_op jit(solution)/shard_map/all_to_all | solution.py:284
  70.6 2.3 %shard_map.105 = (bf16[1536,256]{1,0:T(8,128)(2,1)S(1)}, bf16[32,1536]{1,0:T(8,128)(2,1)}, f32[32,384]{1,0:T(8,128)S(1)}) custom-call(bf16[8,256,256]{2,1,0:T(8,128)(2,1)S(1)} %all_to_all.16.parts), custom_call_target="tpu_custom_call" | custom-call | tf_op jit(solution)/shard_map/pallas_call | solution.py:352
  72.9 9.6 %collective-permute-start.6 = (bf16[1536,256]{1,0:T(8,128)(2,1)S(1)}, bf16[1536,256]{1,0:T(8,128)(2,1)S(1)}, u32[]{:S(2)}, u32[]{:S(2)}) collective-permute-start(bf16[1536,256]{1,0:T(8,128)(2,1)S(1)} %get-tuple-element.24.b0), channel_id=1, source_target_pairs={{497,0},{496,1},{499,2},{498,3},{501,4},{500,5},{503,6},{502,7},{2... | collective-permute-start | bytes 2359304 | tf_op jit(solution)/shard_map/ppermute | solution.py:28
  82.5 1.9 %collective-permute-start.5 = (bf16[1536,256]{1,0:T(8,128)(2,1)S(1)}, bf16[1536,256]{1,0:T(8,128)(2,1)S(1)}, u32[]{:S(2)}, u32[]{:S(2)}) collective-permute-start(bf16[1536,256]{1,0:T(8,128)(2,1)S(1)} %get-tuple-element.24.b0), channel_id=1, source_target_pairs={{16,0},{17,1},{18,2},{19,3},{20,4},{21,5},{22,6},{23,7},{505,8},{5... | collective-permute-start | bytes 2359304 | tf_op jit(solution)/shard_map/ppermute | solution.py:28
  84.4 4.7 %collective-permute-start.9 = (f32[32,384]{1,0:T(8,128)S(1)}, f32[32,384]{1,0:T(8,128)S(1)}, u32[]{:S(2)}, u32[]{:S(2)}) collective-permute-start(f32[32,384]{1,0:T(8,128)S(1)} %get-tuple-element.25), channel_id=1, source_target_pairs={{264,0},{265,1},{266,2},{267,3},{268,4},{269,5},{270,6},{271,7},{2... | collective-permute-start | bytes 147464 | tf_op jit(solution)/shard_map/ppermute | solution.py:28
  89.1 5.2 %collective-permute-start.8 = (f32[32,384]{1,0:T(8,128)S(1)}, f32[32,384]{1,0:T(8,128)S(1)}, u32[]{:S(2)}, u32[]{:S(2)}) collective-permute-start(f32[32,384]{1,0:T(8,128)S(1)} %get-tuple-element.25), channel_id=1, source_target_pairs={{256,0},{257,1},{258,2},{259,3},{260,4},{261,5},{262,6},{263,7},{2... | collective-permute-start | bytes 147464 | tf_op jit(solution)/shard_map/ppermute | solution.py:28
  94.3 1.9 %collective-permute-start.7 = (f32[32,384]{1,0:T(8,128)S(1)}, f32[32,384]{1,0:T(8,128)S(1)}, u32[]{:S(2)}, u32[]{:S(2)}) collective-permute-start(f32[32,384]{1,0:T(8,128)S(1)} %get-tuple-element.25), channel_id=1, source_target_pairs={{8,0},{9,1},{10,2},{11,3},{12,4},{13,5},{14,6},{15,7},{0,8},{1,9},... | collective-permute-start | bytes 147464 | tf_op jit(solution)/shard_map/ppermute | solution.py:28
  96.2 2.4 %collective-permute-start.4 = (bf16[1536,256]{1,0:T(8,128)(2,1)S(1)}, bf16[1536,256]{1,0:T(8,128)(2,1)S(1)}, u32[]{:S(2)}, u32[]{:S(2)}) collective-permute-start(bf16[1536,256]{1,0:T(8,128)(2,1)S(1)} %get-tuple-element.24.b0), channel_id=1, source_target_pairs={{8,0},{9,1},{10,2},{11,3},{12,4},{13,5},{14,6},{15,7},{0,8},{1,9},... | collective-permute-start | bytes 2359304 | tf_op jit(solution)/shard_map/ppermute | solution.py:28
  98.7 6.8 %collective-permute-done.5.b2 = bf16[1536,256]{1,0:T(8,128)(2,1)S(1)} collective-permute-done((bf16[1536,256]{1,0:T(8,128)(2,1)S(1)}, bf16[1536,256]{1,0:T(8,128)(2,1)S(1)}, u32[]{:S(2)}, u32[]{:S(2)}) %collective-permute-start.5) | collective-permute-done | bytes 786464 | tf_op jit(solution)/shard_map/ppermute | solution.py:28
  107.4 1.9 %collective-permute-start.13 = (f32[32,384]{1,0:T(8,128)S(1)}, f32[32,384]{1,0:T(8,128)S(1)}, u32[]{:S(2)}, u32[]{:S(2)}) collective-permute-start(f32[32,384]{1,0:T(8,128)S(1)} %add_add_fusion.1), channel_id=1, source_target_pairs={{192,0},{193,1},{194,2},{195,3},{196,4},{197,5},{198,6},{199,7},{2... | collective-permute-start | bytes 147464 | tf_op jit(solution)/shard_map/ppermute | solution.py:28
  109.3 3.0 %collective-permute-start.12 = (f32[32,384]{1,0:T(8,128)S(1)}, f32[32,384]{1,0:T(8,128)S(1)}, u32[]{:S(2)}, u32[]{:S(2)}) collective-permute-start(f32[32,384]{1,0:T(8,128)S(1)} %add_add_fusion.1), channel_id=1, source_target_pairs={{128,0},{129,1},{130,2},{131,3},{132,4},{133,5},{134,6},{135,7},{1... | collective-permute-start | bytes 147464 | tf_op jit(solution)/shard_map/ppermute | solution.py:28
  112.3 11.3 %collective-permute-start.11 = (f32[32,384]{1,0:T(8,128)S(1)}, f32[32,384]{1,0:T(8,128)S(1)}, u32[]{:S(2)}, u32[]{:S(2)}) collective-permute-start(f32[32,384]{1,0:T(8,128)S(1)} %add_add_fusion.1), channel_id=1, source_target_pairs={{64,0},{65,1},{66,2},{67,3},{68,4},{69,5},{70,6},{71,7},{72,8},{73... | collective-permute-start | bytes 147464 | tf_op jit(solution)/shard_map/ppermute | solution.py:28
  123.6 4.1 %shard_map.106 = bf16[8,32,1536]{2,1,0:T(8,128)(2,1)} custom-call(s32[92]{0:T(128)S(1)} %get-tuple-element.16.pairs, s32[46]{0:T(128)S(1)} %get-tuple-element.17.rows, bf16[1536,256]{1,0:T(8,128)(2,1)S(1)} %get-tuple-element.24.b0, bf16[1536,256]{1,0:T(8,128)(2,1)S(1)} %collective-permute-done.4.b1, bf16[1536,256]{1,0:T(8,128)(2,1)S(1)} %collective-permute-done.5.b2, ...), custom_call_target="tpu_custom_call" | custom-call | flops 671088640 | bytes 6291456 | tf_op jit(solution)/shard_map/pallas_call | solution.py:138
  127.7 3.6 %all-to-all-start.2 = ((bf16[8,32,1536]{2,1,0:T(8,128)(2,1)}), bf16[8,32,1536]{2,1,0:T(8,128)(2,1)S(1)}, u32[]{:S(2)}, u32[]{:S(2)}) async-start(bf16[8,32,1536]{2,1,0:T(8,128)(2,1)} %shard_map.106), calls=%async_computation.2 | async-start | bytes 1572864 | tf_op jit(solution)/shard_map/all_to_all | solution.py:284
  131.4 1.9 %collective-permute-start.16 = (f32[32,384]{1,0:T(8,128)S(1)}, f32[32,384]{1,0:T(8,128)S(1)}, u32[]{:S(2)}, u32[]{:S(2)}) collective-permute-start(f32[32,384]{1,0:T(8,128)S(1)} %add_add_fusion), channel_id=1, source_target_pairs={{48,0},{49,1},{50,2},{51,3},{52,4},{53,5},{54,6},{55,7},{56,8},{57... | collective-permute-start | bytes 147464 | tf_op jit(solution)/shard_map/ppermute | solution.py:28
  135.2 5.4 %collective-permute-start.14 = (f32[32,384]{1,0:T(8,128)S(1)}, f32[32,384]{1,0:T(8,128)S(1)}, u32[]{:S(2)}, u32[]{:S(2)}) collective-permute-start(f32[32,384]{1,0:T(8,128)S(1)} %add_add_fusion), channel_id=1, source_target_pairs={{16,0},{17,1},{18,2},{19,3},{20,4},{21,5},{22,6},{23,7},{24,8},{25... | collective-permute-start | bytes 147464 | tf_op jit(solution)/shard_map/ppermute | solution.py:28
  (32 shorter events, 11.2 us)
Async XLA Ops:
  0.6 25.8 %collective-permute-start.1 = (bf16[256,1536]{1,0:T(8,128)(2,1)}, bf16[256,1536]{1,0:T(8,128)(2,1)S(1)}, u32[]{:S(2)}, u32[]{:S(2)}) collective-permute-start(bf16[256,1536]{1,0:T(8,128)(2,1)} %own.1), channel_id=1, source_target_pairs={{16,0},{17,1},{18,2},{19,3},{20,4},{21,5},{22,6},{23,7},{505,8},{5... | collective-permute-start | bytes 2359304 | tf_op jit(solution)/shard_map/ppermute | solution.py:28
  5.0 26.4 %collective-permute-start = (bf16[256,1536]{1,0:T(8,128)(2,1)}, bf16[256,1536]{1,0:T(8,128)(2,1)S(1)}, u32[]{:S(2)}, u32[]{:S(2)}) collective-permute-start(bf16[256,1536]{1,0:T(8,128)(2,1)} %own.1), channel_id=1, source_target_pairs={{8,0},{9,1},{10,2},{11,3},{12,4},{13,5},{14,6},{15,7},{0,8},{1,9},... | collective-permute-start | bytes 2359304 | tf_op jit(solution)/shard_map/ppermute | solution.py:28
  17.7 15.9 %collective-permute-start.2 = (bf16[256,1536]{1,0:T(8,128)(2,1)}, bf16[256,1536]{1,0:T(8,128)(2,1)S(1)}, u32[]{:S(2)}, u32[]{:S(2)}) collective-permute-start(bf16[256,1536]{1,0:T(8,128)(2,1)} %own.1), channel_id=1, source_target_pairs={{497,0},{496,1},{499,2},{498,3},{501,4},{500,5},{503,6},{502,7},{2... | collective-permute-start | bytes 2359304 | tf_op jit(solution)/shard_map/ppermute | solution.py:28
  21.1 0.9 copy-start
  22.0 0.7 copy-start.1
  22.6 0.7 copy-start.2
  26.4 7.2 %collective-permute-start.3 = (bf16[256,1536]{1,0:T(8,128)(2,1)S(1)}, bf16[256,1536]{1,0:T(8,128)(2,1)S(1)}, u32[]{:S(2)}, u32[]{:S(2)}) collective-permute-start(bf16[256,1536]{1,0:T(8,128)(2,1)S(1)} %collective-permute-done.1.b2), channel_id=1, source_target_pairs={{8,0},{9,1},{10,2},{11,3},{12,4},{13,5},{14,6},{15,7},{0,8},{1,9},... | collective-permute-start | bytes 2359304 | tf_op jit(solution)/shard_map/ppermute | solution.py:28
  72.9 25.8 %collective-permute-start.6 = (bf16[1536,256]{1,0:T(8,128)(2,1)S(1)}, bf16[1536,256]{1,0:T(8,128)(2,1)S(1)}, u32[]{:S(2)}, u32[]{:S(2)}) collective-permute-start(bf16[1536,256]{1,0:T(8,128)(2,1)S(1)} %get-tuple-element.24.b0), channel_id=1, source_target_pairs={{497,0},{496,1},{499,2},{498,3},{501,4},{500,5},{503,6},{502,7},{2... | collective-permute-start | bytes 2359304 | tf_op jit(solution)/shard_map/ppermute | solution.py:28
  82.5 23.0 %collective-permute-start.5 = (bf16[1536,256]{1,0:T(8,128)(2,1)S(1)}, bf16[1536,256]{1,0:T(8,128)(2,1)S(1)}, u32[]{:S(2)}, u32[]{:S(2)}) collective-permute-start(bf16[1536,256]{1,0:T(8,128)(2,1)S(1)} %get-tuple-element.24.b0), channel_id=1, source_target_pairs={{16,0},{17,1},{18,2},{19,3},{20,4},{21,5},{22,6},{23,7},{505,8},{5... | collective-permute-start | bytes 2359304 | tf_op jit(solution)/shard_map/ppermute | solution.py:28
  84.4 11.8 %collective-permute-start.9 = (f32[32,384]{1,0:T(8,128)S(1)}, f32[32,384]{1,0:T(8,128)S(1)}, u32[]{:S(2)}, u32[]{:S(2)}) collective-permute-start(f32[32,384]{1,0:T(8,128)S(1)} %get-tuple-element.25), channel_id=1, source_target_pairs={{264,0},{265,1},{266,2},{267,3},{268,4},{269,5},{270,6},{271,7},{2... | collective-permute-start | bytes 147464 | tf_op jit(solution)/shard_map/ppermute | solution.py:28
  89.1 9.5 %collective-permute-start.8 = (f32[32,384]{1,0:T(8,128)S(1)}, f32[32,384]{1,0:T(8,128)S(1)}, u32[]{:S(2)}, u32[]{:S(2)}) collective-permute-start(f32[32,384]{1,0:T(8,128)S(1)} %get-tuple-element.25), channel_id=1, source_target_pairs={{256,0},{257,1},{258,2},{259,3},{260,4},{261,5},{262,6},{263,7},{2... | collective-permute-start | bytes 147464 | tf_op jit(solution)/shard_map/ppermute | solution.py:28
  94.3 4.4 %collective-permute-start.7 = (f32[32,384]{1,0:T(8,128)S(1)}, f32[32,384]{1,0:T(8,128)S(1)}, u32[]{:S(2)}, u32[]{:S(2)}) collective-permute-start(f32[32,384]{1,0:T(8,128)S(1)} %get-tuple-element.25), channel_id=1, source_target_pairs={{8,0},{9,1},{10,2},{11,3},{12,4},{13,5},{14,6},{15,7},{0,8},{1,9},... | collective-permute-start | bytes 147464 | tf_op jit(solution)/shard_map/ppermute | solution.py:28
  96.2 27.4 %collective-permute-start.4 = (bf16[1536,256]{1,0:T(8,128)(2,1)S(1)}, bf16[1536,256]{1,0:T(8,128)(2,1)S(1)}, u32[]{:S(2)}, u32[]{:S(2)}) collective-permute-start(bf16[1536,256]{1,0:T(8,128)(2,1)S(1)} %get-tuple-element.24.b0), channel_id=1, source_target_pairs={{8,0},{9,1},{10,2},{11,3},{12,4},{13,5},{14,6},{15,7},{0,8},{1,9},... | collective-permute-start | bytes 2359304 | tf_op jit(solution)/shard_map/ppermute | solution.py:28
  105.5 18.1 %collective-permute-start.10 = (bf16[1536,256]{1,0:T(8,128)(2,1)S(1)}, bf16[1536,256]{1,0:T(8,128)(2,1)S(1)}, u32[]{:S(2)}, u32[]{:S(2)}) collective-permute-start(bf16[1536,256]{1,0:T(8,128)(2,1)S(1)} %collective-permute-done.5.b2), channel_id=1, source_target_pairs={{8,0},{9,1},{10,2},{11,3},{12,4},{13,5},{14,6},{15,7},{0,8},{1,9},... | collective-permute-start | bytes 2359304 | tf_op jit(solution)/shard_map/ppermute | solution.py:28
  107.4 23.9 %collective-permute-start.13 = (f32[32,384]{1,0:T(8,128)S(1)}, f32[32,384]{1,0:T(8,128)S(1)}, u32[]{:S(2)}, u32[]{:S(2)}) collective-permute-start(f32[32,384]{1,0:T(8,128)S(1)} %add_add_fusion.1), channel_id=1, source_target_pairs={{192,0},{193,1},{194,2},{195,3},{196,4},{197,5},{198,6},{199,7},{2... | collective-permute-start | bytes 147464 | tf_op jit(solution)/shard_map/ppermute | solution.py:28
  109.3 22.0 %collective-permute-start.12 = (f32[32,384]{1,0:T(8,128)S(1)}, f32[32,384]{1,0:T(8,128)S(1)}, u32[]{:S(2)}, u32[]{:S(2)}) collective-permute-start(f32[32,384]{1,0:T(8,128)S(1)} %add_add_fusion.1), channel_id=1, source_target_pairs={{128,0},{129,1},{130,2},{131,3},{132,4},{133,5},{134,6},{135,7},{1... | collective-permute-start | bytes 147464 | tf_op jit(solution)/shard_map/ppermute | solution.py:28
  112.3 19.0 %collective-permute-start.11 = (f32[32,384]{1,0:T(8,128)S(1)}, f32[32,384]{1,0:T(8,128)S(1)}, u32[]{:S(2)}, u32[]{:S(2)}) collective-permute-start(f32[32,384]{1,0:T(8,128)S(1)} %add_add_fusion.1), channel_id=1, source_target_pairs={{64,0},{65,1},{66,2},{67,3},{68,4},{69,5},{70,6},{71,7},{72,8},{73... | collective-permute-start | bytes 147464 | tf_op jit(solution)/shard_map/ppermute | solution.py:28
  127.7 15.9 %all-to-all-start.2 = ((bf16[8,32,1536]{2,1,0:T(8,128)(2,1)}), bf16[8,32,1536]{2,1,0:T(8,128)(2,1)S(1)}, u32[]{:S(2)}, u32[]{:S(2)}) async-start(bf16[8,32,1536]{2,1,0:T(8,128)(2,1)} %shard_map.106), calls=%async_computation.2 | async-start | bytes 1572864 | tf_op jit(solution)/shard_map/all_to_all | solution.py:284
  131.4 9.3 %collective-permute-start.16 = (f32[32,384]{1,0:T(8,128)S(1)}, f32[32,384]{1,0:T(8,128)S(1)}, u32[]{:S(2)}, u32[]{:S(2)}) collective-permute-start(f32[32,384]{1,0:T(8,128)S(1)} %add_add_fusion), channel_id=1, source_target_pairs={{48,0},{49,1},{50,2},{51,3},{52,4},{53,5},{54,6},{55,7},{56,8},{57... | collective-permute-start | bytes 147464 | tf_op jit(solution)/shard_map/ppermute | solution.py:28
  133.3 7.4 %collective-permute-start.15 = (f32[32,384]{1,0:T(8,128)S(1)}, f32[32,384]{1,0:T(8,128)S(1)}, u32[]{:S(2)}, u32[]{:S(2)}) collective-permute-start(f32[32,384]{1,0:T(8,128)S(1)} %add_add_fusion), channel_id=1, source_target_pairs={{32,0},{33,1},{34,2},{35,3},{36,4},{37,5},{38,6},{39,7},{40,8},{41... | collective-permute-start | bytes 147464 | tf_op jit(solution)/shard_map/ppermute | solution.py:28
  135.2 7.2 %collective-permute-start.14 = (f32[32,384]{1,0:T(8,128)S(1)}, f32[32,384]{1,0:T(8,128)S(1)}, u32[]{:S(2)}, u32[]{:S(2)}) collective-permute-start(f32[32,384]{1,0:T(8,128)S(1)} %add_add_fusion), channel_id=1, source_target_pairs={{16,0},{17,1},{18,2},{19,3},{20,4},{21,5},{22,6},{23,7},{24,8},{25... | collective-permute-start | bytes 147464 | tf_op jit(solution)/shard_map/ppermute | solution.py:28

commit v5 on v4

--- a/solution.py
+++ b/solution.py
@@ -252,10 +252,10 @@
         out[h, mine + share :, mine:] = sums[own]
 
 
-def divide_kernel(parts, back, out, total, side, sems):
+def divide_kernel(parts, back, out, total, side, sums_v, sems):
     helps, _, width = parts.shape
     mine = back.shape[0] // helps
-    share = total.shape[0]
+    share = total.shape[1]
     copies = []
     for s in range(helps):
         copies.append(pltpu.make_async_copy(parts.at[s, mine:], side.at[s], sems.at[s]))
@@ -271,12 +271,17 @@
     sums = side[0].astype(jnp.float32)
     for s in range(1, helps):
         sums = sums + side[s].astype(jnp.float32)
-    total[:, :width] = sums[:share]
     both = sums[share:, mine : mine + 1] + sums[share:, mine + 1 : mine + 2]
-    total[:, width:] = jnp.broadcast_to(both, (share, total.shape[1] - width))
+    both = jnp.broadcast_to(both, (share, total.shape[2] - width))
+    sums_v[:, :width] = sums[:share]
+    sums_v[:, width:] = both
+    copies = copies[1::2]
+    for s in range(total.shape[0]):
+        copies.append(pltpu.make_async_copy(sums_v, total.at[s], sems.at[2 * helps + s]))
+        copies[helps + s].start()
     for s in range(helps):
         out[:, s * mine : (s + 1) * mine] = side[s, share:, :mine]
-    for copy in copies[1::2]:
+    for copy in copies:
         copy.wait()
 
 
@@ -289,6 +294,11 @@
         move(total, functools.partial(lambda s, b, h: (b ^ s, h), s)) for s in (one, two, one ^ two)
     ]
     return (total + got[0]) + (got[1] + got[2])
+
+
+def fours(blks, one, two):
+    bases = [b for b in range(blks) if b & (one | two) == 0]
+    return [[b, b | one, b | two, b | one | two] for b in bases]
 
 
 def per_device(features_t, weight, bias, cotangent_t, tile_vals, slot_row, slot_col):
@@ -354,25 +364,27 @@
         out_shape=(
             pltpu.VMEM((nodes, width), jnp.bfloat16),
             jax.ShapeDtypeStruct((share, nodes), jnp.bfloat16),
-            jax.ShapeDtypeStruct((share, width + tile), jnp.float32),
+            pltpu.HBM((4, share, width + tile), jnp.float32),
         ),
         in_specs=[ANY],
-        out_specs=(ANY, VMEM, VMEM),
+        out_specs=(ANY, VMEM, ANY),
         scratch_shapes=[
             pltpu.VMEM((helps, 2 * share, width), jnp.bfloat16),
-            pltpu.SemaphoreType.DMA((2 * helps,)),
+            pltpu.VMEM((share, width + tile), jnp.float32),
+            pltpu.SemaphoreType.DMA((2 * helps + 4,)),
         ],
         compiler_params=pltpu.CompilerParams(vmem_limit_bytes=4 * 2**20),
     )(spread(sent))
     zero, one, two = near(back)
     half = blks // 2
-    total = after(round_of_four(total, 1, half), two)
-    three = move(after(one, total), swap)
-    total = round_of_four(total, 8, 16)
+    far = lax.all_to_all(total, "blk", 0, 0, axis_index_groups=fours(blks, 8, 16))
+    total = jnp.sum(far, axis=0)
+    three = move(after(one, (total, two)), swap)
     value = aggregate(
         backward_kernel, (back, zero, one, two, three), tiles, slots, (helps, share, nodes)
     )
     propagated = jnp.sum(spread(value).astype(jnp.float32), axis=0)
+    total = round_of_four(total, 1, half)
     total = round_of_four(total, 2, 4)
     total = total * (1.0 / math.sqrt(nodes * blks))
     return (output, propagated, total[:, :width].T, total[:, width])

time: 147 us -> 149 us (1.014)
  starting transfers between devices: 81.2 us -> 70.8 us
  waiting for transfers between devices: 10.7 us -> 19.7 us
  Pallas kernels: 14.5 us -> 17.5 us
  other arithmetic: 0.83 us -> 2.58 us
    ppermute x17 -> x14, starting transfers between devices: 77.7 us -> 63.3 us  [move(): return lax.ppermute(block, AXES, route)]
    all_to_all x0 -> x1, waiting for transfers between devices: none -> 12.5 us  [per_device(): lax.all_to_all(total, 'blk', 0, 0, axis_index_groups=fours(blks, 8, 16))]
    all_to_all x0 -> x1, starting transfers between devices: none -> 4.01 us  [per_device(): lax.all_to_all(total, 'blk', 0, 0, axis_index_groups=fours(blks, 8, 16))]
    ppermute x17 -> x14, waiting for transfers between devices: 10.7 us -> 7.13 us  [move(): return lax.ppermute(block, AXES, route)]
    pallas_call x2, Pallas kernels: 8.47 us -> 10.8 us  [aggregate(): pl.pallas_call(kernel, out_shape=pltpu.HBM(out_shape, jnp.bfloat16), in_s...]
  transfers between devices with their start and end apart: 18 -> 16, of which waited for: 3 -> 5; matrix products, arithmetic and copies ran while one was open for 1% -> 3% of each run, Pallas kernels for 5% -> 6%
where the time goes in v5:
time: 149 us; the launch traced here: 148 us
  starting transfers between devices  70.8 us (48%)
  blocking collectives  32 us (21%)
  waiting for transfers between devices  19.7 us (13%)
  Pallas kernels  17.5 us (12%)
  local copies, waits for them, and re-layouts  4.19 us (3%)
  other arithmetic  2.58 us (2%)
    ppermute x14, starting transfers between devices, move(): return lax.ppermute(block, AXES, route)  63.3 us
    all_to_all x2, blocking collectives, spread(): return lax.all_to_all(x, 'help', 0, 0)  32 us
    all_to_all x1, waiting for transfers between devices, per_device(): lax.all_to_all(total, 'blk', 0, 0, axis_index_groups=fours(blks, 8, 16))  12.5 us
    pallas_call x2, Pallas kernels, aggregate(): pl.pallas_call(kernel, out_shape=pltpu.HBM(out_shape, jnp.bfloat16), in_s...  10.8 us
    ppermute x14, waiting for transfers between devices, move(): return lax.ppermute(block, AXES, route)  7.13 us
    all_to_all x1, starting transfers between devices, per_device(): lax.all_to_all(total, 'blk', 0, 0, axis_index_groups=fours(blks, 8, 16))  4.01 us
    all_to_all x1, starting transfers between devices, spread(): return lax.all_to_all(x, 'help', 0, 0)  3.56 us
    pallas_call x1, Pallas kernels, per_device(): pl.pallas_call(functools.partial(prepare_kernel, row_tiles), out_shape=(j...  3.13 us
  transfers between devices with their start and end apart: 16, of which 5 were waited for; matrix products, arithmetic and copies ran while one was open for 3% of the time, Pallas kernels for 6%

profile of v5, /device:TPU:1, one launch (start us, length us, event | category | flops | bytes accessed | tf_op | source)
XLA Modules:
  0.0 147.7 jit_solution(3341975698687391240)
XLA Ops:
  0.6 4.4 %collective-permute-start.1 = (bf16[256,1536]{1,0:T(8,128)(2,1)}, bf16[256,1536]{1,0:T(8,128)(2,1)S(1)}, u32[]{:S(2)}, u32[]{:S(2)}) collective-permute-start(bf16[256,1536]{1,0:T(8,128)(2,1)} %own.1), channel_id=1, source_target_pairs={{16,0},{17,1},{18,2},{19,3},{20,4},{21,5},{22,6},{23,7},{505,8},{5... | collective-permute-start | bytes 2359304 | tf_op jit(solution)/shard_map/ppermute | solution.py:28
  5.0 12.6 %collective-permute-start = (bf16[256,1536]{1,0:T(8,128)(2,1)}, bf16[256,1536]{1,0:T(8,128)(2,1)}, u32[]{:S(2)}, u32[]{:S(2)}) collective-permute-start(bf16[256,1536]{1,0:T(8,128)(2,1)} %own.1), channel_id=1, source_target_pairs={{8,0},{9,1},{10,2},{11,3},{12,4},{13,5},{14,6},{15,7},{0,8},{1,9},... | collective-permute-start | bytes 2359304 | tf_op jit(solution)/shard_map/ppermute | solution.py:28
  17.7 2.6 %collective-permute-start.2 = (bf16[256,1536]{1,0:T(8,128)(2,1)}, bf16[256,1536]{1,0:T(8,128)(2,1)}, u32[]{:S(2)}, u32[]{:S(2)}) collective-permute-start(bf16[256,1536]{1,0:T(8,128)(2,1)} %own.1), channel_id=1, source_target_pairs={{497,0},{496,1},{499,2},{498,3},{501,4},{500,5},{503,6},{502,7},{2... | collective-permute-start | bytes 2359304 | tf_op jit(solution)/shard_map/ppermute | solution.py:28
  23.3 3.1 %shard_map.102 = (s32[92]{0:T(128)S(1)}, s32[46]{0:T(128)S(1)}, bf16[8,32,256]{2,1,0:T(8,128)(2,1)S(1)}, bf16[256,256]{1,0:T(8,128)(2,1)S(1)}, bf16[80,128,128]{...) custom-call(s32[1]{0:T(128)} %bitcast.odd, s32[80]{0:T(128)S(1)} %bitcast.7, s32[80]{0:T(128)S(1)} %bitcast.8, ...), custom_call_target="tpu_custom_call" | custom-call | tf_op jit(solution)/shard_map/pallas_call | solution.py:318
  26.4 5.0 %collective-permute-start.3 = (bf16[256,1536]{1,0:T(8,128)(2,1)S(1)}, bf16[256,1536]{1,0:T(8,128)(2,1)S(1)}, u32[]{:S(2)}, u32[]{:S(2)}) collective-permute-start(bf16[256,1536]{1,0:T(8,128)(2,1)S(1)} %collective-permute-done.1.b2), channel_id=1, source_target_pairs={{8,0},{9,1},{10,2},{11,3},{12,4},{13,5},{14,6},{15,7},{0,8},{1,9},... | collective-permute-start | bytes 2359304 | tf_op jit(solution)/shard_map/ppermute | solution.py:28
  31.4 2.1 %collective-permute-done.2.b3 = bf16[256,1536]{1,0:T(8,128)(2,1)} collective-permute-done((bf16[256,1536]{1,0:T(8,128)(2,1)}, bf16[256,1536]{1,0:T(8,128)(2,1)}, u32[]{:S(2)}, u32[]{:S(2)}) %collective-permute-start.2) | collective-permute-done | bytes 786464 | tf_op jit(solution)/shard_map/ppermute | solution.py:28
  33.6 5.5 %shard_map.103 = bf16[8,224,256]{2,1,0:T(8,128)(2,1)} custom-call(s32[92]{0:T(128)S(1)} %get-tuple-element.15.pairs, s32[46]{0:T(128)S(1)} %get-tuple-element.16.rows, bf16[256,1536]{1,0:T(8,128)(2,1)S(1)} %get-tuple-element.17.b0, bf16[256,1536]{1,0:T(8,128)(2,1)} %collective-permute-done.b1, bf16[256,1536]{1,0:T(8,128)(2,1)S(1)} %collective-permute-done.1.b2, ...), custom_call_target="tpu_custom_call" | custom-call | flops 671088640 | bytes 6291456 | tf_op jit(solution)/shard_map/pallas_call | solution.py:138
  39.1 16.6 %all_to_all.20.parts = bf16[8,224,256]{2,1,0:T(8,128)(2,1)S(1)} all-to-all(bf16[8,224,256]{2,1,0:T(8,128)(2,1)} %shard_map.103), channel_id=1, replica_groups=mesh['blk'=64,'help'=8] {'help'}, dimensions={0} | all-to-all | bytes 1835008 | tf_op jit(solution)/shard_map/all_to_all | solution.py:289
  56.3 15.4 %all_to_all.21.parts = bf16[8,256,256]{2,1,0:T(8,128)(2,1)S(1)} all-to-all(bf16[8,256,256]{2,1,0:T(8,128)(2,1)S(1)} %shard_map.104), channel_id=1, replica_groups=mesh['blk'=64,'help'=8] {'help'}, dimensions={0} | all-to-all | bytes 2097152 | tf_op jit(solution)/shard_map/all_to_all | solution.py:289
  71.6 3.0 %shard_map.105 = (bf16[1536,256]{1,0:T(8,128)(2,1)S(1)}, bf16[32,1536]{1,0:T(8,128)(2,1)}, f32[4,32,384]{2,1,0:T(8,128)}) custom-call(bf16[8,256,256]{2,1,0:T(8,128)(2,1)S(1)} %all_to_all.21.parts), custom_call_target="tpu_custom_call" | custom-call | tf_op jit(solution)/shard_map/pallas_call | solution.py:362
  74.6 10.1 %collective-permute-start.6 = (bf16[1536,256]{1,0:T(8,128)(2,1)S(1)}, bf16[1536,256]{1,0:T(8,128)(2,1)}, u32[]{:S(2)}, u32[]{:S(2)}) collective-permute-start(bf16[1536,256]{1,0:T(8,128)(2,1)S(1)} %get-tuple-element.23.b0), channel_id=1, source_target_pairs={{497,0},{496,1},{499,2},{498,3},{501,4},{500,5},{503,6},{502,7},{2... | collective-permute-start | bytes 2359304 | tf_op jit(solution)/shard_map/ppermute | solution.py:28
  86.6 4.0 %all-to-all-start.2 = ((f32[4,32,384]{2,1,0:T(8,128)}), f32[4,32,384]{2,1,0:T(8,128)}, u32[]{:S(2)}, u32[]{:S(2)}) async-start(f32[4,32,384]{2,1,0:T(8,128)} %get-tuple-element.24), calls=%async_computation.2 | async-start | bytes 393216 | tf_op jit(solution)/shard_map/all_to_all | solution.py:380
  90.6 5.3 %collective-permute-start.4 = (bf16[1536,256]{1,0:T(8,128)(2,1)S(1)}, bf16[1536,256]{1,0:T(8,128)(2,1)}, u32[]{:S(2)}, u32[]{:S(2)}) collective-permute-start(bf16[1536,256]{1,0:T(8,128)(2,1)S(1)} %get-tuple-element.23.b0), channel_id=1, source_target_pairs={{8,0},{9,1},{10,2},{11,3},{12,4},{13,5},{14,6},{15,7},{0,8},{1,9},... | collective-permute-start | bytes 2359304 | tf_op jit(solution)/shard_map/ppermute | solution.py:28
  95.9 12.5 %all-to-all-done.2 = f32[4,32,384]{2,1,0:T(8,128)} async-done(((f32[4,32,384]{2,1,0:T(8,128)}), f32[4,32,384]{2,1,0:T(8,128)}, u32[]{:S(2)}, u32[]{:S(2)}) %all-to-all-start.2) | async-done | bytes 196640 | tf_op jit(solution)/shard_map/all_to_all | solution.py:380
  111.5 2.4 %collective-permute-start.7 = (bf16[1536,256]{1,0:T(8,128)(2,1)}, bf16[1536,256]{1,0:T(8,128)(2,1)S(1)}, u32[]{:S(2)}, u32[]{:S(2)}) collective-permute-start(bf16[1536,256]{1,0:T(8,128)(2,1)} %collective-permute-done.5.b2), channel_id=1, source_target_pairs={{8,0},{9,1},{10,2},{11,3},{12,4},{13,5},{14,6},{15,7},{0,8},{1,9},... | collective-permute-start | bytes 2359304 | tf_op jit(solution)/shard_map/ppermute | solution.py:28
  113.8 2.3 %collective-permute-start.10 = (f32[32,384]{1,0:T(8,128)S(1)}, f32[32,384]{1,0:T(8,128)S(1)}, u32[]{:S(2)}, u32[]{:S(2)}) collective-permute-start(f32[32,384]{1,0:T(8,128)S(1)} %reduce_sum.18), channel_id=1, source_target_pairs={{264,0},{265,1},{266,2},{267,3},{268,4},{269,5},{270,6},{271,7},{2... | collective-permute-start | bytes 147464 | tf_op jit(solution)/shard_map/ppermute | solution.py:28
  116.2 4.4 %collective-permute-start.9 = (f32[32,384]{1,0:T(8,128)S(1)}, f32[32,384]{1,0:T(8,128)}, u32[]{:S(2)}, u32[]{:S(2)}) collective-permute-start(f32[32,384]{1,0:T(8,128)S(1)} %reduce_sum.18), channel_id=1, source_target_pairs={{256,0},{257,1},{258,2},{259,3},{260,4},{261,5},{262,6},{263,7},{2... | collective-permute-start | bytes 147464 | tf_op jit(solution)/shard_map/ppermute | solution.py:28
  120.6 2.7 %collective-permute-start.8 = (f32[32,384]{1,0:T(8,128)S(1)}, f32[32,384]{1,0:T(8,128)}, u32[]{:S(2)}, u32[]{:S(2)}) collective-permute-start(f32[32,384]{1,0:T(8,128)S(1)} %reduce_sum.18), channel_id=1, source_target_pairs={{8,0},{9,1},{10,2},{11,3},{12,4},{13,5},{14,6},{15,7},{0,8},{1,9},... | collective-permute-start | bytes 147464 | tf_op jit(solution)/shard_map/ppermute | solution.py:28
  123.3 5.4 %shard_map.106 = bf16[8,32,1536]{2,1,0:T(8,128)(2,1)} custom-call(s32[92]{0:T(128)S(1)} %get-tuple-element.15.pairs, s32[46]{0:T(128)S(1)} %get-tuple-element.16.rows, bf16[1536,256]{1,0:T(8,128)(2,1)S(1)} %get-tuple-element.23.b0, bf16[1536,256]{1,0:T(8,128)(2,1)} %collective-permute-done.4.b1, bf16[1536,256]{1,0:T(8,128)(2,1)} %collective-permute-done.5.b2, ...), custom_call_target="tpu_custom_call" | custom-call | flops 671088640 | bytes 6291456 | tf_op jit(solution)/shard_map/pallas_call | solution.py:138
  128.6 3.6 %all-to-all-start.3 = ((bf16[8,32,1536]{2,1,0:T(8,128)(2,1)}), bf16[8,32,1536]{2,1,0:T(8,128)(2,1)S(1)}, u32[]{:S(2)}, u32[]{:S(2)}) async-start(bf16[8,32,1536]{2,1,0:T(8,128)(2,1)} %shard_map.106), calls=%async_computation.3 | async-start | bytes 1572864 | tf_op jit(solution)/shard_map/all_to_all | solution.py:289
  133.1 4.1 %collective-permute-start.13 = (f32[32,384]{1,0:T(8,128)S(1)}, f32[32,384]{1,0:T(8,128)S(1)}, u32[]{:S(2)}, u32[]{:S(2)}) collective-permute-start(f32[32,384]{1,0:T(8,128)S(1)} %add_add_fusion), channel_id=1, source_target_pairs={{48,0},{49,1},{50,2},{51,3},{52,4},{53,5},{54,6},{55,7},{56,8},{57... | collective-permute-start | bytes 147464 | tf_op jit(solution)/shard_map/ppermute | solution.py:28
  137.1 3.3 %collective-permute-start.12 = (f32[32,384]{1,0:T(8,128)S(1)}, f32[32,384]{1,0:T(8,128)S(1)}, u32[]{:S(2)}, u32[]{:S(2)}) collective-permute-start(f32[32,384]{1,0:T(8,128)S(1)} %add_add_fusion), channel_id=1, source_target_pairs={{32,0},{33,1},{34,2},{35,3},{36,4},{37,5},{38,6},{39,7},{40,8},{41... | collective-permute-start | bytes 147464 | tf_op jit(solution)/shard_map/ppermute | solution.py:28
  140.5 2.2 %collective-permute-start.11 = (f32[32,384]{1,0:T(8,128)S(1)}, f32[32,384]{1,0:T(8,128)S(1)}, u32[]{:S(2)}, u32[]{:S(2)}) collective-permute-start(f32[32,384]{1,0:T(8,128)S(1)} %add_add_fusion), channel_id=1, source_target_pairs={{16,0},{17,1},{18,2},{19,3},{20,4},{21,5},{22,6},{23,7},{24,8},{25... | collective-permute-start | bytes 147464 | tf_op jit(solution)/shard_map/ppermute | solution.py:28
  142.9 2.8 %collective-permute-done.11 = f32[32,384]{1,0:T(8,128)S(1)} collective-permute-done((f32[32,384]{1,0:T(8,128)S(1)}, f32[32,384]{1,0:T(8,128)S(1)}, u32[]{:S(2)}, u32[]{:S(2)}) %collective-permute-start.11) | collective-permute-done | bytes 49184 | tf_op jit(solution)/shard_map/ppermute | solution.py:28
  (28 shorter events, 11.5 us)
Async XLA Ops:
  0.6 25.8 %collective-permute-start.1 = (bf16[256,1536]{1,0:T(8,128)(2,1)}, bf16[256,1536]{1,0:T(8,128)(2,1)S(1)}, u32[]{:S(2)}, u32[]{:S(2)}) collective-permute-start(bf16[256,1536]{1,0:T(8,128)(2,1)} %own.1), channel_id=1, source_target_pairs={{16,0},{17,1},{18,2},{19,3},{20,4},{21,5},{22,6},{23,7},{505,8},{5... | collective-permute-start | bytes 2359304 | tf_op jit(solution)/shard_map/ppermute | solution.py:28
  5.0 26.4 %collective-permute-start = (bf16[256,1536]{1,0:T(8,128)(2,1)}, bf16[256,1536]{1,0:T(8,128)(2,1)}, u32[]{:S(2)}, u32[]{:S(2)}) collective-permute-start(bf16[256,1536]{1,0:T(8,128)(2,1)} %own.1), channel_id=1, source_target_pairs={{8,0},{9,1},{10,2},{11,3},{12,4},{13,5},{14,6},{15,7},{0,8},{1,9},... | collective-permute-start | bytes 2359304 | tf_op jit(solution)/shard_map/ppermute | solution.py:28
  17.7 15.9 %collective-permute-start.2 = (bf16[256,1536]{1,0:T(8,128)(2,1)}, bf16[256,1536]{1,0:T(8,128)(2,1)}, u32[]{:S(2)}, u32[]{:S(2)}) collective-permute-start(bf16[256,1536]{1,0:T(8,128)(2,1)} %own.1), channel_id=1, source_target_pairs={{497,0},{496,1},{499,2},{498,3},{501,4},{500,5},{503,6},{502,7},{2... | collective-permute-start | bytes 2359304 | tf_op jit(solution)/shard_map/ppermute | solution.py:28
  21.1 0.9 copy-start
  22.0 0.7 copy-start.1
  22.6 0.7 copy-start.2
  26.4 7.2 %collective-permute-start.3 = (bf16[256,1536]{1,0:T(8,128)(2,1)S(1)}, bf16[256,1536]{1,0:T(8,128)(2,1)S(1)}, u32[]{:S(2)}, u32[]{:S(2)}) collective-permute-start(bf16[256,1536]{1,0:T(8,128)(2,1)S(1)} %collective-permute-done.1.b2), channel_id=1, source_target_pairs={{8,0},{9,1},{10,2},{11,3},{12,4},{13,5},{14,6},{15,7},{0,8},{1,9},... | collective-permute-start | bytes 2359304 | tf_op jit(solution)/shard_map/ppermute | solution.py:28
  74.6 34.8 %collective-permute-start.6 = (bf16[1536,256]{1,0:T(8,128)(2,1)S(1)}, bf16[1536,256]{1,0:T(8,128)(2,1)}, u32[]{:S(2)}, u32[]{:S(2)}) collective-permute-start(bf16[1536,256]{1,0:T(8,128)(2,1)S(1)} %get-tuple-element.23.b0), channel_id=1, source_target_pairs={{497,0},{496,1},{499,2},{498,3},{501,4},{500,5},{503,6},{502,7},{2... | collective-permute-start | bytes 2359304 | tf_op jit(solution)/shard_map/ppermute | solution.py:28
  84.7 26.8 %collective-permute-start.5 = (bf16[1536,256]{1,0:T(8,128)(2,1)S(1)}, bf16[1536,256]{1,0:T(8,128)(2,1)}, u32[]{:S(2)}, u32[]{:S(2)}) collective-permute-start(bf16[1536,256]{1,0:T(8,128)(2,1)S(1)} %get-tuple-element.23.b0), channel_id=1, source_target_pairs={{16,0},{17,1},{18,2},{19,3},{20,4},{21,5},{22,6},{23,7},{505,8},{5... | collective-permute-start | bytes 2359304 | tf_op jit(solution)/shard_map/ppermute | solution.py:28
  86.6 21.9 %all-to-all-start.2 = ((f32[4,32,384]{2,1,0:T(8,128)}), f32[4,32,384]{2,1,0:T(8,128)}, u32[]{:S(2)}, u32[]{:S(2)}) async-start(f32[4,32,384]{2,1,0:T(8,128)} %get-tuple-element.24), calls=%async_computation.2 | async-start | bytes 393216 | tf_op jit(solution)/shard_map/all_to_all | solution.py:380
  90.6 32.6 %collective-permute-start.4 = (bf16[1536,256]{1,0:T(8,128)(2,1)S(1)}, bf16[1536,256]{1,0:T(8,128)(2,1)}, u32[]{:S(2)}, u32[]{:S(2)}) collective-permute-start(bf16[1536,256]{1,0:T(8,128)(2,1)S(1)} %get-tuple-element.23.b0), channel_id=1, source_target_pairs={{8,0},{9,1},{10,2},{11,3},{12,4},{13,5},{14,6},{15,7},{0,8},{1,9},... | collective-permute-start | bytes 2359304 | tf_op jit(solution)/shard_map/ppermute | solution.py:28
  111.5 11.8 %collective-permute-start.7 = (bf16[1536,256]{1,0:T(8,128)(2,1)}, bf16[1536,256]{1,0:T(8,128)(2,1)S(1)}, u32[]{:S(2)}, u32[]{:S(2)}) collective-permute-start(bf16[1536,256]{1,0:T(8,128)(2,1)} %collective-permute-done.5.b2), channel_id=1, source_target_pairs={{8,0},{9,1},{10,2},{11,3},{12,4},{13,5},{14,6},{15,7},{0,8},{1,9},... | collective-permute-start | bytes 2359304 | tf_op jit(solution)/shard_map/ppermute | solution.py:28
  113.8 18.4 %collective-permute-start.10 = (f32[32,384]{1,0:T(8,128)S(1)}, f32[32,384]{1,0:T(8,128)S(1)}, u32[]{:S(2)}, u32[]{:S(2)}) collective-permute-start(f32[32,384]{1,0:T(8,128)S(1)} %reduce_sum.18), channel_id=1, source_target_pairs={{264,0},{265,1},{266,2},{267,3},{268,4},{269,5},{270,6},{271,7},{2... | collective-permute-start | bytes 147464 | tf_op jit(solution)/shard_map/ppermute | solution.py:28
  116.2 16.0 %collective-permute-start.9 = (f32[32,384]{1,0:T(8,128)S(1)}, f32[32,384]{1,0:T(8,128)}, u32[]{:S(2)}, u32[]{:S(2)}) collective-permute-start(f32[32,384]{1,0:T(8,128)S(1)} %reduce_sum.18), channel_id=1, source_target_pairs={{256,0},{257,1},{258,2},{259,3},{260,4},{261,5},{262,6},{263,7},{2... | collective-permute-start | bytes 147464 | tf_op jit(solution)/shard_map/ppermute | solution.py:28
  120.6 11.6 %collective-permute-start.8 = (f32[32,384]{1,0:T(8,128)S(1)}, f32[32,384]{1,0:T(8,128)}, u32[]{:S(2)}, u32[]{:S(2)}) collective-permute-start(f32[32,384]{1,0:T(8,128)S(1)} %reduce_sum.18), channel_id=1, source_target_pairs={{8,0},{9,1},{10,2},{11,3},{12,4},{13,5},{14,6},{15,7},{0,8},{1,9},... | collective-permute-start | bytes 147464 | tf_op jit(solution)/shard_map/ppermute | solution.py:28
  128.6 18.3 %all-to-all-start.3 = ((bf16[8,32,1536]{2,1,0:T(8,128)(2,1)}), bf16[8,32,1536]{2,1,0:T(8,128)(2,1)S(1)}, u32[]{:S(2)}, u32[]{:S(2)}) async-start(bf16[8,32,1536]{2,1,0:T(8,128)(2,1)} %shard_map.106), calls=%async_computation.3 | async-start | bytes 1572864 | tf_op jit(solution)/shard_map/all_to_all | solution.py:289
  133.1 9.6 %collective-permute-start.13 = (f32[32,384]{1,0:T(8,128)S(1)}, f32[32,384]{1,0:T(8,128)S(1)}, u32[]{:S(2)}, u32[]{:S(2)}) collective-permute-start(f32[32,384]{1,0:T(8,128)S(1)} %add_add_fusion), channel_id=1, source_target_pairs={{48,0},{49,1},{50,2},{51,3},{52,4},{53,5},{54,6},{55,7},{56,8},{57... | collective-permute-start | bytes 147464 | tf_op jit(solution)/shard_map/ppermute | solution.py:28
  137.1 5.7 %collective-permute-start.12 = (f32[32,384]{1,0:T(8,128)S(1)}, f32[32,384]{1,0:T(8,128)S(1)}, u32[]{:S(2)}, u32[]{:S(2)}) collective-permute-start(f32[32,384]{1,0:T(8,128)S(1)} %add_add_fusion), channel_id=1, source_target_pairs={{32,0},{33,1},{34,2},{35,3},{36,4},{37,5},{38,6},{39,7},{40,8},{41... | collective-permute-start | bytes 147464 | tf_op jit(solution)/shard_map/ppermute | solution.py:28
  140.5 5.1 %collective-permute-start.11 = (f32[32,384]{1,0:T(8,128)S(1)}, f32[32,384]{1,0:T(8,128)S(1)}, u32[]{:S(2)}, u32[]{:S(2)}) collective-permute-start(f32[32,384]{1,0:T(8,128)S(1)} %add_add_fusion), channel_id=1, source_target_pairs={{16,0},{17,1},{18,2},{19,3},{20,4},{21,5},{22,6},{23,7},{24,8},{25... | collective-permute-start | bytes 147464 | tf_op jit(solution)/shard_map/ppermute | solution.py:28

commit v6 on v4

--- a/solution.py
+++ b/solution.py
@@ -219,10 +219,10 @@
         extra[h, :, mine:] = bias_parts
 
 
-def middle_kernel(parts, weight_t, out):
-    helps, length, width = out.shape
+def middle_kernel(parts, weight_t, back, side):
+    helps, length, width = side.shape
     share = width // helps
-    mine = length - 2 * share
+    mine = back.shape[0]
     total = parts[0, :mine].astype(jnp.float32)
     for s in range(1, helps):
         total = total + parts[s, :mine].astype(jnp.float32)
@@ -234,7 +234,7 @@
     decay = jnp.exp(jnp.minimum(pre, 0.0))
     slope = jnp.where(pre > 0.0, 1.0, decay)
     grad = (cotb[:, :mine].astype(jnp.float32) * slope).astype(jnp.bfloat16)
-    back = lax.dot_general(
+    back[...] = lax.dot_general(
         grad, weight_t[...], TN, preferred_element_type=jnp.float32
     ).astype(jnp.bfloat16)
     terms = lax.dot_general(grad, agg, NN, preferred_element_type=jnp.float32).astype(jnp.bfloat16)
@@ -246,49 +246,60 @@
     sums = jnp.where(lane == 0, high, low)
     for h in range(helps):
         own = slice(h * share, (h + 1) * share)
-        out[h, :mine, :] = back
-        out[h, mine : mine + share, :] = terms[own]
-        out[h, mine + share :, :mine] = result[own]
-        out[h, mine + share :, mine:] = sums[own]
-
-
-def divide_kernel(parts, back, out, total, side, sems):
-    helps, _, width = parts.shape
-    mine = back.shape[0] // helps
-    share = total.shape[0]
-    copies = []
-    for s in range(helps):
-        copies.append(pltpu.make_async_copy(parts.at[s, mine:], side.at[s], sems.at[s]))
-        copies.append(
-            pltpu.make_async_copy(
-                parts.at[s, :mine], back.at[s * mine : (s + 1) * mine], sems.at[helps + s]
-            )
-        )
-    for copy in copies:
-        copy.start()
-    for copy in copies[0::2]:
-        copy.wait()
+        side[h, :share, :] = terms[own]
+        side[h, share:, :mine] = result[own]
+        side[h, share:, mine:] = sums[own]
+
+
+def divide_kernel(side, out, total):
+    helps, length, width = side.shape
+    share = length // 2
+    mine = out.shape[1] // helps
     sums = side[0].astype(jnp.float32)
     for s in range(1, helps):
         sums = sums + side[s].astype(jnp.float32)
-    total[:, :width] = sums[:share]
     both = sums[share:, mine : mine + 1] + sums[share:, mine + 1 : mine + 2]
-    total[:, width:] = jnp.broadcast_to(both, (share, total.shape[1] - width))
+    both = jnp.broadcast_to(both, (share, width))
+    for i in range(share):
+        total[i] = sums[i : i + 1, :]
+        total[share + i] = both[i : i + 1, :]
     for s in range(helps):
         out[:, s * mine : (s + 1) * mine] = side[s, share:, :mine]
-    for copy in copies[1::2]:
-        copy.wait()
+
+
+def gather_row_kernel(rows, out):
+    row = rows[0]
+    for i in range(1, rows.shape[0]):
+        row = row + rows[i]
+    for i in range(out.shape[0]):
+        out[i] = row
+
+
+def place_kernel(turn, *refs):
+    *parts, out, sems = refs
+    count = len(parts)
+    copies = []
+    for i, part in enumerate(parts):
+        at = lax.rem(turn[0] + i, count)
+        copies.append(pltpu.make_async_copy(part, out.at[at], sems.at[i]))
+        copies[i].start()
+    for copy in copies:
+        copy.wait()
+
+
+def in_place(space, turn, *parts):
+    return pl.pallas_call(
+        place_kernel,
+        out_shape=space((len(parts),) + parts[0].shape, parts[0].dtype),
+        in_specs=[SMEM] + [ANY] * len(parts),
+        out_specs=ANY,
+        scratch_shapes=[pltpu.SemaphoreType.DMA((len(parts),))],
+        compiler_params=pltpu.CompilerParams(vmem_limit_bytes=2 * 2**20),
+    )(turn.reshape(1), *(pltpu.with_memory_space_constraint(x, pltpu.HBM) for x in parts))
 
 
 def spread(x):
     return lax.all_to_all(x, "help", 0, 0)
-
-
-def round_of_four(total, one, two):
-    got = [
-        move(total, functools.partial(lambda s, b, h: (b ^ s, h), s)) for s in (one, two, one ^ two)
-    ]
-    return (total + got[0]) + (got[1] + got[2])
 
 
 def per_device(features_t, weight, bias, cotangent_t, tile_vals, slot_row, slot_col):
@@ -341,41 +352,49 @@
         (helps, mine + share, width),
         extra,
     )
-    length = mine + 2 * share
-    sent = pl.pallas_call(
+    back, side = pl.pallas_call(
         middle_kernel,
-        out_shape=jax.ShapeDtypeStruct((helps, length, width), jnp.bfloat16),
+        out_shape=(
+            jax.ShapeDtypeStruct((mine, width), jnp.bfloat16),
+            jax.ShapeDtypeStruct((helps, 2 * share, width), jnp.bfloat16),
+        ),
         in_specs=[VMEM] * 2,
-        out_specs=VMEM,
+        out_specs=(VMEM,) * 2,
         compiler_params=pltpu.CompilerParams(vmem_limit_bytes=16 * 2**20),
     )(spread(sent), weight_t)
-    back, output, total = pl.pallas_call(
+    helper = lax.axis_index("help").astype(jnp.int32)
+    pair = in_place(pltpu.HBM, helper & 1, back, move(back, lambda b, h: (b, h ^ 1)))
+    along = lambda d: functools.partial(lambda d, b, h: (b, (h + 2 * d) % helps), d)
+    back = in_place(pltpu.VMEM, helper >> 1, pair, *(move(pair, along(d)) for d in range(1, helps // 2)))
+    back = back.reshape(nodes, width)
+
+    output, total = pl.pallas_call(
         divide_kernel,
         out_shape=(
-            pltpu.VMEM((nodes, width), jnp.bfloat16),
             jax.ShapeDtypeStruct((share, nodes), jnp.bfloat16),
-            jax.ShapeDtypeStruct((share, width + tile), jnp.float32),
+            jax.ShapeDtypeStruct((blks, 1, width), jnp.float32),
         ),
-        in_specs=[ANY],
-        out_specs=(ANY, VMEM, VMEM),
-        scratch_shapes=[
-            pltpu.VMEM((helps, 2 * share, width), jnp.bfloat16),
-            pltpu.SemaphoreType.DMA((2 * helps,)),
-        ],
+        in_specs=[VMEM],
+        out_specs=(VMEM, VMEM),
         compiler_params=pltpu.CompilerParams(vmem_limit_bytes=4 * 2**20),
-    )(spread(sent))
+    )(spread(side))
+    back = after(back, total)
+    total = pl.pallas_call(
+        gather_row_kernel,
+        out_shape=jax.ShapeDtypeStruct(total.shape, jnp.float32),
+        in_specs=[VMEM],
+        out_specs=VMEM,
+        compiler_params=pltpu.CompilerParams(vmem_limit_bytes=2 * 2**20),
+    )(lax.all_to_all(total, "blk", 0, 0))
     zero, one, two = near(back)
-    half = blks // 2
-    total = after(round_of_four(total, 1, half), two)
-    three = move(after(one, total), swap)
-    total = round_of_four(total, 8, 16)
+    three = move(after(one, (total, two)), swap)
+    total = lax.all_to_all(total, "blk", 0, 0)
     value = aggregate(
         backward_kernel, (back, zero, one, two, three), tiles, slots, (helps, share, nodes)
     )
-    propagated = jnp.sum(spread(value).astype(jnp.float32), axis=0)
-    total = round_of_four(total, 2, 4)
-    total = total * (1.0 / math.sqrt(nodes * blks))
-    return (output, propagated, total[:, :width].T, total[:, width])
+    propagated = jnp.sum(spread(after(value, total)).astype(jnp.float32), axis=0)
+    total = total[:, 0, :] * (1.0 / math.sqrt(nodes * blks))
+    return (output, propagated, total[:share].T, total[share:, 0])
 
 
 def solution(mesh):

time: 147 us -> 172 us (1.17)
  waiting for transfers between devices: 10.7 us -> 42.6 us
  blocking collectives: 32.1 us -> 16.5 us
  Pallas kernels: 14.5 us -> 25.3 us
  starting transfers between devices: 81.2 us -> 79 us
    all_to_all x0 -> x2, waiting for transfers between devices: none -> 24.1 us  [the longest x1 13.7 us: per_device(): lax.all_to_all(total, 'blk', 0, 0)]
    ppermute x17 -> x12, starting transfers between devices: 77.7 us -> 55.4 us  [move(): return lax.ppermute(block, AXES, route)]
    all_to_all x0 -> x2, starting transfers between devices: none -> 16.7 us  [the longest x1 8.97 us: per_device(): lax.all_to_all(total, 'blk', 0, 0)]
    all_to_all x2 -> x1, blocking collectives: 32.1 us -> 16.5 us  [spread(): return lax.all_to_all(x, 'help', 0, 0)]
    all_to_all x1 -> x2, waiting for transfers between devices: 0.01 us -> 11.3 us  [spread(): return lax.all_to_all(x, 'help', 0, 0)]
    pallas_call x2 -> x5, Pallas kernels: 2.9 us -> 11.1 us  [the longest x2 8.32 us: in_place(): pl.pallas_call(place_kernel, out_shape=space((len(parts),) + parts[0].sha...]
    ppermute x17 -> x12, waiting for transfers between devices: 10.7 us -> 7.18 us  [move(): return lax.ppermute(block, AXES, route)]
    all_to_all x1 -> x2, starting transfers between devices: 3.56 us -> 6.97 us  [spread(): return lax.all_to_all(x, 'help', 0, 0)]
  transfers between devices with their start and end apart: 18 -> 16, of which waited for: 3 -> 6; matrix products, arithmetic and copies ran while one was open for 1% -> 1% of each run, Pallas kernels for 5% -> 10%
where the time goes in v6:
time: 172 us; the launch traced here: 171 us
  starting transfers between devices  79 us (46%)
  waiting for transfers between devices  42.6 us (25%)
  Pallas kernels  25.3 us (15%)
  blocking collectives  16.5 us (10%)
  local copies, waits for them, and re-layouts  5.51 us (3%)
    ppermute x12, starting transfers between devices, move(): return lax.ppermute(block, AXES, route)  55.4 us
    all_to_all x1, blocking collectives, spread(): return lax.all_to_all(x, 'help', 0, 0)  16.5 us
    all_to_all x1, waiting for transfers between devices, per_device(): lax.all_to_all(total, 'blk', 0, 0)  13.7 us
    all_to_all x2, waiting for transfers between devices, spread(): return lax.all_to_all(x, 'help', 0, 0)  11.3 us
    pallas_call x2, Pallas kernels, aggregate(): pl.pallas_call(kernel, out_shape=pltpu.HBM(out_shape, jnp.bfloat16), in_s...  11.1 us
    all_to_all x1, waiting for transfers between devices, per_device(): total = lax.all_to_all(total, 'blk', 0, 0)  10.5 us
    all_to_all x1, starting transfers between devices, per_device(): lax.all_to_all(total, 'blk', 0, 0)  8.97 us
    pallas_call x2, Pallas kernels, in_place(): pl.pallas_call(place_kernel, out_shape=space((len(parts),) + parts[0].sha...  8.32 us
  transfers between devices with their start and end apart: 16, of which 6 were waited for; matrix products, arithmetic and copies ran while one was open for 1% of the time, Pallas kernels for 10%

profile of v6, /device:TPU:1, one launch (start us, length us, event | category | flops | bytes accessed | tf_op | source)
XLA Modules:
  0.0 170.7 jit_solution(2460491672677707332)
XLA Ops:
  0.6 4.4 %collective-permute-start.1 = (bf16[256,1536]{1,0:T(8,128)(2,1)}, bf16[256,1536]{1,0:T(8,128)(2,1)S(1)}, u32[]{:S(2)}, u32[]{:S(2)}) collective-permute-start(bf16[256,1536]{1,0:T(8,128)(2,1)} %own.1), channel_id=1, source_target_pairs={{16,0},{17,1},{18,2},{19,3},{20,4},{21,5},{22,6},{23,7},{505,8},{5... | collective-permute-start | bytes 2359304 | tf_op jit(solution)/shard_map/ppermute | solution.py:28
  5.0 12.6 %collective-permute-start = (bf16[256,1536]{1,0:T(8,128)(2,1)}, bf16[256,1536]{1,0:T(8,128)(2,1)}, u32[]{:S(2)}, u32[]{:S(2)}) collective-permute-start(bf16[256,1536]{1,0:T(8,128)(2,1)} %own.1), channel_id=1, source_target_pairs={{8,0},{9,1},{10,2},{11,3},{12,4},{13,5},{14,6},{15,7},{0,8},{1,9},... | collective-permute-start | bytes 2359304 | tf_op jit(solution)/shard_map/ppermute | solution.py:28
  17.7 2.6 %collective-permute-start.2 = (bf16[256,1536]{1,0:T(8,128)(2,1)}, bf16[256,1536]{1,0:T(8,128)(2,1)}, u32[]{:S(2)}, u32[]{:S(2)}) collective-permute-start(bf16[256,1536]{1,0:T(8,128)(2,1)} %own.1), channel_id=1, source_target_pairs={{497,0},{496,1},{499,2},{498,3},{501,4},{500,5},{503,6},{502,7},{2... | collective-permute-start | bytes 2359304 | tf_op jit(solution)/shard_map/ppermute | solution.py:28
  23.3 3.1 %shard_map.102 = (s32[92]{0:T(128)S(1)}, s32[46]{0:T(128)S(1)}, bf16[8,32,256]{2,1,0:T(8,128)(2,1)S(1)}, bf16[256,256]{1,0:T(8,128)(2,1)S(1)}, bf16[80,128,128]{...) custom-call(s32[1]{0:T(128)} %bitcast.odd, s32[80]{0:T(128)S(1)} %bitcast.20, s32[80]{0:T(128)S(1)} %bitcast.21, ...), custom_call_target="tpu_custom_call" | custom-call | tf_op jit(solution)/shard_map/pallas_call | solution.py:319
  26.4 5.0 %collective-permute-start.3 = (bf16[256,1536]{1,0:T(8,128)(2,1)S(1)}, bf16[256,1536]{1,0:T(8,128)(2,1)S(1)}, u32[]{:S(2)}, u32[]{:S(2)}) collective-permute-start(bf16[256,1536]{1,0:T(8,128)(2,1)S(1)} %collective-permute-done.1.b2), channel_id=1, source_target_pairs={{8,0},{9,1},{10,2},{11,3},{12,4},{13,5},{14,6},{15,7},{0,8},{1,9},... | collective-permute-start | bytes 2359304 | tf_op jit(solution)/shard_map/ppermute | solution.py:28
  33.6 5.5 %shard_map.103 = bf16[8,224,256]{2,1,0:T(8,128)(2,1)} custom-call(s32[92]{0:T(128)S(1)} %get-tuple-element.18.pairs, s32[46]{0:T(128)S(1)} %get-tuple-element.19.rows, bf16[256,1536]{1,0:T(8,128)(2,1)S(1)} %get-tuple-element.20.b0, bf16[256,1536]{1,0:T(8,128)(2,1)} %collective-permute-done.b1, bf16[256,1536]{1,0:T(8,128)(2,1)S(1)} %collective-permute-done.1.b2, ...), custom_call_target="tpu_custom_call" | custom-call | flops 671088640 | bytes 6291456 | tf_op jit(solution)/shard_map/pallas_call | solution.py:138
  39.1 16.5 %all_to_all.25.parts = bf16[8,224,256]{2,1,0:T(8,128)(2,1)S(1)} all-to-all(bf16[8,224,256]{2,1,0:T(8,128)(2,1)} %shard_map.103), channel_id=1, replica_groups=mesh['blk'=64,'help'=8] {'help'}, dimensions={0} | all-to-all | bytes 1835008 | tf_op jit(solution)/shard_map/all_to_all | solution.py:302
  56.9 2.7 %collective-permute-start.4 = (bf16[192,256]{1,0:T(8,128)(2,1)S(1)}, bf16[192,256]{1,0:T(8,128)(2,1)S(1)}, u32[]{:S(2)}, u32[]{:S(2)}) collective-permute-start(bf16[192,256]{1,0:T(8,128)(2,1)S(1)} %get-tuple-element.27.refs_0_), channel_id=1, source_target_pairs={{1,0},{0,1},{3,2},{2,3},{5,4},{4,5},{7,6},{6,7},{9,8},{8,9},{11,10... | collective-permute-start | bytes 294920 | tf_op jit(solution)/shard_map/ppermute | solution.py:28
  59.6 3.4 %all-to-all-start.1 = ((bf16[8,64,256]{2,1,0:T(8,128)(2,1)}), bf16[8,64,256]{2,1,0:T(8,128)(2,1)S(1)}, u32[]{:S(2)}, u32[]{:S(2)}) async-start(bf16[8,64,256]{2,1,0:T(8,128)(2,1)} %get-tuple-element.25), calls=%async_computation.1 | async-start | bytes 524288 | tf_op jit(solution)/shard_map/all_to_all | solution.py:302
  63.7 7.1 %shard_map.106.refs_0_ = bf16[2,192,256]{2,1,0:T(8,128)(2,1)} custom-call(s32[1]{0:T(128)} %bitcast.6.turn, bf16[192,256]{1,0:T(8,128)(2,1)} %copy-done.1, bf16[192,256]{1,0:T(8,128)(2,1)} %copy-done.7), custom_call_target="tpu_custom_call" | custom-call | tf_op jit(solution)/shard_map/pallas_call | solution.py:291
  70.8 4.5 %collective-permute-start.5 = (bf16[2,192,256]{2,1,0:T(8,128)(2,1)}, bf16[2,192,256]{2,1,0:T(8,128)(2,1)S(1)}, u32[]{:S(2)}, u32[]{:S(2)}) collective-permute-start(bf16[2,192,256]{2,1,0:T(8,128)(2,1)} %shard_map.106.refs_0_), channel_id=1, source_target_pairs={{2,0},{3,1},{4,2},{5,3},{6,4},{7,5},{0,6},{1,7},{10,8},{11,9},{12,... | collective-permute-start | bytes 589832 | tf_op jit(solution)/shard_map/ppermute | solution.py:28
  75.3 2.5 %collective-permute-start.6 = (bf16[2,192,256]{2,1,0:T(8,128)(2,1)}, bf16[2,192,256]{2,1,0:T(8,128)(2,1)S(1)}, u32[]{:S(2)}, u32[]{:S(2)}) collective-permute-start(bf16[2,192,256]{2,1,0:T(8,128)(2,1)} %shard_map.106.refs_0_), channel_id=1, source_target_pairs={{4,0},{5,1},{6,2},{7,3},{0,4},{1,5},{2,6},{3,7},{12,8},{13,9},{14,... | collective-permute-start | bytes 589832 | tf_op jit(solution)/shard_map/ppermute | solution.py:28
  77.7 2.5 %collective-permute-start.7 = (bf16[2,192,256]{2,1,0:T(8,128)(2,1)}, bf16[2,192,256]{2,1,0:T(8,128)(2,1)S(1)}, u32[]{:S(2)}, u32[]{:S(2)}) collective-permute-start(bf16[2,192,256]{2,1,0:T(8,128)(2,1)} %shard_map.106.refs_0_), channel_id=1, source_target_pairs={{6,0},{7,1},{0,2},{1,3},{2,4},{3,5},{4,6},{5,7},{14,8},{15,9},{8,1... | collective-permute-start | bytes 589832 | tf_op jit(solution)/shard_map/ppermute | solution.py:28
  81.1 2.4 %collective-permute-done.6.refs_2_ = bf16[2,192,256]{2,1,0:T(8,128)(2,1)S(1)} collective-permute-done((bf16[2,192,256]{2,1,0:T(8,128)(2,1)}, bf16[2,192,256]{2,1,0:T(8,128)(2,1)S(1)}, u32[]{:S(2)}, u32[]{:S(2)}) %collective-permute-start.6) | collective-permute-done | bytes 196640 | tf_op jit(solution)/shard_map/ppermute | solution.py:28
  83.4 2.7 %collective-permute-done.7.refs_3_ = bf16[2,192,256]{2,1,0:T(8,128)(2,1)S(1)} collective-permute-done((bf16[2,192,256]{2,1,0:T(8,128)(2,1)}, bf16[2,192,256]{2,1,0:T(8,128)(2,1)S(1)}, u32[]{:S(2)}, u32[]{:S(2)}) %collective-permute-start.7) | collective-permute-done | bytes 196640 | tf_op jit(solution)/shard_map/ppermute | solution.py:28
  88.0 11.9 %collective-permute-start.10 = (bf16[1536,256]{1,0:T(8,128)(2,1)S(1)}, bf16[1536,256]{1,0:T(8,128)(2,1)}, u32[]{:S(2)}, u32[]{:S(2)}) collective-permute-start(bf16[1536,256]{1,0:T(8,128)(2,1)S(1)} %bitcast.16), channel_id=1, source_target_pairs={{497,0},{496,1},{499,2},{498,3},{501,4},{500,5},{503,6},{502,7},{2... | collective-permute-start | bytes 2359304 | tf_op jit(solution)/shard_map/ppermute | solution.py:28
  101.9 9.0 %all-to-all-start.2 = ((f32[64,1,256]{2,1,0:T(1,128)}), f32[64,1,256]{2,1,0:T(1,128)S(1)}, u32[]{:S(2)}, u32[]{:S(2)}) async-start(f32[64,1,256]{2,1,0:T(1,128)} %get-tuple-element.28), calls=%async_computation.2 | async-start | bytes 131072 | tf_op jit(solution)/shard_map/all_to_all | solution.py:388
  110.9 2.4 %collective-permute-start.8 = (bf16[1536,256]{1,0:T(8,128)(2,1)S(1)}, bf16[1536,256]{1,0:T(8,128)(2,1)}, u32[]{:S(2)}, u32[]{:S(2)}) collective-permute-start(bf16[1536,256]{1,0:T(8,128)(2,1)S(1)} %bitcast.18), channel_id=1, source_target_pairs={{8,0},{9,1},{10,2},{11,3},{12,4},{13,5},{14,6},{15,7},{0,8},{1,9},... | collective-permute-start | bytes 2359304 | tf_op jit(solution)/shard_map/ppermute | solution.py:28
  113.2 13.7 %all-to-all-done.2.rows = f32[64,1,256]{2,1,0:T(1,128)S(1)} async-done(((f32[64,1,256]{2,1,0:T(1,128)}), f32[64,1,256]{2,1,0:T(1,128)S(1)}, u32[]{:S(2)}, u32[]{:S(2)}) %all-to-all-start.2) | async-done | bytes 65568 | tf_op jit(solution)/shard_map/all_to_all | solution.py:388
  129.9 7.7 %all-to-all-start.3 = ((f32[64,1,256]{2,1,0:T(1,128)}), f32[64,1,256]{2,1,0:T(1,128)S(1)}, u32[]{:S(2)}, u32[]{:S(2)}) async-start(f32[64,1,256]{2,1,0:T(1,128)} %shard_map.108), calls=%async_computation.3 | async-start | bytes 131072 | tf_op jit(solution)/shard_map/all_to_all | solution.py:391
  137.6 5.6 %shard_map.109 = bf16[8,32,1536]{2,1,0:T(8,128)(2,1)} custom-call(s32[92]{0:T(128)S(1)} %get-tuple-element.18.pairs, s32[46]{0:T(128)S(1)} %get-tuple-element.19.rows, bf16[1536,256]{1,0:T(8,128)(2,1)S(1)} %bitcast.19, bf16[1536,256]{1,0:T(8,128)(2,1)} %collective-permute-done.8.b1, bf16[1536,256]{1,0:T(8,128)(2,1)} %collective-permute-done.9.b2, ...), custom_call_target="tpu_custom_call" | custom-call | flops 671088640 | bytes 6291456 | tf_op jit(solution)/shard_map/pallas_call | solution.py:138
  143.2 10.5 %all-to-all-done.3 = f32[64,1,256]{2,1,0:T(1,128)S(1)} async-done(((f32[64,1,256]{2,1,0:T(1,128)}), f32[64,1,256]{2,1,0:T(1,128)S(1)}, u32[]{:S(2)}, u32[]{:S(2)}) %all-to-all-start.3) | async-done | bytes 65568 | tf_op jit(solution)/shard_map/all_to_all | solution.py:391
  153.7 3.5 %all-to-all-start.4 = ((bf16[8,32,1536]{2,1,0:T(8,128)(2,1)}), bf16[8,32,1536]{2,1,0:T(8,128)(2,1)S(1)}, u32[]{:S(2)}, u32[]{:S(2)}) async-start(bf16[8,32,1536]{2,1,0:T(8,128)(2,1)} %shard_map.109), calls=%async_computation.4 | async-start | bytes 1572864 | tf_op jit(solution)/shard_map/all_to_all | solution.py:302
  158.6 11.2 %all-to-all-done.4 = bf16[8,32,1536]{2,1,0:T(8,128)(2,1)S(1)} async-done(((bf16[8,32,1536]{2,1,0:T(8,128)(2,1)}), bf16[8,32,1536]{2,1,0:T(8,128)(2,1)S(1)}, u32[]{:S(2)}, u32[]{:S(2)}) %all-to-all-start.4) | async-done | bytes 786464 | tf_op jit(solution)/shard_map/all_to_all | solution.py:302
  (40 shorter events, 16.8 us)
Async XLA Ops:
  0.6 25.8 %collective-permute-start.1 = (bf16[256,1536]{1,0:T(8,128)(2,1)}, bf16[256,1536]{1,0:T(8,128)(2,1)S(1)}, u32[]{:S(2)}, u32[]{:S(2)}) collective-permute-start(bf16[256,1536]{1,0:T(8,128)(2,1)} %own.1), channel_id=1, source_target_pairs={{16,0},{17,1},{18,2},{19,3},{20,4},{21,5},{22,6},{23,7},{505,8},{5... | collective-permute-start | bytes 2359304 | tf_op jit(solution)/shard_map/ppermute | solution.py:28
  5.0 26.4 %collective-permute-start = (bf16[256,1536]{1,0:T(8,128)(2,1)}, bf16[256,1536]{1,0:T(8,128)(2,1)}, u32[]{:S(2)}, u32[]{:S(2)}) collective-permute-start(bf16[256,1536]{1,0:T(8,128)(2,1)} %own.1), channel_id=1, source_target_pairs={{8,0},{9,1},{10,2},{11,3},{12,4},{13,5},{14,6},{15,7},{0,8},{1,9},... | collective-permute-start | bytes 2359304 | tf_op jit(solution)/shard_map/ppermute | solution.py:28
  17.7 15.9 %collective-permute-start.2 = (bf16[256,1536]{1,0:T(8,128)(2,1)}, bf16[256,1536]{1,0:T(8,128)(2,1)}, u32[]{:S(2)}, u32[]{:S(2)}) collective-permute-start(bf16[256,1536]{1,0:T(8,128)(2,1)} %own.1), channel_id=1, source_target_pairs={{497,0},{496,1},{499,2},{498,3},{501,4},{500,5},{503,6},{502,7},{2... | collective-permute-start | bytes 2359304 | tf_op jit(solution)/shard_map/ppermute | solution.py:28
  21.1 0.9 copy-start
  22.0 0.7 copy-start.2
  22.6 0.7 copy-start.3
  26.4 7.2 %collective-permute-start.3 = (bf16[256,1536]{1,0:T(8,128)(2,1)S(1)}, bf16[256,1536]{1,0:T(8,128)(2,1)S(1)}, u32[]{:S(2)}, u32[]{:S(2)}) collective-permute-start(bf16[256,1536]{1,0:T(8,128)(2,1)S(1)} %collective-permute-done.1.b2), channel_id=1, source_target_pairs={{8,0},{9,1},{10,2},{11,3},{12,4},{13,5},{14,6},{15,7},{0,8},{1,9},... | collective-permute-start | bytes 2359304 | tf_op jit(solution)/shard_map/ppermute | solution.py:28
  56.9 6.2 %copy-start.1 = (bf16[192,256]{1,0:T(8,128)(2,1)}, bf16[192,256]{1,0:T(8,128)(2,1)S(1)}, u32[]{:S(2)}) copy-start(bf16[192,256]{1,0:T(8,128)(2,1)S(1)} %get-tuple-element.27.refs_0_) | copy-start | bytes 294916
  56.9 6.2 %collective-permute-start.4 = (bf16[192,256]{1,0:T(8,128)(2,1)S(1)}, bf16[192,256]{1,0:T(8,128)(2,1)S(1)}, u32[]{:S(2)}, u32[]{:S(2)}) collective-permute-start(bf16[192,256]{1,0:T(8,128)(2,1)S(1)} %get-tuple-element.27.refs_0_), channel_id=1, source_target_pairs={{1,0},{0,1},{3,2},{2,3},{5,4},{4,5},{7,6},{6,7},{9,8},{8,9},{11,10... | collective-permute-start | bytes 294920 | tf_op jit(solution)/shard_map/ppermute | solution.py:28
  59.6 20.6 %all-to-all-start.1 = ((bf16[8,64,256]{2,1,0:T(8,128)(2,1)}), bf16[8,64,256]{2,1,0:T(8,128)(2,1)S(1)}, u32[]{:S(2)}, u32[]{:S(2)}) async-start(bf16[8,64,256]{2,1,0:T(8,128)(2,1)} %get-tuple-element.25), calls=%async_computation.1 | async-start | bytes 524288 | tf_op jit(solution)/shard_map/all_to_all | solution.py:302
  63.1 0.6 copy-start.7
  70.8 10.3 %collective-permute-start.5 = (bf16[2,192,256]{2,1,0:T(8,128)(2,1)}, bf16[2,192,256]{2,1,0:T(8,128)(2,1)S(1)}, u32[]{:S(2)}, u32[]{:S(2)}) collective-permute-start(bf16[2,192,256]{2,1,0:T(8,128)(2,1)} %shard_map.106.refs_0_), channel_id=1, source_target_pairs={{2,0},{3,1},{4,2},{5,3},{6,4},{7,5},{0,6},{1,7},{10,8},{11,9},{12,... | collective-permute-start | bytes 589832 | tf_op jit(solution)/shard_map/ppermute | solution.py:28
  75.3 8.1 %collective-permute-start.6 = (bf16[2,192,256]{2,1,0:T(8,128)(2,1)}, bf16[2,192,256]{2,1,0:T(8,128)(2,1)S(1)}, u32[]{:S(2)}, u32[]{:S(2)}) collective-permute-start(bf16[2,192,256]{2,1,0:T(8,128)(2,1)} %shard_map.106.refs_0_), channel_id=1, source_target_pairs={{4,0},{5,1},{6,2},{7,3},{0,4},{1,5},{2,6},{3,7},{12,8},{13,9},{14,... | collective-permute-start | bytes 589832 | tf_op jit(solution)/shard_map/ppermute | solution.py:28
  77.7 8.3 %collective-permute-start.7 = (bf16[2,192,256]{2,1,0:T(8,128)(2,1)}, bf16[2,192,256]{2,1,0:T(8,128)(2,1)S(1)}, u32[]{:S(2)}, u32[]{:S(2)}) collective-permute-start(bf16[2,192,256]{2,1,0:T(8,128)(2,1)} %shard_map.106.refs_0_), channel_id=1, source_target_pairs={{6,0},{7,1},{0,2},{1,3},{2,4},{3,5},{4,6},{5,7},{14,8},{15,9},{8,1... | collective-permute-start | bytes 589832 | tf_op jit(solution)/shard_map/ppermute | solution.py:28
  81.1 5.0 %copy-start.4 = (bf16[2,192,256]{2,1,0:T(8,128)(2,1)}, bf16[2,192,256]{2,1,0:T(8,128)(2,1)S(1)}, u32[]{:S(2)}) copy-start(bf16[2,192,256]{2,1,0:T(8,128)(2,1)S(1)} %collective-permute-done.5.refs_1_) | copy-start | bytes 589828
  83.4 2.7 %copy-start.5 = (bf16[2,192,256]{2,1,0:T(8,128)(2,1)}, bf16[2,192,256]{2,1,0:T(8,128)(2,1)S(1)}, u32[]{:S(2)}) copy-start(bf16[2,192,256]{2,1,0:T(8,128)(2,1)S(1)} %collective-permute-done.6.refs_2_) | copy-start | bytes 589828
  86.1 0.7 copy-start.6
  88.0 39.6 %collective-permute-start.10 = (bf16[1536,256]{1,0:T(8,128)(2,1)S(1)}, bf16[1536,256]{1,0:T(8,128)(2,1)}, u32[]{:S(2)}, u32[]{:S(2)}) collective-permute-start(bf16[1536,256]{1,0:T(8,128)(2,1)S(1)} %bitcast.16), channel_id=1, source_target_pairs={{497,0},{496,1},{499,2},{498,3},{501,4},{500,5},{503,6},{502,7},{2... | collective-permute-start | bytes 2359304 | tf_op jit(solution)/shard_map/ppermute | solution.py:28
  99.9 27.7 %collective-permute-start.9 = (bf16[1536,256]{1,0:T(8,128)(2,1)S(1)}, bf16[1536,256]{1,0:T(8,128)(2,1)}, u32[]{:S(2)}, u32[]{:S(2)}) collective-permute-start(bf16[1536,256]{1,0:T(8,128)(2,1)S(1)} %bitcast.17), channel_id=1, source_target_pairs={{16,0},{17,1},{18,2},{19,3},{20,4},{21,5},{22,6},{23,7},{505,8},{5... | collective-permute-start | bytes 2359304 | tf_op jit(solution)/shard_map/ppermute | solution.py:28
  101.9 25.0 %all-to-all-start.2 = ((f32[64,1,256]{2,1,0:T(1,128)}), f32[64,1,256]{2,1,0:T(1,128)S(1)}, u32[]{:S(2)}, u32[]{:S(2)}) async-start(f32[64,1,256]{2,1,0:T(1,128)} %get-tuple-element.28), calls=%async_computation.2 | async-start | bytes 131072 | tf_op jit(solution)/shard_map/all_to_all | solution.py:388
  110.9 26.8 %collective-permute-start.8 = (bf16[1536,256]{1,0:T(8,128)(2,1)S(1)}, bf16[1536,256]{1,0:T(8,128)(2,1)}, u32[]{:S(2)}, u32[]{:S(2)}) collective-permute-start(bf16[1536,256]{1,0:T(8,128)(2,1)S(1)} %bitcast.18), channel_id=1, source_target_pairs={{8,0},{9,1},{10,2},{11,3},{12,4},{13,5},{14,6},{15,7},{0,8},{1,9},... | collective-permute-start | bytes 2359304 | tf_op jit(solution)/shard_map/ppermute | solution.py:28
  127.6 10.0 %collective-permute-start.11 = (bf16[1536,256]{1,0:T(8,128)(2,1)}, bf16[1536,256]{1,0:T(8,128)(2,1)}, u32[]{:S(2)}, u32[]{:S(2)}) collective-permute-start(bf16[1536,256]{1,0:T(8,128)(2,1)} %collective-permute-done.9.b2), channel_id=1, source_target_pairs={{8,0},{9,1},{10,2},{11,3},{12,4},{13,5},{14,6},{15,7},{0,8},{1,9},... | collective-permute-start | bytes 2359304 | tf_op jit(solution)/shard_map/ppermute | solution.py:28
  129.9 23.8 %all-to-all-start.3 = ((f32[64,1,256]{2,1,0:T(1,128)}), f32[64,1,256]{2,1,0:T(1,128)S(1)}, u32[]{:S(2)}, u32[]{:S(2)}) async-start(f32[64,1,256]{2,1,0:T(1,128)} %shard_map.108), calls=%async_computation.3 | async-start | bytes 131072 | tf_op jit(solution)/shard_map/all_to_all | solution.py:391
  153.7 16.2 %all-to-all-start.4 = ((bf16[8,32,1536]{2,1,0:T(8,128)(2,1)}), bf16[8,32,1536]{2,1,0:T(8,128)(2,1)S(1)}, u32[]{:S(2)}, u32[]{:S(2)}) async-start(bf16[8,32,1536]{2,1,0:T(8,128)(2,1)} %shard_map.109), calls=%async_computation.4 | async-start | bytes 1572864 | tf_op jit(solution)/shard_map/all_to_all | solution.py:302

commit v7 on v5

--- a/solution.py
+++ b/solution.py
@@ -289,16 +289,8 @@
     return lax.all_to_all(x, "help", 0, 0)
 
 
-def round_of_four(total, one, two):
-    got = [
-        move(total, functools.partial(lambda s, b, h: (b ^ s, h), s)) for s in (one, two, one ^ two)
-    ]
-    return (total + got[0]) + (got[1] + got[2])
-
-
-def fours(blks, one, two):
-    bases = [b for b in range(blks) if b & (one | two) == 0]
-    return [[b, b | one, b | two, b | one | two] for b in bases]
+def alike(blks, steps):
+    return [[b for b in range(blks) if b & ~steps == base] for base in range(blks) if base & steps == 0]
 
 
 def per_device(features_t, weight, bias, cotangent_t, tile_vals, slot_row, slot_col):
@@ -364,28 +356,28 @@
         out_shape=(
             pltpu.VMEM((nodes, width), jnp.bfloat16),
             jax.ShapeDtypeStruct((share, nodes), jnp.bfloat16),
-            pltpu.HBM((4, share, width + tile), jnp.float32),
+            pltpu.HBM((8, share, width + tile), jnp.float32),
         ),
         in_specs=[ANY],
         out_specs=(ANY, VMEM, ANY),
         scratch_shapes=[
             pltpu.VMEM((helps, 2 * share, width), jnp.bfloat16),
             pltpu.VMEM((share, width + tile), jnp.float32),
-            pltpu.SemaphoreType.DMA((2 * helps + 4,)),
+            pltpu.SemaphoreType.DMA((2 * helps + 8,)),
         ],
         compiler_params=pltpu.CompilerParams(vmem_limit_bytes=4 * 2**20),
     )(spread(sent))
     zero, one, two = near(back)
     half = blks // 2
-    far = lax.all_to_all(total, "blk", 0, 0, axis_index_groups=fours(blks, 8, 16))
+    far = lax.all_to_all(total, "blk", 0, 0, axis_index_groups=alike(blks, half | 3))
     total = jnp.sum(far, axis=0)
     three = move(after(one, (total, two)), swap)
     value = aggregate(
         backward_kernel, (back, zero, one, two, three), tiles, slots, (helps, share, nodes)
     )
     propagated = jnp.sum(spread(value).astype(jnp.float32), axis=0)
-    total = round_of_four(total, 1, half)
-    total = round_of_four(total, 2, 4)
+    for step in (16, 8, 4):
+        total = total + move(total, functools.partial(lambda s, b, h: (b ^ s, h), step))
     total = total * (1.0 / math.sqrt(nodes * blks))
     return (output, propagated, total[:, :width].T, total[:, width])
 

time: 149 us -> 147 us (0.987)
  starting transfers between devices: 70.8 us -> 63.6 us
  waiting for transfers between devices: 19.7 us -> 24.1 us
    ppermute x14 -> x11, waiting for transfers between devices: 7.13 us -> 24.1 us  [move(): return lax.ppermute(block, AXES, route)]
    all_to_all x1, waiting for transfers between devices: 12.5 us -> 0.01 us  [per_device(): lax.all_to_all(total, 'blk', 0, 0, axis_index_groups=alike(blks, half | 3))]
    ppermute x14 -> x11, starting transfers between devices: 63.3 us -> 52.3 us  [move(): return lax.ppermute(block, AXES, route)]
    all_to_all x1, starting transfers between devices: 4.01 us -> 7.77 us  [per_device(): lax.all_to_all(total, 'blk', 0, 0, axis_index_groups=alike(blks, half | 3))]
  transfers between devices with their start and end apart: 16 -> 13, of which waited for: 5 -> 6; matrix products, arithmetic and copies ran while one was open for 3% -> 2% of each run, Pallas kernels for 6% -> 6%
where the time goes in v7:
time: 147 us; the launch traced here: 144 us
  starting transfers between devices  63.6 us (43%)
  blocking collectives  32 us (22%)
  waiting for transfers between devices  24.1 us (16%)
  Pallas kernels  17.6 us (12%)
  local copies, waits for them, and re-layouts  4.19 us (3%)
  other arithmetic  1.83 us (1%)
    ppermute x11, starting transfers between devices, move(): return lax.ppermute(block, AXES, route)  52.3 us
    all_to_all x2, blocking collectives, spread(): return lax.all_to_all(x, 'help', 0, 0)  32 us
    ppermute x11, waiting for transfers between devices, move(): return lax.ppermute(block, AXES, route)  24.1 us
    pallas_call x2, Pallas kernels, aggregate(): pl.pallas_call(kernel, out_shape=pltpu.HBM(out_shape, jnp.bfloat16), in_s...  10.8 us
    all_to_all x1, starting transfers between devices, per_device(): lax.all_to_all(total, 'blk', 0, 0, axis_index_groups=alike(blks, half | 3))  7.77 us
    all_to_all x1, starting transfers between devices, spread(): return lax.all_to_all(x, 'help', 0, 0)  3.56 us
    pallas_call x1, Pallas kernels, per_device(): pl.pallas_call(functools.partial(prepare_kernel, row_tiles), out_shape=(j...  3.13 us
    pallas_call x1, Pallas kernels, per_device(): pl.pallas_call(divide_kernel, out_shape=(pltpu.VMEM((nodes, width), jnp.b...  3.1 us
  transfers between devices with their start and end apart: 13, of which 6 were waited for; matrix products, arithmetic and copies ran while one was open for 2% of the time, Pallas kernels for 6%

profile of v7, /device:TPU:1, one launch (start us, length us, event | category | flops | bytes accessed | tf_op | source)
XLA Modules:
  0.0 144.2 jit_solution(16371671385007557611)
XLA Ops:
  0.6 4.4 %collective-permute-start.1 = (bf16[256,1536]{1,0:T(8,128)(2,1)}, bf16[256,1536]{1,0:T(8,128)(2,1)S(1)}, u32[]{:S(2)}, u32[]{:S(2)}) collective-permute-start(bf16[256,1536]{1,0:T(8,128)(2,1)} %own.1), channel_id=1, source_target_pairs={{16,0},{17,1},{18,2},{19,3},{20,4},{21,5},{22,6},{23,7},{505,8},{5... | collective-permute-start | bytes 2359304 | tf_op jit(solution)/shard_map/ppermute | solution.py:28
  5.0 12.6 %collective-permute-start = (bf16[256,1536]{1,0:T(8,128)(2,1)}, bf16[256,1536]{1,0:T(8,128)(2,1)}, u32[]{:S(2)}, u32[]{:S(2)}) collective-permute-start(bf16[256,1536]{1,0:T(8,128)(2,1)} %own.1), channel_id=1, source_target_pairs={{8,0},{9,1},{10,2},{11,3},{12,4},{13,5},{14,6},{15,7},{0,8},{1,9},... | collective-permute-start | bytes 2359304 | tf_op jit(solution)/shard_map/ppermute | solution.py:28
  17.7 2.6 %collective-permute-start.2 = (bf16[256,1536]{1,0:T(8,128)(2,1)}, bf16[256,1536]{1,0:T(8,128)(2,1)}, u32[]{:S(2)}, u32[]{:S(2)}) collective-permute-start(bf16[256,1536]{1,0:T(8,128)(2,1)} %own.1), channel_id=1, source_target_pairs={{497,0},{496,1},{499,2},{498,3},{501,4},{500,5},{503,6},{502,7},{2... | collective-permute-start | bytes 2359304 | tf_op jit(solution)/shard_map/ppermute | solution.py:28
  23.3 3.1 %shard_map.102 = (s32[92]{0:T(128)S(1)}, s32[46]{0:T(128)S(1)}, bf16[8,32,256]{2,1,0:T(8,128)(2,1)S(1)}, bf16[256,256]{1,0:T(8,128)(2,1)S(1)}, bf16[80,128,128]{...) custom-call(s32[1]{0:T(128)} %bitcast.odd, s32[80]{0:T(128)S(1)} %bitcast.7, s32[80]{0:T(128)S(1)} %bitcast.8, ...), custom_call_target="tpu_custom_call" | custom-call | tf_op jit(solution)/shard_map/pallas_call | solution.py:310
  26.4 5.0 %collective-permute-start.3 = (bf16[256,1536]{1,0:T(8,128)(2,1)S(1)}, bf16[256,1536]{1,0:T(8,128)(2,1)S(1)}, u32[]{:S(2)}, u32[]{:S(2)}) collective-permute-start(bf16[256,1536]{1,0:T(8,128)(2,1)S(1)} %collective-permute-done.1.b2), channel_id=1, source_target_pairs={{8,0},{9,1},{10,2},{11,3},{12,4},{13,5},{14,6},{15,7},{0,8},{1,9},... | collective-permute-start | bytes 2359304 | tf_op jit(solution)/shard_map/ppermute | solution.py:28
  31.4 2.1 %collective-permute-done.2.b3 = bf16[256,1536]{1,0:T(8,128)(2,1)} collective-permute-done((bf16[256,1536]{1,0:T(8,128)(2,1)}, bf16[256,1536]{1,0:T(8,128)(2,1)}, u32[]{:S(2)}, u32[]{:S(2)}) %collective-permute-start.2) | collective-permute-done | bytes 786464 | tf_op jit(solution)/shard_map/ppermute | solution.py:28
  33.6 5.5 %shard_map.103 = bf16[8,224,256]{2,1,0:T(8,128)(2,1)} custom-call(s32[92]{0:T(128)S(1)} %get-tuple-element.15.pairs, s32[46]{0:T(128)S(1)} %get-tuple-element.16.rows, bf16[256,1536]{1,0:T(8,128)(2,1)S(1)} %get-tuple-element.17.b0, bf16[256,1536]{1,0:T(8,128)(2,1)} %collective-permute-done.b1, bf16[256,1536]{1,0:T(8,128)(2,1)S(1)} %collective-permute-done.1.b2, ...), custom_call_target="tpu_custom_call" | custom-call | flops 671088640 | bytes 6291456 | tf_op jit(solution)/shard_map/pallas_call | solution.py:138
  39.1 16.6 %all_to_all.20.parts = bf16[8,224,256]{2,1,0:T(8,128)(2,1)S(1)} all-to-all(bf16[8,224,256]{2,1,0:T(8,128)(2,1)} %shard_map.103), channel_id=1, replica_groups=mesh['blk'=64,'help'=8] {'help'}, dimensions={0} | all-to-all | bytes 1835008 | tf_op jit(solution)/shard_map/all_to_all | solution.py:289
  56.3 15.4 %all_to_all.21.parts = bf16[8,256,256]{2,1,0:T(8,128)(2,1)S(1)} all-to-all(bf16[8,256,256]{2,1,0:T(8,128)(2,1)S(1)} %shard_map.104), channel_id=1, replica_groups=mesh['blk'=64,'help'=8] {'help'}, dimensions={0} | all-to-all | bytes 2097152 | tf_op jit(solution)/shard_map/all_to_all | solution.py:289
  71.7 3.1 %shard_map.105 = (bf16[1536,256]{1,0:T(8,128)(2,1)S(1)}, bf16[32,1536]{1,0:T(8,128)(2,1)}, f32[8,32,384]{2,1,0:T(8,128)}) custom-call(bf16[8,256,256]{2,1,0:T(8,128)(2,1)S(1)} %all_to_all.21.parts), custom_call_target="tpu_custom_call" | custom-call | tf_op jit(solution)/shard_map/pallas_call | solution.py:354
  74.8 7.8 %all-to-all-start.2 = ((f32[8,32,384]{2,1,0:T(8,128)}), f32[8,32,384]{2,1,0:T(8,128)}, u32[]{:S(2)}, u32[]{:S(2)}) async-start(f32[8,32,384]{2,1,0:T(8,128)} %get-tuple-element.24), calls=%async_computation.2 | async-start | bytes 786432 | tf_op jit(solution)/shard_map/all_to_all | solution.py:372
  82.6 10.3 %collective-permute-start.6 = (bf16[1536,256]{1,0:T(8,128)(2,1)S(1)}, bf16[1536,256]{1,0:T(8,128)(2,1)}, u32[]{:S(2)}, u32[]{:S(2)}) collective-permute-start(bf16[1536,256]{1,0:T(8,128)(2,1)S(1)} %get-tuple-element.23.b0), channel_id=1, source_target_pairs={{497,0},{496,1},{499,2},{498,3},{501,4},{500,5},{503,6},{502,7},{2... | collective-permute-start | bytes 2359304 | tf_op jit(solution)/shard_map/ppermute | solution.py:28
  92.8 1.9 %collective-permute-start.5 = (bf16[1536,256]{1,0:T(8,128)(2,1)S(1)}, bf16[1536,256]{1,0:T(8,128)(2,1)}, u32[]{:S(2)}, u32[]{:S(2)}) collective-permute-start(bf16[1536,256]{1,0:T(8,128)(2,1)S(1)} %get-tuple-element.23.b0), channel_id=1, source_target_pairs={{16,0},{17,1},{18,2},{19,3},{20,4},{21,5},{22,6},{23,7},{505,8},{5... | collective-permute-start | bytes 2359304 | tf_op jit(solution)/shard_map/ppermute | solution.py:28
  94.8 2.6 %collective-permute-start.4 = (bf16[1536,256]{1,0:T(8,128)(2,1)S(1)}, bf16[1536,256]{1,0:T(8,128)(2,1)}, u32[]{:S(2)}, u32[]{:S(2)}) collective-permute-start(bf16[1536,256]{1,0:T(8,128)(2,1)S(1)} %get-tuple-element.23.b0), channel_id=1, source_target_pairs={{8,0},{9,1},{10,2},{11,3},{12,4},{13,5},{14,6},{15,7},{0,8},{1,9},... | collective-permute-start | bytes 2359304 | tf_op jit(solution)/shard_map/ppermute | solution.py:28
  98.4 9.0 %collective-permute-done.6.b3 = bf16[1536,256]{1,0:T(8,128)(2,1)} collective-permute-done((bf16[1536,256]{1,0:T(8,128)(2,1)S(1)}, bf16[1536,256]{1,0:T(8,128)(2,1)}, u32[]{:S(2)}, u32[]{:S(2)}) %collective-permute-start.6) | collective-permute-done | bytes 786464 | tf_op jit(solution)/shard_map/ppermute | solution.py:28
  107.4 3.9 %collective-permute-done.5.b2 = bf16[1536,256]{1,0:T(8,128)(2,1)} collective-permute-done((bf16[1536,256]{1,0:T(8,128)(2,1)S(1)}, bf16[1536,256]{1,0:T(8,128)(2,1)}, u32[]{:S(2)}, u32[]{:S(2)}) %collective-permute-start.5) | collective-permute-done | bytes 786464 | tf_op jit(solution)/shard_map/ppermute | solution.py:28
  111.3 1.9 %collective-permute-start.7 = (bf16[1536,256]{1,0:T(8,128)(2,1)}, bf16[1536,256]{1,0:T(8,128)(2,1)S(1)}, u32[]{:S(2)}, u32[]{:S(2)}) collective-permute-start(bf16[1536,256]{1,0:T(8,128)(2,1)} %collective-permute-done.5.b2), channel_id=1, source_target_pairs={{8,0},{9,1},{10,2},{11,3},{12,4},{13,5},{14,6},{15,7},{0,8},{1,9},... | collective-permute-start | bytes 2359304 | tf_op jit(solution)/shard_map/ppermute | solution.py:28
  113.2 4.7 %collective-permute-start.8 = (f32[32,384]{1,0:T(8,128)S(1)}, f32[32,384]{1,0:T(8,128)S(1)}, u32[]{:S(2)}, u32[]{:S(2)}) collective-permute-start(f32[32,384]{1,0:T(8,128)S(1)} %reduce_sum.18), channel_id=1, source_target_pairs={{128,0},{129,1},{130,2},{131,3},{132,4},{133,5},{134,6},{135,7},{1... | collective-permute-start | bytes 147464 | tf_op jit(solution)/shard_map/ppermute | solution.py:28
  117.9 5.4 %shard_map.106 = bf16[8,32,1536]{2,1,0:T(8,128)(2,1)} custom-call(s32[92]{0:T(128)S(1)} %get-tuple-element.15.pairs, s32[46]{0:T(128)S(1)} %get-tuple-element.16.rows, bf16[1536,256]{1,0:T(8,128)(2,1)S(1)} %get-tuple-element.23.b0, bf16[1536,256]{1,0:T(8,128)(2,1)} %collective-permute-done.4.b1, bf16[1536,256]{1,0:T(8,128)(2,1)} %collective-permute-done.5.b2, ...), custom_call_target="tpu_custom_call" | custom-call | flops 671088640 | bytes 6291456 | tf_op jit(solution)/shard_map/pallas_call | solution.py:138
  123.2 3.6 %all-to-all-start.3 = ((bf16[8,32,1536]{2,1,0:T(8,128)(2,1)}), bf16[8,32,1536]{2,1,0:T(8,128)(2,1)S(1)}, u32[]{:S(2)}, u32[]{:S(2)}) async-start(bf16[8,32,1536]{2,1,0:T(8,128)(2,1)} %shard_map.106), calls=%async_computation.3 | async-start | bytes 1572864 | tf_op jit(solution)/shard_map/all_to_all | solution.py:289
  127.7 3.0 %collective-permute-start.9 = (f32[32,384]{1,0:T(8,128)S(1)}, f32[32,384]{1,0:T(8,128)S(1)}, u32[]{:S(2)}, u32[]{:S(2)}) collective-permute-start(f32[32,384]{1,0:T(8,128)S(1)} %add.14), channel_id=1, source_target_pairs={{64,0},{65,1},{66,2},{67,3},{68,4},{69,5},{70,6},{71,7},{72,8},{73... | collective-permute-start | bytes 147464 | tf_op jit(solution)/shard_map/ppermute | solution.py:28
  130.7 5.8 %collective-permute-done.9 = f32[32,384]{1,0:T(8,128)S(1)} collective-permute-done((f32[32,384]{1,0:T(8,128)S(1)}, f32[32,384]{1,0:T(8,128)S(1)}, u32[]{:S(2)}, u32[]{:S(2)}) %collective-permute-start.9) | collective-permute-done | bytes 49184 | tf_op jit(solution)/shard_map/ppermute | solution.py:28
  136.5 3.3 %collective-permute-start.10 = (f32[32,384]{1,0:T(8,128)S(1)}, f32[32,384]{1,0:T(8,128)S(1)}, u32[]{:S(2)}, u32[]{:S(2)}) collective-permute-start(f32[32,384]{1,0:T(8,128)S(1)} %add.15), channel_id=1, source_target_pairs={{32,0},{33,1},{34,2},{35,3},{36,4},{37,5},{38,6},{39,7},{40,8},{41... | collective-permute-start | bytes 147464 | tf_op jit(solution)/shard_map/ppermute | solution.py:28
  139.8 2.4 %collective-permute-done.10 = f32[32,384]{1,0:T(8,128)S(1)} collective-permute-done((f32[32,384]{1,0:T(8,128)S(1)}, f32[32,384]{1,0:T(8,128)S(1)}, u32[]{:S(2)}, u32[]{:S(2)}) %collective-permute-start.10) | collective-permute-done | bytes 49184 | tf_op jit(solution)/shard_map/ppermute | solution.py:28
  (23 shorter events, 7.5 us)
Async XLA Ops:
  0.6 25.8 %collective-permute-start.1 = (bf16[256,1536]{1,0:T(8,128)(2,1)}, bf16[256,1536]{1,0:T(8,128)(2,1)S(1)}, u32[]{:S(2)}, u32[]{:S(2)}) collective-permute-start(bf16[256,1536]{1,0:T(8,128)(2,1)} %own.1), channel_id=1, source_target_pairs={{16,0},{17,1},{18,2},{19,3},{20,4},{21,5},{22,6},{23,7},{505,8},{5... | collective-permute-start | bytes 2359304 | tf_op jit(solution)/shard_map/ppermute | solution.py:28
  5.0 26.4 %collective-permute-start = (bf16[256,1536]{1,0:T(8,128)(2,1)}, bf16[256,1536]{1,0:T(8,128)(2,1)}, u32[]{:S(2)}, u32[]{:S(2)}) collective-permute-start(bf16[256,1536]{1,0:T(8,128)(2,1)} %own.1), channel_id=1, source_target_pairs={{8,0},{9,1},{10,2},{11,3},{12,4},{13,5},{14,6},{15,7},{0,8},{1,9},... | collective-permute-start | bytes 2359304 | tf_op jit(solution)/shard_map/ppermute | solution.py:28
  17.7 15.9 %collective-permute-start.2 = (bf16[256,1536]{1,0:T(8,128)(2,1)}, bf16[256,1536]{1,0:T(8,128)(2,1)}, u32[]{:S(2)}, u32[]{:S(2)}) collective-permute-start(bf16[256,1536]{1,0:T(8,128)(2,1)} %own.1), channel_id=1, source_target_pairs={{497,0},{496,1},{499,2},{498,3},{501,4},{500,5},{503,6},{502,7},{2... | collective-permute-start | bytes 2359304 | tf_op jit(solution)/shard_map/ppermute | solution.py:28
  21.1 0.9 copy-start
  22.0 0.7 copy-start.1
  22.6 0.7 copy-start.2
  26.4 7.2 %collective-permute-start.3 = (bf16[256,1536]{1,0:T(8,128)(2,1)S(1)}, bf16[256,1536]{1,0:T(8,128)(2,1)S(1)}, u32[]{:S(2)}, u32[]{:S(2)}) collective-permute-start(bf16[256,1536]{1,0:T(8,128)(2,1)S(1)} %collective-permute-done.1.b2), channel_id=1, source_target_pairs={{8,0},{9,1},{10,2},{11,3},{12,4},{13,5},{14,6},{15,7},{0,8},{1,9},... | collective-permute-start | bytes 2359304 | tf_op jit(solution)/shard_map/ppermute | solution.py:28
  74.8 22.5 %all-to-all-start.2 = ((f32[8,32,384]{2,1,0:T(8,128)}), f32[8,32,384]{2,1,0:T(8,128)}, u32[]{:S(2)}, u32[]{:S(2)}) async-start(f32[8,32,384]{2,1,0:T(8,128)} %get-tuple-element.24), calls=%async_computation.2 | async-start | bytes 786432 | tf_op jit(solution)/shard_map/all_to_all | solution.py:372
  82.6 24.8 %collective-permute-start.6 = (bf16[1536,256]{1,0:T(8,128)(2,1)S(1)}, bf16[1536,256]{1,0:T(8,128)(2,1)}, u32[]{:S(2)}, u32[]{:S(2)}) collective-permute-start(bf16[1536,256]{1,0:T(8,128)(2,1)S(1)} %get-tuple-element.23.b0), channel_id=1, source_target_pairs={{497,0},{496,1},{499,2},{498,3},{501,4},{500,5},{503,6},{502,7},{2... | collective-permute-start | bytes 2359304 | tf_op jit(solution)/shard_map/ppermute | solution.py:28
  92.8 18.4 %collective-permute-start.5 = (bf16[1536,256]{1,0:T(8,128)(2,1)S(1)}, bf16[1536,256]{1,0:T(8,128)(2,1)}, u32[]{:S(2)}, u32[]{:S(2)}) collective-permute-start(bf16[1536,256]{1,0:T(8,128)(2,1)S(1)} %get-tuple-element.23.b0), channel_id=1, source_target_pairs={{16,0},{17,1},{18,2},{19,3},{20,4},{21,5},{22,6},{23,7},{505,8},{5... | collective-permute-start | bytes 2359304 | tf_op jit(solution)/shard_map/ppermute | solution.py:28
  94.8 23.1 %collective-permute-start.4 = (bf16[1536,256]{1,0:T(8,128)(2,1)S(1)}, bf16[1536,256]{1,0:T(8,128)(2,1)}, u32[]{:S(2)}, u32[]{:S(2)}) collective-permute-start(bf16[1536,256]{1,0:T(8,128)(2,1)S(1)} %get-tuple-element.23.b0), channel_id=1, source_target_pairs={{8,0},{9,1},{10,2},{11,3},{12,4},{13,5},{14,6},{15,7},{0,8},{1,9},... | collective-permute-start | bytes 2359304 | tf_op jit(solution)/shard_map/ppermute | solution.py:28
  111.3 6.6 %collective-permute-start.7 = (bf16[1536,256]{1,0:T(8,128)(2,1)}, bf16[1536,256]{1,0:T(8,128)(2,1)S(1)}, u32[]{:S(2)}, u32[]{:S(2)}) collective-permute-start(bf16[1536,256]{1,0:T(8,128)(2,1)} %collective-permute-done.5.b2), channel_id=1, source_target_pairs={{8,0},{9,1},{10,2},{11,3},{12,4},{13,5},{14,6},{15,7},{0,8},{1,9},... | collective-permute-start | bytes 2359304 | tf_op jit(solution)/shard_map/ppermute | solution.py:28
  113.2 14.5 %collective-permute-start.8 = (f32[32,384]{1,0:T(8,128)S(1)}, f32[32,384]{1,0:T(8,128)S(1)}, u32[]{:S(2)}, u32[]{:S(2)}) collective-permute-start(f32[32,384]{1,0:T(8,128)S(1)} %reduce_sum.18), channel_id=1, source_target_pairs={{128,0},{129,1},{130,2},{131,3},{132,4},{133,5},{134,6},{135,7},{1... | collective-permute-start | bytes 147464 | tf_op jit(solution)/shard_map/ppermute | solution.py:28
  123.2 20.2 %all-to-all-start.3 = ((bf16[8,32,1536]{2,1,0:T(8,128)(2,1)}), bf16[8,32,1536]{2,1,0:T(8,128)(2,1)S(1)}, u32[]{:S(2)}, u32[]{:S(2)}) async-start(bf16[8,32,1536]{2,1,0:T(8,128)(2,1)} %shard_map.106), calls=%async_computation.3 | async-start | bytes 1572864 | tf_op jit(solution)/shard_map/all_to_all | solution.py:289
  127.7 8.8 %collective-permute-start.9 = (f32[32,384]{1,0:T(8,128)S(1)}, f32[32,384]{1,0:T(8,128)S(1)}, u32[]{:S(2)}, u32[]{:S(2)}) collective-permute-start(f32[32,384]{1,0:T(8,128)S(1)} %add.14), channel_id=1, source_target_pairs={{64,0},{65,1},{66,2},{67,3},{68,4},{69,5},{70,6},{71,7},{72,8},{73... | collective-permute-start | bytes 147464 | tf_op jit(solution)/shard_map/ppermute | solution.py:28
  136.5 5.7 %collective-permute-start.10 = (f32[32,384]{1,0:T(8,128)S(1)}, f32[32,384]{1,0:T(8,128)S(1)}, u32[]{:S(2)}, u32[]{:S(2)}) collective-permute-start(f32[32,384]{1,0:T(8,128)S(1)} %add.15), channel_id=1, source_target_pairs={{32,0},{33,1},{34,2},{35,3},{36,4},{37,5},{38,6},{39,7},{40,8},{41... | collective-permute-start | bytes 147464 | tf_op jit(solution)/shard_map/ppermute | solution.py:28

commit v8 on v7

--- a/solution.py
+++ b/solution.py
@@ -371,7 +371,7 @@
     half = blks // 2
     far = lax.all_to_all(total, "blk", 0, 0, axis_index_groups=alike(blks, half | 3))
     total = jnp.sum(far, axis=0)
-    three = move(after(one, (total, two)), swap)
+    three = move(one, swap)
     value = aggregate(
         backward_kernel, (back, zero, one, two, three), tiles, slots, (helps, share, nodes)
     )

time: 147 us -> 142 us (0.966)
  waiting for transfers between devices: 24.1 us -> 18.1 us
  starting transfers between devices: 63.6 us -> 65.7 us
    all_to_all x1, starting transfers between devices: 7.77 us -> 14 us  [per_device(): lax.all_to_all(total, 'blk', 0, 0, axis_index_groups=alike(blks, half | 3))]
    ppermute x11, waiting for transfers between devices: 24.1 us -> 18.1 us  [move(): return lax.ppermute(block, AXES, route)]
    ppermute x11, starting transfers between devices: 52.3 us -> 48.2 us  [move(): return lax.ppermute(block, AXES, route)]
  transfers between devices with their start and end apart: 13 -> 13, of which waited for: 6 -> 5; matrix products, arithmetic and copies ran while one was open for 2% -> 2% of each run, Pallas kernels for 6% -> 6%
where the time goes in v8:
time: 142 us; the launch traced here: 141 us
  starting transfers between devices  65.7 us (46%)
  blocking collectives  32 us (23%)
  waiting for transfers between devices  18.1 us (13%)
  Pallas kernels  17.9 us (13%)
  local copies, waits for them, and re-layouts  4.19 us (3%)
  other arithmetic  1.83 us (1%)
    ppermute x11, starting transfers between devices, move(): return lax.ppermute(block, AXES, route)  48.2 us
    all_to_all x2, blocking collectives, spread(): return lax.all_to_all(x, 'help', 0, 0)  32 us
    ppermute x11, waiting for transfers between devices, move(): return lax.ppermute(block, AXES, route)  18.1 us
    all_to_all x1, starting transfers between devices, per_device(): lax.all_to_all(total, 'blk', 0, 0, axis_index_groups=alike(blks, half | 3))  14 us
    pallas_call x2, Pallas kernels, aggregate(): pl.pallas_call(kernel, out_shape=pltpu.HBM(out_shape, jnp.bfloat16), in_s...  11.1 us
    all_to_all x1, starting transfers between devices, spread(): return lax.all_to_all(x, 'help', 0, 0)  3.56 us
    pallas_call x1, Pallas kernels, per_device(): pl.pallas_call(functools.partial(prepare_kernel, row_tiles), out_shape=(j...  3.13 us
    pallas_call x1, Pallas kernels, per_device(): pl.pallas_call(divide_kernel, out_shape=(pltpu.VMEM((nodes, width), jnp.b...  3.09 us
  transfers between devices with their start and end apart: 13, of which 5 were waited for; matrix products, arithmetic and copies ran while one was open for 2% of the time, Pallas kernels for 6%

profile of v8, /device:TPU:1, one launch (start us, length us, event | category | flops | bytes accessed | tf_op | source)
XLA Modules:
  0.0 140.6 jit_solution(5652736053286729084)
XLA Ops:
  0.6 4.4 %collective-permute-start.1 = (bf16[256,1536]{1,0:T(8,128)(2,1)}, bf16[256,1536]{1,0:T(8,128)(2,1)S(1)}, u32[]{:S(2)}, u32[]{:S(2)}) collective-permute-start(bf16[256,1536]{1,0:T(8,128)(2,1)} %own.1), channel_id=1, source_target_pairs={{16,0},{17,1},{18,2},{19,3},{20,4},{21,5},{22,6},{23,7},{505,8},{5... | collective-permute-start | bytes 2359304 | tf_op jit(solution)/shard_map/ppermute | solution.py:28
  5.0 12.6 %collective-permute-start = (bf16[256,1536]{1,0:T(8,128)(2,1)}, bf16[256,1536]{1,0:T(8,128)(2,1)}, u32[]{:S(2)}, u32[]{:S(2)}) collective-permute-start(bf16[256,1536]{1,0:T(8,128)(2,1)} %own.1), channel_id=1, source_target_pairs={{8,0},{9,1},{10,2},{11,3},{12,4},{13,5},{14,6},{15,7},{0,8},{1,9},... | collective-permute-start | bytes 2359304 | tf_op jit(solution)/shard_map/ppermute | solution.py:28
  17.7 2.6 %collective-permute-start.2 = (bf16[256,1536]{1,0:T(8,128)(2,1)}, bf16[256,1536]{1,0:T(8,128)(2,1)}, u32[]{:S(2)}, u32[]{:S(2)}) collective-permute-start(bf16[256,1536]{1,0:T(8,128)(2,1)} %own.1), channel_id=1, source_target_pairs={{497,0},{496,1},{499,2},{498,3},{501,4},{500,5},{503,6},{502,7},{2... | collective-permute-start | bytes 2359304 | tf_op jit(solution)/shard_map/ppermute | solution.py:28
  23.3 3.1 %shard_map.102 = (s32[92]{0:T(128)S(1)}, s32[46]{0:T(128)S(1)}, bf16[8,32,256]{2,1,0:T(8,128)(2,1)S(1)}, bf16[256,256]{1,0:T(8,128)(2,1)S(1)}, bf16[80,128,128]{...) custom-call(s32[1]{0:T(128)} %bitcast.odd, s32[80]{0:T(128)S(1)} %bitcast.7, s32[80]{0:T(128)S(1)} %bitcast.8, ...), custom_call_target="tpu_custom_call" | custom-call | tf_op jit(solution)/shard_map/pallas_call | solution.py:310
  26.4 5.0 %collective-permute-start.3 = (bf16[256,1536]{1,0:T(8,128)(2,1)S(1)}, bf16[256,1536]{1,0:T(8,128)(2,1)S(1)}, u32[]{:S(2)}, u32[]{:S(2)}) collective-permute-start(bf16[256,1536]{1,0:T(8,128)(2,1)S(1)} %collective-permute-done.1.b2), channel_id=1, source_target_pairs={{8,0},{9,1},{10,2},{11,3},{12,4},{13,5},{14,6},{15,7},{0,8},{1,9},... | collective-permute-start | bytes 2359304 | tf_op jit(solution)/shard_map/ppermute | solution.py:28
  31.4 2.1 %collective-permute-done.2.b3 = bf16[256,1536]{1,0:T(8,128)(2,1)} collective-permute-done((bf16[256,1536]{1,0:T(8,128)(2,1)}, bf16[256,1536]{1,0:T(8,128)(2,1)}, u32[]{:S(2)}, u32[]{:S(2)}) %collective-permute-start.2) | collective-permute-done | bytes 786464 | tf_op jit(solution)/shard_map/ppermute | solution.py:28
  33.6 5.5 %shard_map.103 = bf16[8,224,256]{2,1,0:T(8,128)(2,1)} custom-call(s32[92]{0:T(128)S(1)} %get-tuple-element.14.pairs, s32[46]{0:T(128)S(1)} %get-tuple-element.15.rows, bf16[256,1536]{1,0:T(8,128)(2,1)S(1)} %get-tuple-element.16.b0, bf16[256,1536]{1,0:T(8,128)(2,1)} %collective-permute-done.b1, bf16[256,1536]{1,0:T(8,128)(2,1)S(1)} %collective-permute-done.1.b2, ...), custom_call_target="tpu_custom_call" | custom-call | flops 671088640 | bytes 6291456 | tf_op jit(solution)/shard_map/pallas_call | solution.py:138
  39.1 16.6 %all_to_all.20.parts = bf16[8,224,256]{2,1,0:T(8,128)(2,1)S(1)} all-to-all(bf16[8,224,256]{2,1,0:T(8,128)(2,1)} %shard_map.103), channel_id=1, replica_groups=mesh['blk'=64,'help'=8] {'help'}, dimensions={0} | all-to-all | bytes 1835008 | tf_op jit(solution)/shard_map/all_to_all | solution.py:289
  56.3 15.4 %all_to_all.21.parts = bf16[8,256,256]{2,1,0:T(8,128)(2,1)S(1)} all-to-all(bf16[8,256,256]{2,1,0:T(8,128)(2,1)S(1)} %shard_map.104), channel_id=1, replica_groups=mesh['blk'=64,'help'=8] {'help'}, dimensions={0} | all-to-all | bytes 2097152 | tf_op jit(solution)/shard_map/all_to_all | solution.py:289
  71.7 3.1 %shard_map.105 = (bf16[1536,256]{1,0:T(8,128)(2,1)S(1)}, bf16[32,1536]{1,0:T(8,128)(2,1)}, f32[8,32,384]{2,1,0:T(8,128)}) custom-call(bf16[8,256,256]{2,1,0:T(8,128)(2,1)S(1)} %all_to_all.21.parts), custom_call_target="tpu_custom_call" | custom-call | tf_op jit(solution)/shard_map/pallas_call | solution.py:354
  74.8 3.0 %collective-permute-start.5 = (bf16[1536,256]{1,0:T(8,128)(2,1)S(1)}, bf16[1536,256]{1,0:T(8,128)(2,1)}, u32[]{:S(2)}, u32[]{:S(2)}) collective-permute-start(bf16[1536,256]{1,0:T(8,128)(2,1)S(1)} %get-tuple-element.22.b0), channel_id=1, source_target_pairs={{16,0},{17,1},{18,2},{19,3},{20,4},{21,5},{22,6},{23,7},{505,8},{5... | collective-permute-start | bytes 2359304 | tf_op jit(solution)/shard_map/ppermute | solution.py:28
  77.8 14.0 %all-to-all-start.3 = ((f32[8,32,384]{2,1,0:T(8,128)}), f32[8,32,384]{2,1,0:T(8,128)}, u32[]{:S(2)}, u32[]{:S(2)}) async-start(f32[8,32,384]{2,1,0:T(8,128)} %get-tuple-element.23), calls=%async_computation.3 | async-start | bytes 786432 | tf_op jit(solution)/shard_map/all_to_all | solution.py:372
  91.7 3.0 %collective-permute-start.6 = (bf16[1536,256]{1,0:T(8,128)(2,1)S(1)}, bf16[1536,256]{1,0:T(8,128)(2,1)}, u32[]{:S(2)}, u32[]{:S(2)}) collective-permute-start(bf16[1536,256]{1,0:T(8,128)(2,1)S(1)} %get-tuple-element.22.b0), channel_id=1, source_target_pairs={{497,0},{496,1},{499,2},{498,3},{501,4},{500,5},{503,6},{502,7},{2... | collective-permute-start | bytes 2359304 | tf_op jit(solution)/shard_map/ppermute | solution.py:28
  94.7 2.8 %collective-permute-start.4 = (bf16[1536,256]{1,0:T(8,128)(2,1)S(1)}, bf16[1536,256]{1,0:T(8,128)(2,1)}, u32[]{:S(2)}, u32[]{:S(2)}) collective-permute-start(bf16[1536,256]{1,0:T(8,128)(2,1)S(1)} %get-tuple-element.22.b0), channel_id=1, source_target_pairs={{8,0},{9,1},{10,2},{11,3},{12,4},{13,5},{14,6},{15,7},{0,8},{1,9},... | collective-permute-start | bytes 2359304 | tf_op jit(solution)/shard_map/ppermute | solution.py:28
  97.6 8.9 %collective-permute-start.7 = (bf16[1536,256]{1,0:T(8,128)(2,1)}, bf16[1536,256]{1,0:T(8,128)(2,1)}, u32[]{:S(2)}, u32[]{:S(2)}) collective-permute-start(bf16[1536,256]{1,0:T(8,128)(2,1)} %collective-permute-done.5.b2), channel_id=1, source_target_pairs={{8,0},{9,1},{10,2},{11,3},{12,4},{13,5},{14,6},{15,7},{0,8},{1,9},... | collective-permute-start | bytes 2359304 | tf_op jit(solution)/shard_map/ppermute | solution.py:28
  106.6 1.0 reduce_sum.19
  107.6 1.9 %collective-permute-start.8 = (f32[32,384]{1,0:T(8,128)S(1)}, f32[32,384]{1,0:T(8,128)S(1)}, u32[]{:S(2)}, u32[]{:S(2)}) collective-permute-start(f32[32,384]{1,0:T(8,128)S(1)} %reduce_sum.19), channel_id=1, source_target_pairs={{128,0},{129,1},{130,2},{131,3},{132,4},{133,5},{134,6},{135,7},{1... | collective-permute-start | bytes 147464 | tf_op jit(solution)/shard_map/ppermute | solution.py:28
  109.5 3.1 %collective-permute-done.6.b3 = bf16[1536,256]{1,0:T(8,128)(2,1)} collective-permute-done((bf16[1536,256]{1,0:T(8,128)(2,1)S(1)}, bf16[1536,256]{1,0:T(8,128)(2,1)}, u32[]{:S(2)}, u32[]{:S(2)}) %collective-permute-start.6) | collective-permute-done | bytes 786464 | tf_op jit(solution)/shard_map/ppermute | solution.py:28
  112.6 5.6 %shard_map.106 = bf16[8,32,1536]{2,1,0:T(8,128)(2,1)} custom-call(s32[92]{0:T(128)S(1)} %get-tuple-element.14.pairs, s32[46]{0:T(128)S(1)} %get-tuple-element.15.rows, bf16[1536,256]{1,0:T(8,128)(2,1)S(1)} %get-tuple-element.22.b0, bf16[1536,256]{1,0:T(8,128)(2,1)} %collective-permute-done.4.b1, bf16[1536,256]{1,0:T(8,128)(2,1)} %collective-permute-done.5.b2, ...), custom_call_target="tpu_custom_call" | custom-call | flops 671088640 | bytes 6291456 | tf_op jit(solution)/shard_map/pallas_call | solution.py:138
  118.2 3.6 %all-to-all-start.2 = ((bf16[8,32,1536]{2,1,0:T(8,128)(2,1)}), bf16[8,32,1536]{2,1,0:T(8,128)(2,1)S(1)}, u32[]{:S(2)}, u32[]{:S(2)}) async-start(bf16[8,32,1536]{2,1,0:T(8,128)(2,1)} %shard_map.106), calls=%async_computation.2 | async-start | bytes 1572864 | tf_op jit(solution)/shard_map/all_to_all | solution.py:289
  122.0 1.9 %collective-permute-start.9 = (f32[32,384]{1,0:T(8,128)S(1)}, f32[32,384]{1,0:T(8,128)S(1)}, u32[]{:S(2)}, u32[]{:S(2)}) collective-permute-start(f32[32,384]{1,0:T(8,128)S(1)} %add.14), channel_id=1, source_target_pairs={{64,0},{65,1},{66,2},{67,3},{68,4},{69,5},{70,6},{71,7},{72,8},{73... | collective-permute-start | bytes 147464 | tf_op jit(solution)/shard_map/ppermute | solution.py:28
  123.9 8.9 %collective-permute-done.9 = f32[32,384]{1,0:T(8,128)S(1)} collective-permute-done((f32[32,384]{1,0:T(8,128)S(1)}, f32[32,384]{1,0:T(8,128)S(1)}, u32[]{:S(2)}, u32[]{:S(2)}) %collective-permute-start.9) | collective-permute-done | bytes 49184 | tf_op jit(solution)/shard_map/ppermute | solution.py:28
  132.8 1.9 %collective-permute-start.10 = (f32[32,384]{1,0:T(8,128)S(1)}, f32[32,384]{1,0:T(8,128)S(1)}, u32[]{:S(2)}, u32[]{:S(2)}) collective-permute-start(f32[32,384]{1,0:T(8,128)S(1)} %add.15), channel_id=1, source_target_pairs={{32,0},{33,1},{34,2},{35,3},{36,4},{37,5},{38,6},{39,7},{40,8},{41... | collective-permute-start | bytes 147464 | tf_op jit(solution)/shard_map/ppermute | solution.py:28
  134.7 3.8 %collective-permute-done.10 = f32[32,384]{1,0:T(8,128)S(1)} collective-permute-done((f32[32,384]{1,0:T(8,128)S(1)}, f32[32,384]{1,0:T(8,128)S(1)}, u32[]{:S(2)}, u32[]{:S(2)}) %collective-permute-start.10) | collective-permute-done | bytes 49184 | tf_op jit(solution)/shard_map/ppermute | solution.py:28
  (23 shorter events, 5.8 us)
Async XLA Ops:
  0.6 25.8 %collective-permute-start.1 = (bf16[256,1536]{1,0:T(8,128)(2,1)}, bf16[256,1536]{1,0:T(8,128)(2,1)S(1)}, u32[]{:S(2)}, u32[]{:S(2)}) collective-permute-start(bf16[256,1536]{1,0:T(8,128)(2,1)} %own.1), channel_id=1, source_target_pairs={{16,0},{17,1},{18,2},{19,3},{20,4},{21,5},{22,6},{23,7},{505,8},{5... | collective-permute-start | bytes 2359304 | tf_op jit(solution)/shard_map/ppermute | solution.py:28
  5.0 26.4 %collective-permute-start = (bf16[256,1536]{1,0:T(8,128)(2,1)}, bf16[256,1536]{1,0:T(8,128)(2,1)}, u32[]{:S(2)}, u32[]{:S(2)}) collective-permute-start(bf16[256,1536]{1,0:T(8,128)(2,1)} %own.1), channel_id=1, source_target_pairs={{8,0},{9,1},{10,2},{11,3},{12,4},{13,5},{14,6},{15,7},{0,8},{1,9},... | collective-permute-start | bytes 2359304 | tf_op jit(solution)/shard_map/ppermute | solution.py:28
  17.7 15.9 %collective-permute-start.2 = (bf16[256,1536]{1,0:T(8,128)(2,1)}, bf16[256,1536]{1,0:T(8,128)(2,1)}, u32[]{:S(2)}, u32[]{:S(2)}) collective-permute-start(bf16[256,1536]{1,0:T(8,128)(2,1)} %own.1), channel_id=1, source_target_pairs={{497,0},{496,1},{499,2},{498,3},{501,4},{500,5},{503,6},{502,7},{2... | collective-permute-start | bytes 2359304 | tf_op jit(solution)/shard_map/ppermute | solution.py:28
  21.1 0.9 copy-start
  22.0 0.7 copy-start.1
  22.6 0.7 copy-start.2
  26.4 7.2 %collective-permute-start.3 = (bf16[256,1536]{1,0:T(8,128)(2,1)S(1)}, bf16[256,1536]{1,0:T(8,128)(2,1)S(1)}, u32[]{:S(2)}, u32[]{:S(2)}) collective-permute-start(bf16[256,1536]{1,0:T(8,128)(2,1)S(1)} %collective-permute-done.1.b2), channel_id=1, source_target_pairs={{8,0},{9,1},{10,2},{11,3},{12,4},{13,5},{14,6},{15,7},{0,8},{1,9},... | collective-permute-start | bytes 2359304 | tf_op jit(solution)/shard_map/ppermute | solution.py:28
  74.8 22.8 %collective-permute-start.5 = (bf16[1536,256]{1,0:T(8,128)(2,1)S(1)}, bf16[1536,256]{1,0:T(8,128)(2,1)}, u32[]{:S(2)}, u32[]{:S(2)}) collective-permute-start(bf16[1536,256]{1,0:T(8,128)(2,1)S(1)} %get-tuple-element.22.b0), channel_id=1, source_target_pairs={{16,0},{17,1},{18,2},{19,3},{20,4},{21,5},{22,6},{23,7},{505,8},{5... | collective-permute-start | bytes 2359304 | tf_op jit(solution)/shard_map/ppermute | solution.py:28
  77.8 28.8 %all-to-all-start.3 = ((f32[8,32,384]{2,1,0:T(8,128)}), f32[8,32,384]{2,1,0:T(8,128)}, u32[]{:S(2)}, u32[]{:S(2)}) async-start(f32[8,32,384]{2,1,0:T(8,128)} %get-tuple-element.23), calls=%async_computation.3 | async-start | bytes 786432 | tf_op jit(solution)/shard_map/all_to_all | solution.py:372
  91.7 20.9 %collective-permute-start.6 = (bf16[1536,256]{1,0:T(8,128)(2,1)S(1)}, bf16[1536,256]{1,0:T(8,128)(2,1)}, u32[]{:S(2)}, u32[]{:S(2)}) collective-permute-start(bf16[1536,256]{1,0:T(8,128)(2,1)S(1)} %get-tuple-element.22.b0), channel_id=1, source_target_pairs={{497,0},{496,1},{499,2},{498,3},{501,4},{500,5},{503,6},{502,7},{2... | collective-permute-start | bytes 2359304 | tf_op jit(solution)/shard_map/ppermute | solution.py:28
  94.7 17.8 %collective-permute-start.4 = (bf16[1536,256]{1,0:T(8,128)(2,1)S(1)}, bf16[1536,256]{1,0:T(8,128)(2,1)}, u32[]{:S(2)}, u32[]{:S(2)}) collective-permute-start(bf16[1536,256]{1,0:T(8,128)(2,1)S(1)} %get-tuple-element.22.b0), channel_id=1, source_target_pairs={{8,0},{9,1},{10,2},{11,3},{12,4},{13,5},{14,6},{15,7},{0,8},{1,9},... | collective-permute-start | bytes 2359304 | tf_op jit(solution)/shard_map/ppermute | solution.py:28
  97.6 15.0 %collective-permute-start.7 = (bf16[1536,256]{1,0:T(8,128)(2,1)}, bf16[1536,256]{1,0:T(8,128)(2,1)}, u32[]{:S(2)}, u32[]{:S(2)}) collective-permute-start(bf16[1536,256]{1,0:T(8,128)(2,1)} %collective-permute-done.5.b2), channel_id=1, source_target_pairs={{8,0},{9,1},{10,2},{11,3},{12,4},{13,5},{14,6},{15,7},{0,8},{1,9},... | collective-permute-start | bytes 2359304 | tf_op jit(solution)/shard_map/ppermute | solution.py:28
  107.6 14.4 %collective-permute-start.8 = (f32[32,384]{1,0:T(8,128)S(1)}, f32[32,384]{1,0:T(8,128)S(1)}, u32[]{:S(2)}, u32[]{:S(2)}) collective-permute-start(f32[32,384]{1,0:T(8,128)S(1)} %reduce_sum.19), channel_id=1, source_target_pairs={{128,0},{129,1},{130,2},{131,3},{132,4},{133,5},{134,6},{135,7},{1... | collective-permute-start | bytes 147464 | tf_op jit(solution)/shard_map/ppermute | solution.py:28
  118.2 21.6 %all-to-all-start.2 = ((bf16[8,32,1536]{2,1,0:T(8,128)(2,1)}), bf16[8,32,1536]{2,1,0:T(8,128)(2,1)S(1)}, u32[]{:S(2)}, u32[]{:S(2)}) async-start(bf16[8,32,1536]{2,1,0:T(8,128)(2,1)} %shard_map.106), calls=%async_computation.2 | async-start | bytes 1572864 | tf_op jit(solution)/shard_map/all_to_all | solution.py:289
  122.0 10.8 %collective-permute-start.9 = (f32[32,384]{1,0:T(8,128)S(1)}, f32[32,384]{1,0:T(8,128)S(1)}, u32[]{:S(2)}, u32[]{:S(2)}) collective-permute-start(f32[32,384]{1,0:T(8,128)S(1)} %add.14), channel_id=1, source_target_pairs={{64,0},{65,1},{66,2},{67,3},{68,4},{69,5},{70,6},{71,7},{72,8},{73... | collective-permute-start | bytes 147464 | tf_op jit(solution)/shard_map/ppermute | solution.py:28
  132.8 5.7 %collective-permute-start.10 = (f32[32,384]{1,0:T(8,128)S(1)}, f32[32,384]{1,0:T(8,128)S(1)}, u32[]{:S(2)}, u32[]{:S(2)}) collective-permute-start(f32[32,384]{1,0:T(8,128)S(1)} %add.15), channel_id=1, source_target_pairs={{32,0},{33,1},{34,2},{35,3},{36,4},{37,5},{38,6},{39,7},{40,8},{41... | collective-permute-start | bytes 147464 | tf_op jit(solution)/shard_map/ppermute | solution.py:28

commit v9 on v8

--- a/solution.py
+++ b/solution.py
@@ -376,8 +376,9 @@
         backward_kernel, (back, zero, one, two, three), tiles, slots, (helps, share, nodes)
     )
     propagated = jnp.sum(spread(value).astype(jnp.float32), axis=0)
-    for step in (16, 8, 4):
-        total = total + move(total, functools.partial(lambda s, b, h: (b ^ s, h), step))
+    flip = lambda s: functools.partial(lambda s, b, h: (b ^ s, h), s)
+    total = (total + move(total, flip(4))) + (move(total, flip(8)) + move(total, flip(12)))
+    total = total + move(total, flip(16))
     total = total * (1.0 / math.sqrt(nodes * blks))
     return (output, propagated, total[:, :width].T, total[:, width])
 

time: 142 us -> 149 us (1.049)
  starting transfers between devices: 65.7 us -> 75 us
  waiting for transfers between devices: 18.1 us -> 13.8 us
    ppermute x11 -> x12, starting transfers between devices: 48.2 us -> 57.1 us  [move(): return lax.ppermute(block, AXES, route)]
    ppermute x11 -> x12, waiting for transfers between devices: 18.1 us -> 13.8 us  [move(): return lax.ppermute(block, AXES, route)]
  transfers between devices with their start and end apart: 13 -> 14, of which waited for: 5 -> 2; matrix products, arithmetic and copies ran while one was open for 2% -> 3% of each run, Pallas kernels for 6% -> 6%
where the time goes in v9:
time: 149 us; the launch traced here: 146 us
  starting transfers between devices  75 us (50%)
  blocking collectives  32 us (21%)
  Pallas kernels  17.8 us (12%)
  waiting for transfers between devices  13.8 us (9%)
  local copies, waits for them, and re-layouts  4.19 us (3%)
  other arithmetic  2.66 us (2%)
    ppermute x12, starting transfers between devices, move(): return lax.ppermute(block, AXES, route)  57.1 us
    all_to_all x2, blocking collectives, spread(): return lax.all_to_all(x, 'help', 0, 0)  32 us
    all_to_all x1, starting transfers between devices, per_device(): lax.all_to_all(total, 'blk', 0, 0, axis_index_groups=alike(blks, half | 3))  14.4 us
    ppermute x12, waiting for transfers between devices, move(): return lax.ppermute(block, AXES, route)  13.8 us
    pallas_call x2, Pallas kernels, aggregate(): pl.pallas_call(kernel, out_shape=pltpu.HBM(out_shape, jnp.bfloat16), in_s...  11 us
    all_to_all x1, starting transfers between devices, spread(): return lax.all_to_all(x, 'help', 0, 0)  3.56 us
    pallas_call x1, Pallas kernels, per_device(): pl.pallas_call(functools.partial(prepare_kernel, row_tiles), out_shape=(j...  3.13 us
    pallas_call x1, Pallas kernels, per_device(): pl.pallas_call(divide_kernel, out_shape=(pltpu.VMEM((nodes, width), jnp.b...  3.08 us
  transfers between devices with their start and end apart: 14, of which 2 were waited for; matrix products, arithmetic and copies ran while one was open for 3% of the time, Pallas kernels for 6%

profile of v9, /device:TPU:1, one launch (start us, length us, event | category | flops | bytes accessed | tf_op | source)
XLA Modules:
  0.0 146.4 jit_solution(3881846204914824689)
XLA Ops:
  0.6 4.4 %collective-permute-start.1 = (bf16[256,1536]{1,0:T(8,128)(2,1)}, bf16[256,1536]{1,0:T(8,128)(2,1)S(1)}, u32[]{:S(2)}, u32[]{:S(2)}) collective-permute-start(bf16[256,1536]{1,0:T(8,128)(2,1)} %own.1), channel_id=1, source_target_pairs={{16,0},{17,1},{18,2},{19,3},{20,4},{21,5},{22,6},{23,7},{505,8},{5... | collective-permute-start | bytes 2359304 | tf_op jit(solution)/shard_map/ppermute | solution.py:28
  5.0 12.6 %collective-permute-start = (bf16[256,1536]{1,0:T(8,128)(2,1)}, bf16[256,1536]{1,0:T(8,128)(2,1)}, u32[]{:S(2)}, u32[]{:S(2)}) collective-permute-start(bf16[256,1536]{1,0:T(8,128)(2,1)} %own.1), channel_id=1, source_target_pairs={{8,0},{9,1},{10,2},{11,3},{12,4},{13,5},{14,6},{15,7},{0,8},{1,9},... | collective-permute-start | bytes 2359304 | tf_op jit(solution)/shard_map/ppermute | solution.py:28
  17.7 2.6 %collective-permute-start.2 = (bf16[256,1536]{1,0:T(8,128)(2,1)}, bf16[256,1536]{1,0:T(8,128)(2,1)}, u32[]{:S(2)}, u32[]{:S(2)}) collective-permute-start(bf16[256,1536]{1,0:T(8,128)(2,1)} %own.1), channel_id=1, source_target_pairs={{497,0},{496,1},{499,2},{498,3},{501,4},{500,5},{503,6},{502,7},{2... | collective-permute-start | bytes 2359304 | tf_op jit(solution)/shard_map/ppermute | solution.py:28
  21.1 0.9 copy-done
  23.3 3.1 %shard_map.102 = (s32[92]{0:T(128)S(1)}, s32[46]{0:T(128)S(1)}, bf16[8,32,256]{2,1,0:T(8,128)(2,1)S(1)}, bf16[256,256]{1,0:T(8,128)(2,1)S(1)}, bf16[80,128,128]{...) custom-call(s32[1]{0:T(128)} %bitcast.odd, s32[80]{0:T(128)S(1)} %bitcast.7, s32[80]{0:T(128)S(1)} %bitcast.8, ...), custom_call_target="tpu_custom_call" | custom-call | tf_op jit(solution)/shard_map/pallas_call | solution.py:310
  26.4 5.0 %collective-permute-start.3 = (bf16[256,1536]{1,0:T(8,128)(2,1)S(1)}, bf16[256,1536]{1,0:T(8,128)(2,1)S(1)}, u32[]{:S(2)}, u32[]{:S(2)}) collective-permute-start(bf16[256,1536]{1,0:T(8,128)(2,1)S(1)} %collective-permute-done.1.b2), channel_id=1, source_target_pairs={{8,0},{9,1},{10,2},{11,3},{12,4},{13,5},{14,6},{15,7},{0,8},{1,9},... | collective-permute-start | bytes 2359304 | tf_op jit(solution)/shard_map/ppermute | solution.py:28
  31.4 2.1 %collective-permute-done.2.b3 = bf16[256,1536]{1,0:T(8,128)(2,1)} collective-permute-done((bf16[256,1536]{1,0:T(8,128)(2,1)}, bf16[256,1536]{1,0:T(8,128)(2,1)}, u32[]{:S(2)}, u32[]{:S(2)}) %collective-permute-start.2) | collective-permute-done | bytes 786464 | tf_op jit(solution)/shard_map/ppermute | solution.py:28
  33.6 5.4 %shard_map.103 = bf16[8,224,256]{2,1,0:T(8,128)(2,1)} custom-call(s32[92]{0:T(128)S(1)} %get-tuple-element.14.pairs, s32[46]{0:T(128)S(1)} %get-tuple-element.15.rows, bf16[256,1536]{1,0:T(8,128)(2,1)S(1)} %get-tuple-element.16.b0, bf16[256,1536]{1,0:T(8,128)(2,1)} %collective-permute-done.b1, bf16[256,1536]{1,0:T(8,128)(2,1)S(1)} %collective-permute-done.1.b2, ...), custom_call_target="tpu_custom_call" | custom-call | flops 671088640 | bytes 6291456 | tf_op jit(solution)/shard_map/pallas_call | solution.py:138
  39.0 16.6 %all_to_all.20.parts = bf16[8,224,256]{2,1,0:T(8,128)(2,1)S(1)} all-to-all(bf16[8,224,256]{2,1,0:T(8,128)(2,1)} %shard_map.103), channel_id=1, replica_groups=mesh['blk'=64,'help'=8] {'help'}, dimensions={0} | all-to-all | bytes 1835008 | tf_op jit(solution)/shard_map/all_to_all | solution.py:289
  56.3 15.4 %all_to_all.21.parts = bf16[8,256,256]{2,1,0:T(8,128)(2,1)S(1)} all-to-all(bf16[8,256,256]{2,1,0:T(8,128)(2,1)S(1)} %shard_map.104), channel_id=1, replica_groups=mesh['blk'=64,'help'=8] {'help'}, dimensions={0} | all-to-all | bytes 2097152 | tf_op jit(solution)/shard_map/all_to_all | solution.py:289
  71.6 3.1 %shard_map.105 = (bf16[1536,256]{1,0:T(8,128)(2,1)S(1)}, bf16[32,1536]{1,0:T(8,128)(2,1)}, f32[8,32,384]{2,1,0:T(8,128)}) custom-call(bf16[8,256,256]{2,1,0:T(8,128)(2,1)S(1)} %all_to_all.21.parts), custom_call_target="tpu_custom_call" | custom-call | tf_op jit(solution)/shard_map/pallas_call | solution.py:354
  74.7 2.6 %collective-permute-start.5 = (bf16[1536,256]{1,0:T(8,128)(2,1)S(1)}, bf16[1536,256]{1,0:T(8,128)(2,1)}, u32[]{:S(2)}, u32[]{:S(2)}) collective-permute-start(bf16[1536,256]{1,0:T(8,128)(2,1)S(1)} %get-tuple-element.22.b0), channel_id=1, source_target_pairs={{16,0},{17,1},{18,2},{19,3},{20,4},{21,5},{22,6},{23,7},{505,8},{5... | collective-permute-start | bytes 2359304 | tf_op jit(solution)/shard_map/ppermute | solution.py:28
  77.3 14.4 %all-to-all-start.3 = ((f32[8,32,384]{2,1,0:T(8,128)}), f32[8,32,384]{2,1,0:T(8,128)}, u32[]{:S(2)}, u32[]{:S(2)}) async-start(f32[8,32,384]{2,1,0:T(8,128)} %get-tuple-element.23), calls=%async_computation.3 | async-start | bytes 786432 | tf_op jit(solution)/shard_map/all_to_all | solution.py:372
  91.7 3.0 %collective-permute-start.6 = (bf16[1536,256]{1,0:T(8,128)(2,1)S(1)}, bf16[1536,256]{1,0:T(8,128)(2,1)}, u32[]{:S(2)}, u32[]{:S(2)}) collective-permute-start(bf16[1536,256]{1,0:T(8,128)(2,1)S(1)} %get-tuple-element.22.b0), channel_id=1, source_target_pairs={{497,0},{496,1},{499,2},{498,3},{501,4},{500,5},{503,6},{502,7},{2... | collective-permute-start | bytes 2359304 | tf_op jit(solution)/shard_map/ppermute | solution.py:28
  94.7 2.8 %collective-permute-start.4 = (bf16[1536,256]{1,0:T(8,128)(2,1)S(1)}, bf16[1536,256]{1,0:T(8,128)(2,1)}, u32[]{:S(2)}, u32[]{:S(2)}) collective-permute-start(bf16[1536,256]{1,0:T(8,128)(2,1)S(1)} %get-tuple-element.22.b0), channel_id=1, source_target_pairs={{8,0},{9,1},{10,2},{11,3},{12,4},{13,5},{14,6},{15,7},{0,8},{1,9},... | collective-permute-start | bytes 2359304 | tf_op jit(solution)/shard_map/ppermute | solution.py:28
  97.6 8.9 %collective-permute-start.7 = (bf16[1536,256]{1,0:T(8,128)(2,1)}, bf16[1536,256]{1,0:T(8,128)(2,1)}, u32[]{:S(2)}, u32[]{:S(2)}) collective-permute-start(bf16[1536,256]{1,0:T(8,128)(2,1)} %collective-permute-done.5.b2), channel_id=1, source_target_pairs={{8,0},{9,1},{10,2},{11,3},{12,4},{13,5},{14,6},{15,7},{0,8},{1,9},... | collective-permute-start | bytes 2359304 | tf_op jit(solution)/shard_map/ppermute | solution.py:28
  106.5 1.0 reduce_sum.19
  107.6 1.9 %collective-permute-start.10 = (f32[32,384]{1,0:T(8,128)S(1)}, f32[32,384]{1,0:T(8,128)S(1)}, u32[]{:S(2)}, u32[]{:S(2)}) collective-permute-start(f32[32,384]{1,0:T(8,128)S(1)} %reduce_sum.19), channel_id=1, source_target_pairs={{96,0},{97,1},{98,2},{99,3},{100,4},{101,5},{102,6},{103,7},{104,8... | collective-permute-start | bytes 147464 | tf_op jit(solution)/shard_map/ppermute | solution.py:28
  109.5 1.9 %collective-permute-start.9 = (f32[32,384]{1,0:T(8,128)S(1)}, f32[32,384]{1,0:T(8,128)}, u32[]{:S(2)}, u32[]{:S(2)}) collective-permute-start(f32[32,384]{1,0:T(8,128)S(1)} %reduce_sum.19), channel_id=1, source_target_pairs={{64,0},{65,1},{66,2},{67,3},{68,4},{69,5},{70,6},{71,7},{72,8},{73... | collective-permute-start | bytes 147464 | tf_op jit(solution)/shard_map/ppermute | solution.py:28
  111.4 9.3 %collective-permute-start.8 = (f32[32,384]{1,0:T(8,128)S(1)}, f32[32,384]{1,0:T(8,128)}, u32[]{:S(2)}, u32[]{:S(2)}) collective-permute-start(f32[32,384]{1,0:T(8,128)S(1)} %reduce_sum.19), channel_id=1, source_target_pairs={{32,0},{33,1},{34,2},{35,3},{36,4},{37,5},{38,6},{39,7},{40,8},{41... | collective-permute-start | bytes 147464 | tf_op jit(solution)/shard_map/ppermute | solution.py:28
  120.8 5.6 %shard_map.106 = bf16[8,32,1536]{2,1,0:T(8,128)(2,1)} custom-call(s32[92]{0:T(128)S(1)} %get-tuple-element.14.pairs, s32[46]{0:T(128)S(1)} %get-tuple-element.15.rows, bf16[1536,256]{1,0:T(8,128)(2,1)S(1)} %get-tuple-element.22.b0, bf16[1536,256]{1,0:T(8,128)(2,1)} %collective-permute-done.4.b1, bf16[1536,256]{1,0:T(8,128)(2,1)} %collective-permute-done.5.b2, ...), custom_call_target="tpu_custom_call" | custom-call | flops 671088640 | bytes 6291456 | tf_op jit(solution)/shard_map/pallas_call | solution.py:138
  126.4 3.6 %all-to-all-start.2 = ((bf16[8,32,1536]{2,1,0:T(8,128)(2,1)}), bf16[8,32,1536]{2,1,0:T(8,128)(2,1)S(1)}, u32[]{:S(2)}, u32[]{:S(2)}) async-start(bf16[8,32,1536]{2,1,0:T(8,128)(2,1)} %shard_map.106), calls=%async_computation.2 | async-start | bytes 1572864 | tf_op jit(solution)/shard_map/all_to_all | solution.py:289
  130.8 1.9 %collective-permute-start.11 = (f32[32,384]{1,0:T(8,128)S(1)}, f32[32,384]{1,0:T(8,128)S(1)}, u32[]{:S(2)}, u32[]{:S(2)}) collective-permute-start(f32[32,384]{1,0:T(8,128)S(1)} %add_add_fusion), channel_id=1, source_target_pairs={{128,0},{129,1},{130,2},{131,3},{132,4},{133,5},{134,6},{135,7},{1... | collective-permute-start | bytes 147464 | tf_op jit(solution)/shard_map/ppermute | solution.py:28
  132.8 11.6 %collective-permute-done.11 = f32[32,384]{1,0:T(8,128)S(1)} collective-permute-done((f32[32,384]{1,0:T(8,128)S(1)}, f32[32,384]{1,0:T(8,128)S(1)}, u32[]{:S(2)}, u32[]{:S(2)}) %collective-permute-start.11) | collective-permute-done | bytes 49184 | tf_op jit(solution)/shard_map/ppermute | solution.py:28
  (24 shorter events, 5.5 us)
Async XLA Ops:
  0.6 25.8 %collective-permute-start.1 = (bf16[256,1536]{1,0:T(8,128)(2,1)}, bf16[256,1536]{1,0:T(8,128)(2,1)S(1)}, u32[]{:S(2)}, u32[]{:S(2)}) collective-permute-start(bf16[256,1536]{1,0:T(8,128)(2,1)} %own.1), channel_id=1, source_target_pairs={{16,0},{17,1},{18,2},{19,3},{20,4},{21,5},{22,6},{23,7},{505,8},{5... | collective-permute-start | bytes 2359304 | tf_op jit(solution)/shard_map/ppermute | solution.py:28
  5.0 26.4 %collective-permute-start = (bf16[256,1536]{1,0:T(8,128)(2,1)}, bf16[256,1536]{1,0:T(8,128)(2,1)}, u32[]{:S(2)}, u32[]{:S(2)}) collective-permute-start(bf16[256,1536]{1,0:T(8,128)(2,1)} %own.1), channel_id=1, source_target_pairs={{8,0},{9,1},{10,2},{11,3},{12,4},{13,5},{14,6},{15,7},{0,8},{1,9},... | collective-permute-start | bytes 2359304 | tf_op jit(solution)/shard_map/ppermute | solution.py:28
  17.7 15.9 %collective-permute-start.2 = (bf16[256,1536]{1,0:T(8,128)(2,1)}, bf16[256,1536]{1,0:T(8,128)(2,1)}, u32[]{:S(2)}, u32[]{:S(2)}) collective-permute-start(bf16[256,1536]{1,0:T(8,128)(2,1)} %own.1), channel_id=1, source_target_pairs={{497,0},{496,1},{499,2},{498,3},{501,4},{500,5},{503,6},{502,7},{2... | collective-permute-start | bytes 2359304 | tf_op jit(solution)/shard_map/ppermute | solution.py:28
  21.1 0.9 copy-start
  22.0 0.7 copy-start.1
  22.6 0.7 copy-start.2
  26.4 7.2 %collective-permute-start.3 = (bf16[256,1536]{1,0:T(8,128)(2,1)S(1)}, bf16[256,1536]{1,0:T(8,128)(2,1)S(1)}, u32[]{:S(2)}, u32[]{:S(2)}) collective-permute-start(bf16[256,1536]{1,0:T(8,128)(2,1)S(1)} %collective-permute-done.1.b2), channel_id=1, source_target_pairs={{8,0},{9,1},{10,2},{11,3},{12,4},{13,5},{14,6},{15,7},{0,8},{1,9},... | collective-permute-start | bytes 2359304 | tf_op jit(solution)/shard_map/ppermute | solution.py:28
  74.7 22.8 %collective-permute-start.5 = (bf16[1536,256]{1,0:T(8,128)(2,1)S(1)}, bf16[1536,256]{1,0:T(8,128)(2,1)}, u32[]{:S(2)}, u32[]{:S(2)}) collective-permute-start(bf16[1536,256]{1,0:T(8,128)(2,1)S(1)} %get-tuple-element.22.b0), channel_id=1, source_target_pairs={{16,0},{17,1},{18,2},{19,3},{20,4},{21,5},{22,6},{23,7},{505,8},{5... | collective-permute-start | bytes 2359304 | tf_op jit(solution)/shard_map/ppermute | solution.py:28
  77.3 29.2 %all-to-all-start.3 = ((f32[8,32,384]{2,1,0:T(8,128)}), f32[8,32,384]{2,1,0:T(8,128)}, u32[]{:S(2)}, u32[]{:S(2)}) async-start(f32[8,32,384]{2,1,0:T(8,128)} %get-tuple-element.23), calls=%async_computation.3 | async-start | bytes 786432 | tf_op jit(solution)/shard_map/all_to_all | solution.py:372
  91.7 19.7 %collective-permute-start.6 = (bf16[1536,256]{1,0:T(8,128)(2,1)S(1)}, bf16[1536,256]{1,0:T(8,128)(2,1)}, u32[]{:S(2)}, u32[]{:S(2)}) collective-permute-start(bf16[1536,256]{1,0:T(8,128)(2,1)S(1)} %get-tuple-element.22.b0), channel_id=1, source_target_pairs={{497,0},{496,1},{499,2},{498,3},{501,4},{500,5},{503,6},{502,7},{2... | collective-permute-start | bytes 2359304 | tf_op jit(solution)/shard_map/ppermute | solution.py:28
  94.7 26.1 %collective-permute-start.4 = (bf16[1536,256]{1,0:T(8,128)(2,1)S(1)}, bf16[1536,256]{1,0:T(8,128)(2,1)}, u32[]{:S(2)}, u32[]{:S(2)}) collective-permute-start(bf16[1536,256]{1,0:T(8,128)(2,1)S(1)} %get-tuple-element.22.b0), channel_id=1, source_target_pairs={{8,0},{9,1},{10,2},{11,3},{12,4},{13,5},{14,6},{15,7},{0,8},{1,9},... | collective-permute-start | bytes 2359304 | tf_op jit(solution)/shard_map/ppermute | solution.py:28
  97.6 23.2 %collective-permute-start.7 = (bf16[1536,256]{1,0:T(8,128)(2,1)}, bf16[1536,256]{1,0:T(8,128)(2,1)}, u32[]{:S(2)}, u32[]{:S(2)}) collective-permute-start(bf16[1536,256]{1,0:T(8,128)(2,1)} %collective-permute-done.5.b2), channel_id=1, source_target_pairs={{8,0},{9,1},{10,2},{11,3},{12,4},{13,5},{14,6},{15,7},{0,8},{1,9},... | collective-permute-start | bytes 2359304 | tf_op jit(solution)/shard_map/ppermute | solution.py:28
  107.6 22.4 %collective-permute-start.10 = (f32[32,384]{1,0:T(8,128)S(1)}, f32[32,384]{1,0:T(8,128)S(1)}, u32[]{:S(2)}, u32[]{:S(2)}) collective-permute-start(f32[32,384]{1,0:T(8,128)S(1)} %reduce_sum.19), channel_id=1, source_target_pairs={{96,0},{97,1},{98,2},{99,3},{100,4},{101,5},{102,6},{103,7},{104,8... | collective-permute-start | bytes 147464 | tf_op jit(solution)/shard_map/ppermute | solution.py:28
  109.5 20.5 %collective-permute-start.9 = (f32[32,384]{1,0:T(8,128)S(1)}, f32[32,384]{1,0:T(8,128)}, u32[]{:S(2)}, u32[]{:S(2)}) collective-permute-start(f32[32,384]{1,0:T(8,128)S(1)} %reduce_sum.19), channel_id=1, source_target_pairs={{64,0},{65,1},{66,2},{67,3},{68,4},{69,5},{70,6},{71,7},{72,8},{73... | collective-permute-start | bytes 147464 | tf_op jit(solution)/shard_map/ppermute | solution.py:28
  111.4 18.6 %collective-permute-start.8 = (f32[32,384]{1,0:T(8,128)S(1)}, f32[32,384]{1,0:T(8,128)}, u32[]{:S(2)}, u32[]{:S(2)}) collective-permute-start(f32[32,384]{1,0:T(8,128)S(1)} %reduce_sum.19), channel_id=1, source_target_pairs={{32,0},{33,1},{34,2},{35,3},{36,4},{37,5},{38,6},{39,7},{40,8},{41... | collective-permute-start | bytes 147464 | tf_op jit(solution)/shard_map/ppermute | solution.py:28
  126.4 19.2 %all-to-all-start.2 = ((bf16[8,32,1536]{2,1,0:T(8,128)(2,1)}), bf16[8,32,1536]{2,1,0:T(8,128)(2,1)S(1)}, u32[]{:S(2)}, u32[]{:S(2)}) async-start(bf16[8,32,1536]{2,1,0:T(8,128)(2,1)} %shard_map.106), calls=%async_computation.2 | async-start | bytes 1572864 | tf_op jit(solution)/shard_map/all_to_all | solution.py:289
  130.8 13.5 %collective-permute-start.11 = (f32[32,384]{1,0:T(8,128)S(1)}, f32[32,384]{1,0:T(8,128)S(1)}, u32[]{:S(2)}, u32[]{:S(2)}) collective-permute-start(f32[32,384]{1,0:T(8,128)S(1)} %add_add_fusion), channel_id=1, source_target_pairs={{128,0},{129,1},{130,2},{131,3},{132,4},{133,5},{134,6},{135,7},{1... | collective-permute-start | bytes 147464 | tf_op jit(solution)/shard_map/ppermute | solution.py:28

commit v10 on v9

--- a/solution.py
+++ b/solution.py
@@ -377,8 +377,8 @@
     )
     propagated = jnp.sum(spread(value).astype(jnp.float32), axis=0)
     flip = lambda s: functools.partial(lambda s, b, h: (b ^ s, h), s)
+    total = after(total + move(total, flip(16)), value)
     total = (total + move(total, flip(4))) + (move(total, flip(8)) + move(total, flip(12)))
-    total = total + move(total, flip(16))
     total = total * (1.0 / math.sqrt(nodes * blks))
     return (output, propagated, total[:, :width].T, total[:, width])
 

time: 149 us -> 153 us (1.027)
  waiting for transfers between devices: 13.8 us -> 17 us
  starting transfers between devices: 75 us -> 77 us
    ppermute x12, waiting for transfers between devices: 13.8 us -> 17 us  [move(): return lax.ppermute(block, AXES, route)]
    ppermute x12, starting transfers between devices: 57.1 us -> 59.1 us  [move(): return lax.ppermute(block, AXES, route)]
  transfers between devices with their start and end apart: 14 -> 14, of which waited for: 2 -> 5; matrix products, arithmetic and copies ran while one was open for 3% -> 2% of each run, Pallas kernels for 6% -> 5%
where the time goes in v10:
time: 153 us; the launch traced here: 150 us
  starting transfers between devices  77 us (50%)
  blocking collectives  32 us (21%)
  Pallas kernels  17.2 us (11%)
  waiting for transfers between devices  17 us (11%)
  local copies, waits for them, and re-layouts  4.19 us (3%)
  other arithmetic  1.83 us (1%)
    ppermute x12, starting transfers between devices, move(): return lax.ppermute(block, AXES, route)  59.1 us
    all_to_all x2, blocking collectives, spread(): return lax.all_to_all(x, 'help', 0, 0)  32 us
    ppermute x12, waiting for transfers between devices, move(): return lax.ppermute(block, AXES, route)  17 us
    all_to_all x1, starting transfers between devices, per_device(): lax.all_to_all(total, 'blk', 0, 0, axis_index_groups=alike(blks, half | 3))  14.3 us
    pallas_call x2, Pallas kernels, aggregate(): pl.pallas_call(kernel, out_shape=pltpu.HBM(out_shape, jnp.bfloat16), in_s...  10.4 us
    all_to_all x1, starting transfers between devices, spread(): return lax.all_to_all(x, 'help', 0, 0)  3.56 us
    pallas_call x1, Pallas kernels, per_device(): pl.pallas_call(functools.partial(prepare_kernel, row_tiles), out_shape=(j...  3.13 us
    pallas_call x1, Pallas kernels, per_device(): pl.pallas_call(divide_kernel, out_shape=(pltpu.VMEM((nodes, width), jnp.b...  3.08 us
  transfers between devices with their start and end apart: 14, of which 5 were waited for; matrix products, arithmetic and copies ran while one was open for 2% of the time, Pallas kernels for 5%

profile of v10, /device:TPU:1, one launch (start us, length us, event | category | flops | bytes accessed | tf_op | source)
XLA Modules:
  0.0 150.1 jit_solution(9101413270204943006)
XLA Ops:
  0.6 4.4 %collective-permute-start.1 = (bf16[256,1536]{1,0:T(8,128)(2,1)}, bf16[256,1536]{1,0:T(8,128)(2,1)S(1)}, u32[]{:S(2)}, u32[]{:S(2)}) collective-permute-start(bf16[256,1536]{1,0:T(8,128)(2,1)} %own.1), channel_id=1, source_target_pairs={{16,0},{17,1},{18,2},{19,3},{20,4},{21,5},{22,6},{23,7},{505,8},{5... | collective-permute-start | bytes 2359304 | tf_op jit(solution)/shard_map/ppermute | solution.py:28
  5.0 12.6 %collective-permute-start = (bf16[256,1536]{1,0:T(8,128)(2,1)}, bf16[256,1536]{1,0:T(8,128)(2,1)}, u32[]{:S(2)}, u32[]{:S(2)}) collective-permute-start(bf16[256,1536]{1,0:T(8,128)(2,1)} %own.1), channel_id=1, source_target_pairs={{8,0},{9,1},{10,2},{11,3},{12,4},{13,5},{14,6},{15,7},{0,8},{1,9},... | collective-permute-start | bytes 2359304 | tf_op jit(solution)/shard_map/ppermute | solution.py:28
  17.7 2.6 %collective-permute-start.2 = (bf16[256,1536]{1,0:T(8,128)(2,1)}, bf16[256,1536]{1,0:T(8,128)(2,1)}, u32[]{:S(2)}, u32[]{:S(2)}) collective-permute-start(bf16[256,1536]{1,0:T(8,128)(2,1)} %own.1), channel_id=1, source_target_pairs={{497,0},{496,1},{499,2},{498,3},{501,4},{500,5},{503,6},{502,7},{2... | collective-permute-start | bytes 2359304 | tf_op jit(solution)/shard_map/ppermute | solution.py:28
  23.3 3.1 %shard_map.102 = (s32[92]{0:T(128)S(1)}, s32[46]{0:T(128)S(1)}, bf16[8,32,256]{2,1,0:T(8,128)(2,1)S(1)}, bf16[256,256]{1,0:T(8,128)(2,1)S(1)}, bf16[80,128,128]{...) custom-call(s32[1]{0:T(128)} %bitcast.odd, s32[80]{0:T(128)S(1)} %bitcast.7, s32[80]{0:T(128)S(1)} %bitcast.8, ...), custom_call_target="tpu_custom_call" | custom-call | tf_op jit(solution)/shard_map/pallas_call | solution.py:310
  26.4 5.0 %collective-permute-start.3 = (bf16[256,1536]{1,0:T(8,128)(2,1)S(1)}, bf16[256,1536]{1,0:T(8,128)(2,1)S(1)}, u32[]{:S(2)}, u32[]{:S(2)}) collective-permute-start(bf16[256,1536]{1,0:T(8,128)(2,1)S(1)} %collective-permute-done.1.b2), channel_id=1, source_target_pairs={{8,0},{9,1},{10,2},{11,3},{12,4},{13,5},{14,6},{15,7},{0,8},{1,9},... | collective-permute-start | bytes 2359304 | tf_op jit(solution)/shard_map/ppermute | solution.py:28
  31.4 2.1 %collective-permute-done.2.b3 = bf16[256,1536]{1,0:T(8,128)(2,1)} collective-permute-done((bf16[256,1536]{1,0:T(8,128)(2,1)}, bf16[256,1536]{1,0:T(8,128)(2,1)}, u32[]{:S(2)}, u32[]{:S(2)}) %collective-permute-start.2) | collective-permute-done | bytes 786464 | tf_op jit(solution)/shard_map/ppermute | solution.py:28
  33.6 5.5 %shard_map.103 = bf16[8,224,256]{2,1,0:T(8,128)(2,1)} custom-call(s32[92]{0:T(128)S(1)} %get-tuple-element.15.pairs, s32[46]{0:T(128)S(1)} %get-tuple-element.16.rows, bf16[256,1536]{1,0:T(8,128)(2,1)S(1)} %get-tuple-element.17.b0, bf16[256,1536]{1,0:T(8,128)(2,1)} %collective-permute-done.b1, bf16[256,1536]{1,0:T(8,128)(2,1)S(1)} %collective-permute-done.1.b2, ...), custom_call_target="tpu_custom_call" | custom-call | flops 671088640 | bytes 6291456 | tf_op jit(solution)/shard_map/pallas_call | solution.py:138
  39.1 16.6 %all_to_all.20.parts = bf16[8,224,256]{2,1,0:T(8,128)(2,1)S(1)} all-to-all(bf16[8,224,256]{2,1,0:T(8,128)(2,1)} %shard_map.103), channel_id=1, replica_groups=mesh['blk'=64,'help'=8] {'help'}, dimensions={0} | all-to-all | bytes 1835008 | tf_op jit(solution)/shard_map/all_to_all | solution.py:289
  56.2 15.4 %all_to_all.21.parts = bf16[8,256,256]{2,1,0:T(8,128)(2,1)S(1)} all-to-all(bf16[8,256,256]{2,1,0:T(8,128)(2,1)S(1)} %shard_map.104), channel_id=1, replica_groups=mesh['blk'=64,'help'=8] {'help'}, dimensions={0} | all-to-all | bytes 2097152 | tf_op jit(solution)/shard_map/all_to_all | solution.py:289
  71.6 3.1 %shard_map.105 = (bf16[1536,256]{1,0:T(8,128)(2,1)S(1)}, bf16[32,1536]{1,0:T(8,128)(2,1)}, f32[8,32,384]{2,1,0:T(8,128)}) custom-call(bf16[8,256,256]{2,1,0:T(8,128)(2,1)S(1)} %all_to_all.21.parts), custom_call_target="tpu_custom_call" | custom-call | tf_op jit(solution)/shard_map/pallas_call | solution.py:354
  74.7 2.6 %collective-permute-start.5 = (bf16[1536,256]{1,0:T(8,128)(2,1)S(1)}, bf16[1536,256]{1,0:T(8,128)(2,1)}, u32[]{:S(2)}, u32[]{:S(2)}) collective-permute-start(bf16[1536,256]{1,0:T(8,128)(2,1)S(1)} %get-tuple-element.23.b0), channel_id=1, source_target_pairs={{16,0},{17,1},{18,2},{19,3},{20,4},{21,5},{22,6},{23,7},{505,8},{5... | collective-permute-start | bytes 2359304 | tf_op jit(solution)/shard_map/ppermute | solution.py:28
  77.3 14.3 %all-to-all-start.3 = ((f32[8,32,384]{2,1,0:T(8,128)}), f32[8,32,384]{2,1,0:T(8,128)}, u32[]{:S(2)}, u32[]{:S(2)}) async-start(f32[8,32,384]{2,1,0:T(8,128)} %get-tuple-element.24), calls=%async_computation.3 | async-start | bytes 786432 | tf_op jit(solution)/shard_map/all_to_all | solution.py:372
  91.7 3.0 %collective-permute-start.6 = (bf16[1536,256]{1,0:T(8,128)(2,1)S(1)}, bf16[1536,256]{1,0:T(8,128)(2,1)S(1)}, u32[]{:S(2)}, u32[]{:S(2)}) collective-permute-start(bf16[1536,256]{1,0:T(8,128)(2,1)S(1)} %get-tuple-element.23.b0), channel_id=1, source_target_pairs={{497,0},{496,1},{499,2},{498,3},{501,4},{500,5},{503,6},{502,7},{2... | collective-permute-start | bytes 2359304 | tf_op jit(solution)/shard_map/ppermute | solution.py:28
  94.7 2.8 %collective-permute-start.4 = (bf16[1536,256]{1,0:T(8,128)(2,1)S(1)}, bf16[1536,256]{1,0:T(8,128)(2,1)S(1)}, u32[]{:S(2)}, u32[]{:S(2)}) collective-permute-start(bf16[1536,256]{1,0:T(8,128)(2,1)S(1)} %get-tuple-element.23.b0), channel_id=1, source_target_pairs={{8,0},{9,1},{10,2},{11,3},{12,4},{13,5},{14,6},{15,7},{0,8},{1,9},... | collective-permute-start | bytes 2359304 | tf_op jit(solution)/shard_map/ppermute | solution.py:28
  97.5 8.9 %collective-permute-start.7 = (bf16[1536,256]{1,0:T(8,128)(2,1)}, bf16[1536,256]{1,0:T(8,128)(2,1)S(1)}, u32[]{:S(2)}, u32[]{:S(2)}) collective-permute-start(bf16[1536,256]{1,0:T(8,128)(2,1)} %collective-permute-done.5.b2), channel_id=1, source_target_pairs={{8,0},{9,1},{10,2},{11,3},{12,4},{13,5},{14,6},{15,7},{0,8},{1,9},... | collective-permute-start | bytes 2359304 | tf_op jit(solution)/shard_map/ppermute | solution.py:28
  106.5 2.9 %collective-permute-done.6.b3 = bf16[1536,256]{1,0:T(8,128)(2,1)S(1)} collective-permute-done((bf16[1536,256]{1,0:T(8,128)(2,1)S(1)}, bf16[1536,256]{1,0:T(8,128)(2,1)S(1)}, u32[]{:S(2)}, u32[]{:S(2)}) %collective-permute-start.6) | collective-permute-done | bytes 786464 | tf_op jit(solution)/shard_map/ppermute | solution.py:28
  109.4 4.9 %shard_map.106 = bf16[8,32,1536]{2,1,0:T(8,128)(2,1)} custom-call(s32[92]{0:T(128)S(1)} %get-tuple-element.15.pairs, s32[46]{0:T(128)S(1)} %get-tuple-element.16.rows, bf16[1536,256]{1,0:T(8,128)(2,1)S(1)} %get-tuple-element.23.b0, bf16[1536,256]{1,0:T(8,128)(2,1)S(1)} %collective-permute-done.4.b1, bf16[1536,256]{1,0:T(8,128)(2,1)} %collective-permute-done.5.b2, ...), custom_call_target="tpu_custom_call" | custom-call | flops 671088640 | bytes 6291456 | tf_op jit(solution)/shard_map/pallas_call | solution.py:138
  114.3 3.6 %all-to-all-start.2 = ((bf16[8,32,1536]{2,1,0:T(8,128)(2,1)}), bf16[8,32,1536]{2,1,0:T(8,128)(2,1)S(1)}, u32[]{:S(2)}, u32[]{:S(2)}) async-start(bf16[8,32,1536]{2,1,0:T(8,128)(2,1)} %shard_map.106), calls=%async_computation.2 | async-start | bytes 1572864 | tf_op jit(solution)/shard_map/all_to_all | solution.py:289
  118.9 3.9 %collective-permute-start.8 = (f32[32,384]{1,0:T(8,128)S(1)}, f32[32,384]{1,0:T(8,128)S(1)}, u32[]{:S(2)}, u32[]{:S(2)}) collective-permute-start(f32[32,384]{1,0:T(8,128)S(1)} %reduce_sum.19), channel_id=1, source_target_pairs={{128,0},{129,1},{130,2},{131,3},{132,4},{133,5},{134,6},{135,7},{1... | collective-permute-start | bytes 147464 | tf_op jit(solution)/shard_map/ppermute | solution.py:28
  122.8 9.6 %collective-permute-done.8 = f32[32,384]{1,0:T(8,128)S(1)} collective-permute-done((f32[32,384]{1,0:T(8,128)S(1)}, f32[32,384]{1,0:T(8,128)S(1)}, u32[]{:S(2)}, u32[]{:S(2)}) %collective-permute-start.8) | collective-permute-done | bytes 49184 | tf_op jit(solution)/shard_map/ppermute | solution.py:28
  132.5 1.9 %collective-permute-start.11 = (f32[32,384]{1,0:T(8,128)S(1)}, f32[32,384]{1,0:T(8,128)S(1)}, u32[]{:S(2)}, u32[]{:S(2)}) collective-permute-start(f32[32,384]{1,0:T(8,128)S(1)} %add.17), channel_id=1, source_target_pairs={{96,0},{97,1},{98,2},{99,3},{100,4},{101,5},{102,6},{103,7},{104,8... | collective-permute-start | bytes 147464 | tf_op jit(solution)/shard_map/ppermute | solution.py:28
  134.4 1.9 %collective-permute-start.10 = (f32[32,384]{1,0:T(8,128)S(1)}, f32[32,384]{1,0:T(8,128)S(1)}, u32[]{:S(2)}, u32[]{:S(2)}) collective-permute-start(f32[32,384]{1,0:T(8,128)S(1)} %add.17), channel_id=1, source_target_pairs={{64,0},{65,1},{66,2},{67,3},{68,4},{69,5},{70,6},{71,7},{72,8},{73... | collective-permute-start | bytes 147464 | tf_op jit(solution)/shard_map/ppermute | solution.py:28
  136.3 9.3 %collective-permute-start.9 = (f32[32,384]{1,0:T(8,128)S(1)}, f32[32,384]{1,0:T(8,128)S(1)}, u32[]{:S(2)}, u32[]{:S(2)}) collective-permute-start(f32[32,384]{1,0:T(8,128)S(1)} %add.17), channel_id=1, source_target_pairs={{32,0},{33,1},{34,2},{35,3},{36,4},{37,5},{38,6},{39,7},{40,8},{41... | collective-permute-start | bytes 147464 | tf_op jit(solution)/shard_map/ppermute | solution.py:28
  145.7 1.5 %collective-permute-done.10 = f32[32,384]{1,0:T(8,128)S(1)} collective-permute-done((f32[32,384]{1,0:T(8,128)S(1)}, f32[32,384]{1,0:T(8,128)S(1)}, u32[]{:S(2)}, u32[]{:S(2)}) %collective-permute-start.10) | collective-permute-done | bytes 49184 | tf_op jit(solution)/shard_map/ppermute | solution.py:28
  (24 shorter events, 7.5 us)
Async XLA Ops:
  0.6 25.8 %collective-permute-start.1 = (bf16[256,1536]{1,0:T(8,128)(2,1)}, bf16[256,1536]{1,0:T(8,128)(2,1)S(1)}, u32[]{:S(2)}, u32[]{:S(2)}) collective-permute-start(bf16[256,1536]{1,0:T(8,128)(2,1)} %own.1), channel_id=1, source_target_pairs={{16,0},{17,1},{18,2},{19,3},{20,4},{21,5},{22,6},{23,7},{505,8},{5... | collective-permute-start | bytes 2359304 | tf_op jit(solution)/shard_map/ppermute | solution.py:28
  5.0 26.4 %collective-permute-start = (bf16[256,1536]{1,0:T(8,128)(2,1)}, bf16[256,1536]{1,0:T(8,128)(2,1)}, u32[]{:S(2)}, u32[]{:S(2)}) collective-permute-start(bf16[256,1536]{1,0:T(8,128)(2,1)} %own.1), channel_id=1, source_target_pairs={{8,0},{9,1},{10,2},{11,3},{12,4},{13,5},{14,6},{15,7},{0,8},{1,9},... | collective-permute-start | bytes 2359304 | tf_op jit(solution)/shard_map/ppermute | solution.py:28
  17.7 15.9 %collective-permute-start.2 = (bf16[256,1536]{1,0:T(8,128)(2,1)}, bf16[256,1536]{1,0:T(8,128)(2,1)}, u32[]{:S(2)}, u32[]{:S(2)}) collective-permute-start(bf16[256,1536]{1,0:T(8,128)(2,1)} %own.1), channel_id=1, source_target_pairs={{497,0},{496,1},{499,2},{498,3},{501,4},{500,5},{503,6},{502,7},{2... | collective-permute-start | bytes 2359304 | tf_op jit(solution)/shard_map/ppermute | solution.py:28
  21.1 0.9 copy-start
  22.0 0.7 copy-start.1
  22.6 0.7 copy-start.2
  26.4 7.2 %collective-permute-start.3 = (bf16[256,1536]{1,0:T(8,128)(2,1)S(1)}, bf16[256,1536]{1,0:T(8,128)(2,1)S(1)}, u32[]{:S(2)}, u32[]{:S(2)}) collective-permute-start(bf16[256,1536]{1,0:T(8,128)(2,1)S(1)} %collective-permute-done.1.b2), channel_id=1, source_target_pairs={{8,0},{9,1},{10,2},{11,3},{12,4},{13,5},{14,6},{15,7},{0,8},{1,9},... | collective-permute-start | bytes 2359304 | tf_op jit(solution)/shard_map/ppermute | solution.py:28
  74.7 22.8 %collective-permute-start.5 = (bf16[1536,256]{1,0:T(8,128)(2,1)S(1)}, bf16[1536,256]{1,0:T(8,128)(2,1)}, u32[]{:S(2)}, u32[]{:S(2)}) collective-permute-start(bf16[1536,256]{1,0:T(8,128)(2,1)S(1)} %get-tuple-element.23.b0), channel_id=1, source_target_pairs={{16,0},{17,1},{18,2},{19,3},{20,4},{21,5},{22,6},{23,7},{505,8},{5... | collective-permute-start | bytes 2359304 | tf_op jit(solution)/shard_map/ppermute | solution.py:28
  77.3 37.0 %all-to-all-start.3 = ((f32[8,32,384]{2,1,0:T(8,128)}), f32[8,32,384]{2,1,0:T(8,128)}, u32[]{:S(2)}, u32[]{:S(2)}) async-start(f32[8,32,384]{2,1,0:T(8,128)} %get-tuple-element.24), calls=%async_computation.3 | async-start | bytes 786432 | tf_op jit(solution)/shard_map/all_to_all | solution.py:372
  91.7 17.7 %collective-permute-start.6 = (bf16[1536,256]{1,0:T(8,128)(2,1)S(1)}, bf16[1536,256]{1,0:T(8,128)(2,1)S(1)}, u32[]{:S(2)}, u32[]{:S(2)}) collective-permute-start(bf16[1536,256]{1,0:T(8,128)(2,1)S(1)} %get-tuple-element.23.b0), channel_id=1, source_target_pairs={{497,0},{496,1},{499,2},{498,3},{501,4},{500,5},{503,6},{502,7},{2... | collective-permute-start | bytes 2359304 | tf_op jit(solution)/shard_map/ppermute | solution.py:28
  94.7 14.7 %collective-permute-start.4 = (bf16[1536,256]{1,0:T(8,128)(2,1)S(1)}, bf16[1536,256]{1,0:T(8,128)(2,1)S(1)}, u32[]{:S(2)}, u32[]{:S(2)}) collective-permute-start(bf16[1536,256]{1,0:T(8,128)(2,1)S(1)} %get-tuple-element.23.b0), channel_id=1, source_target_pairs={{8,0},{9,1},{10,2},{11,3},{12,4},{13,5},{14,6},{15,7},{0,8},{1,9},... | collective-permute-start | bytes 2359304 | tf_op jit(solution)/shard_map/ppermute | solution.py:28
  97.5 11.8 %collective-permute-start.7 = (bf16[1536,256]{1,0:T(8,128)(2,1)}, bf16[1536,256]{1,0:T(8,128)(2,1)S(1)}, u32[]{:S(2)}, u32[]{:S(2)}) collective-permute-start(bf16[1536,256]{1,0:T(8,128)(2,1)} %collective-permute-done.5.b2), channel_id=1, source_target_pairs={{8,0},{9,1},{10,2},{11,3},{12,4},{13,5},{14,6},{15,7},{0,8},{1,9},... | collective-permute-start | bytes 2359304 | tf_op jit(solution)/shard_map/ppermute | solution.py:28
  114.3 35.0 %all-to-all-start.2 = ((bf16[8,32,1536]{2,1,0:T(8,128)(2,1)}), bf16[8,32,1536]{2,1,0:T(8,128)(2,1)S(1)}, u32[]{:S(2)}, u32[]{:S(2)}) async-start(bf16[8,32,1536]{2,1,0:T(8,128)(2,1)} %shard_map.106), calls=%async_computation.2 | async-start | bytes 1572864 | tf_op jit(solution)/shard_map/all_to_all | solution.py:289
  118.9 13.6 %collective-permute-start.8 = (f32[32,384]{1,0:T(8,128)S(1)}, f32[32,384]{1,0:T(8,128)S(1)}, u32[]{:S(2)}, u32[]{:S(2)}) collective-permute-start(f32[32,384]{1,0:T(8,128)S(1)} %reduce_sum.19), channel_id=1, source_target_pairs={{128,0},{129,1},{130,2},{131,3},{132,4},{133,5},{134,6},{135,7},{1... | collective-permute-start | bytes 147464 | tf_op jit(solution)/shard_map/ppermute | solution.py:28
  132.5 13.2 %collective-permute-start.11 = (f32[32,384]{1,0:T(8,128)S(1)}, f32[32,384]{1,0:T(8,128)S(1)}, u32[]{:S(2)}, u32[]{:S(2)}) collective-permute-start(f32[32,384]{1,0:T(8,128)S(1)} %add.17), channel_id=1, source_target_pairs={{96,0},{97,1},{98,2},{99,3},{100,4},{101,5},{102,6},{103,7},{104,8... | collective-permute-start | bytes 147464 | tf_op jit(solution)/shard_map/ppermute | solution.py:28
  134.4 12.8 %collective-permute-start.10 = (f32[32,384]{1,0:T(8,128)S(1)}, f32[32,384]{1,0:T(8,128)S(1)}, u32[]{:S(2)}, u32[]{:S(2)}) collective-permute-start(f32[32,384]{1,0:T(8,128)S(1)} %add.17), channel_id=1, source_target_pairs={{64,0},{65,1},{66,2},{67,3},{68,4},{69,5},{70,6},{71,7},{72,8},{73... | collective-permute-start | bytes 147464 | tf_op jit(solution)/shard_map/ppermute | solution.py:28
  136.3 11.7 %collective-permute-start.9 = (f32[32,384]{1,0:T(8,128)S(1)}, f32[32,384]{1,0:T(8,128)S(1)}, u32[]{:S(2)}, u32[]{:S(2)}) collective-permute-start(f32[32,384]{1,0:T(8,128)S(1)} %add.17), channel_id=1, source_target_pairs={{32,0},{33,1},{34,2},{35,3},{36,4},{37,5},{38,6},{39,7},{40,8},{41... | collective-permute-start | bytes 147464 | tf_op jit(solution)/shard_map/ppermute | solution.py:28
